TPU v7x, 256 devices: a whole 4x4x8 slice. The times are simulated.
256 devices in a mesh: gx: 8 (over y, core), gy: 4 (over x), gz: 8 (over z).
Axes of the slice: x: 4, y: 4, z: 8, core: 2. Of those that a mesh axis runs over, the one named last changes fastest.
Arguments:
- velocity: float32 [3, 256, 128, 1024], P(None, 'gx', 'gy', 'gz'), may hold values from -3 to 3
- box_level: float32 [8192, 16, 256], P(('gx', 'gy', 'gz')), may hold values from -9 to 9
- corners: int32 [8192, 3], P(('gx', 'gy', 'gz')), may hold values from 0 to 112, as said below
- owner_list: int32 [8192], P(('gx', 'gy', 'gz')), may hold values from -1 to 31, as said below
Outputs:
- new_velocity: float32 [3, 256, 128, 1024], P(None, 'gx', 'gy', 'gz')
- level_sets: float32 [8192, 16, 256], P(('gx', 'gy', 'gz'))
- curvature: float32 [8192, 16, 256], P(('gx', 'gy', 'gz'))
Inputs may be any that keep to these rules, and one draw needn't show every extreme that they name: `owner_list`: -1 marks an empty slot. The live slots of one device name different helpers, numbered in the order of the devices of its gy+gz group (gy slowest) at the device's own index along gx; every helper is named by exactly 16 slots of its group; a device has 0 to 32 live slots, and some device of every group has 32. `corners`: columns 0, 1, 2 lie in 0 to 16, 16, 112: every box lies inside its home device's block. Boxes may intersect.
All inputs are finite; a program needn't handle non-finite values.
Results may differ from a plain program's by a relative error of at most 0.0003.
Values sent between devices are 32-bit elements; how exact they have to be, the bound alone decides.
No kernel may reach another device: no remote copies, remote signals or barrier semaphores. Data moves between devices by JAX's collectives and lax.ppermute only.
A program may use at most 128 MiB of HBM per device.

v0:
```python
import math

import jax
import jax.numpy as jnp
from jax import lax
from jax.sharding import PartitionSpec as P

ITERS = 12


box_step = 0.25
pseudo_step = 0.3
weno_floor = 1e-06
band_width = 1.5
tension = 2.0
grid_step = 0.2
viscosity = 0.1
normal_floor = 0.5


def extended(x, sides, width):
    for axis, dim in sides:
        size, length = (lax.axis_size(axis), x.shape[dim])
        up = [(i, (i + 1) % size) for i in range(size)]
        down = [(j, i) for i, j in up]
        last = lax.slice_in_dim(x, length - width, length, axis=dim)
        leading = lax.slice_in_dim(x, 0, width, axis=dim)
        before = lax.ppermute(last, axis, up)
        after = lax.ppermute(leading, axis, down)
        x = jnp.concatenate([before, x, after], axis=dim)
    return x


def neighbour(values, across, forward):
    length = values.shape[-2]
    plane_size = values.shape[-1]
    if across == 0:
        if forward:
            return jnp.concatenate([values[..., 1:, :], values[..., -1:, :]], axis=-2)
        return jnp.concatenate([values[..., :1, :], values[..., :-1, :]], axis=-2)
    stride = length if across == 1 else 1
    places = jnp.arange(plane_size, dtype=jnp.int32)
    column = places // length if across == 1 else places % length
    if forward:
        shifted = jnp.concatenate([values[..., stride:], values[..., :stride]], axis=-1)
        return jnp.where(column == length - 1, values, shifted)
    shifted = jnp.concatenate(
        [values[..., plane_size - stride :], values[..., : plane_size - stride]], axis=-1
    )
    return jnp.where(column == 0, values, shifted)


def weno_blend(slope_one, slope_two, slope_three, slope_four, slope_five):
    smooth_one = (
        13.0 / 12.0 * (slope_one - 2.0 * slope_two + slope_three) ** 2
        + 0.25 * (slope_one - 4.0 * slope_two + 3.0 * slope_three) ** 2
    )
    smooth_two = (
        13.0 / 12.0 * (slope_two - 2.0 * slope_three + slope_four) ** 2
        + 0.25 * (slope_two - slope_four) ** 2
    )
    smooth_three = (
        13.0 / 12.0 * (slope_three - 2.0 * slope_four + slope_five) ** 2
        + 0.25 * (3.0 * slope_three - 4.0 * slope_four + slope_five) ** 2
    )
    weight_one = 0.1 / (weno_floor + smooth_one) ** 2
    weight_two = 0.6 / (weno_floor + smooth_two) ** 2
    weight_three = 0.3 / (weno_floor + smooth_three) ** 2
    poly_one = slope_one / 3.0 - 7.0 * slope_two / 6.0 + 11.0 * slope_three / 6.0
    poly_two = -slope_two / 6.0 + 5.0 * slope_three / 6.0 + slope_four / 3.0
    poly_three = slope_three / 3.0 + 5.0 * slope_four / 6.0 - slope_five / 6.0
    return (weight_one * poly_one + weight_two * poly_two + weight_three * poly_three) / (
        weight_one + weight_two + weight_three
    )


def upwind_slopes(values, across):
    behind = values - neighbour(values, across, False)
    back_one = neighbour(behind, across, False)
    back_two = neighbour(back_one, across, False)
    ahead_one = neighbour(behind, across, True)
    ahead_two = neighbour(ahead_one, across, True)
    ahead_three = neighbour(ahead_two, across, True)
    minus_side = weno_blend(back_two, back_one, behind, ahead_one, ahead_two)
    plus_side = weno_blend(ahead_three, ahead_two, ahead_one, behind, back_one)
    return (minus_side, plus_side)


def central_slopes(values):
    return [
        0.5 * (neighbour(values, across, True) - neighbour(values, across, False))
        for across in range(3)
    ]


def evolve_boxes(levels, motion):
    change = jnp.zeros_like(levels)
    for across in range(3):
        minus_side, plus_side = upwind_slopes(levels, across)
        speed_d = motion[:, across]
        change = (
            change + jnp.maximum(speed_d, 0.0) * minus_side + jnp.minimum(speed_d, 0.0) * plus_side
        )
    advected = levels - box_step * change
    sign_soft = advected / jnp.sqrt(advected * advected + 1.0)
    outside = advected > 0.0

    def one_sweep(counter, current):
        squared = jnp.zeros_like(current)
        for across in range(3):
            behind = current - neighbour(current, across, False)
            ahead_d = neighbour(current, across, True) - current
            upper_sq = jnp.maximum(jnp.maximum(behind, 0.0) ** 2, jnp.minimum(ahead_d, 0.0) ** 2)
            lower_sq = jnp.maximum(jnp.minimum(behind, 0.0) ** 2, jnp.maximum(ahead_d, 0.0) ** 2)
            squared = squared + jnp.where(outside, upper_sq, lower_sq)
        return current - pseudo_step * sign_soft * (jnp.sqrt(squared) - 1.0)

    settled = lax.fori_loop(0, ITERS, one_sweep, advected)
    slopes = central_slopes(settled)
    magnitude = jnp.maximum(
        jnp.sqrt(slopes[0] ** 2 + slopes[1] ** 2 + slopes[2] ** 2), normal_floor
    )
    bending = jnp.zeros_like(settled)
    for across in range(3):
        unit_d = slopes[across] / magnitude
        bending = bending + 0.5 * (
            neighbour(unit_d, across, True) - neighbour(unit_d, across, False)
        )
    return (settled, bending)


def surface_force(levels, bending):
    slopes = central_slopes(levels)
    delta_band = jnp.exp(-((levels / band_width) ** 2)) / (band_width * math.sqrt(math.pi))
    strength = tension * bending * delta_band
    return jnp.stack([strength * slopes[0], strength * slopes[1], strength * slopes[2]], axis=1)


def tendency(padded):
    centre = padded[:, 1:-1, 1:-1, 1:-1]
    uppers = (padded[:, 2:, 1:-1, 1:-1], padded[:, 1:-1, 2:, 1:-1], padded[:, 1:-1, 1:-1, 2:])
    lowers = (padded[:, :-2, 1:-1, 1:-1], padded[:, 1:-1, :-2, 1:-1], padded[:, 1:-1, 1:-1, :-2])
    advect = jnp.zeros_like(centre)
    spread = -6.0 * centre
    for across in range(3):
        advect = advect + centre[across : across + 1] * (uppers[across] - lowers[across]) * 0.5
        spread = spread + uppers[across] + lowers[across]
    return viscosity * spread - advect


def face_pad(values):
    return extended(values, (("gx", 1), ("gy", 2), ("gz", 3)), 1)


def local(velocity, box_level, corners, owner_list):
    slot_count = box_level.shape[0]
    box_edge = box_level.shape[1]
    alive_mask = (owner_list >= 0).astype(jnp.float32)
    nought = jnp.zeros((), jnp.int32)

    def cut_slot(slot_no, boxes_now):
        corner_at = (nought, corners[slot_no, 0], corners[slot_no, 1], corners[slot_no, 2])
        region = lax.dynamic_slice(velocity, corner_at, (3, box_edge, box_edge, box_edge))
        return boxes_now.at[slot_no].set(region.reshape(3, box_edge, box_edge * box_edge))

    motion_boxes = lax.fori_loop(
        0,
        slot_count,
        cut_slot,
        jnp.zeros((slot_count, 3, box_edge, box_edge * box_edge), jnp.float32),
    )
    group_size = lax.axis_size(("gy", "gz"))
    member = lax.axis_index(("gy", "gz"))
    work_count = slot_count // 2
    group_lists = lax.all_gather(owner_list, ("gy", "gz"), axis=0, tiled=True).reshape(
        group_size, slot_count
    )
    helper_ids = jnp.arange(group_size, dtype=jnp.int32)
    slot_ids = jnp.arange(slot_count, dtype=jnp.int32)
    matches = owner_list[None, :] == helper_ids[:, None]
    chosen = jnp.where(
        jnp.any(matches, axis=1),
        jnp.sum(jnp.where(matches, slot_ids[None, :], 0), axis=1),
        slot_count,
    )
    level_padded = jnp.concatenate([box_level, jnp.zeros_like(box_level[:1])], axis=0)
    motion_padded = jnp.concatenate([motion_boxes, jnp.zeros_like(motion_boxes[:1])], axis=0)
    outgoing = (jnp.take(level_padded, chosen, axis=0), jnp.take(motion_padded, chosen, axis=0))
    incoming = (
        lax.all_to_all(outgoing[0], ("gy", "gz"), split_axis=0, concat_axis=0, tiled=True),
        lax.all_to_all(outgoing[1], ("gy", "gz"), split_axis=0, concat_axis=0, tiled=True),
    )
    senders = jnp.any(group_lists == member, axis=1)
    sender_count = senders.astype(jnp.int32)
    rank_of = jnp.cumsum(sender_count) - sender_count
    work_ids = jnp.arange(work_count, dtype=jnp.int32)
    pick_mask = senders[None, :] & (rank_of[None, :] == work_ids[:, None])
    sources = jnp.sum(jnp.where(pick_mask, helper_ids[None, :], 0), axis=1)
    settled_work, bending_work = evolve_boxes(
        jnp.take(incoming[0], sources, axis=0), jnp.take(incoming[1], sources, axis=0)
    )
    rows_back = jnp.clip(rank_of, 0, work_count - 1)
    replies = (jnp.take(settled_work, rows_back, axis=0), jnp.take(bending_work, rows_back, axis=0))
    answers = (
        lax.all_to_all(replies[0], ("gy", "gz"), split_axis=0, concat_axis=0, tiled=True),
        lax.all_to_all(replies[1], ("gy", "gz"), split_axis=0, concat_axis=0, tiled=True),
    )
    from_helper = jnp.clip(owner_list, 0, group_size - 1)
    settled = jnp.take(answers[0], from_helper, axis=0) * alive_mask[:, None, None]
    bending = jnp.take(answers[1], from_helper, axis=0) * alive_mask[:, None, None]
    predictor = velocity + grid_step * tendency(face_pad(velocity))
    second = predictor + grid_step * tendency(face_pad(predictor))
    stepped = 0.5 * (velocity + second)
    push_boxes = surface_force(settled, bending).reshape(
        slot_count, 3, box_edge, box_edge, box_edge
    )

    def deposit_slot(slot_no, grid_now):
        corner_at = (nought, corners[slot_no, 0], corners[slot_no, 1], corners[slot_no, 2])
        region = lax.dynamic_slice(grid_now, corner_at, (3, box_edge, box_edge, box_edge))
        return lax.dynamic_update_slice(
            grid_now, region + grid_step * push_boxes[slot_no], corner_at
        )

    result = lax.fori_loop(0, slot_count, deposit_slot, stepped)
    return (result, settled, bending)


def solution(mesh):
    placed = (
        P(None, "gx", "gy", "gz"),
        P(("gx", "gy", "gz"), None, None),
        P(("gx", "gy", "gz"), None),
        P(("gx", "gy", "gz")),
    )
    return jax.shard_map(
        local,
        mesh=mesh,
        in_specs=placed,
        out_specs=(
            P(None, "gx", "gy", "gz"),
            P(("gx", "gy", "gz"), None, None),
            P(("gx", "gy", "gz"), None, None),
        ),
        check_vma=False,
    )
```

profile of v0, /device:TPU:1, one launch (start us, length us, event | category | flops | bytes accessed | tf_op | source)
XLA Modules:
  0.0 1450.7 jit_solution(361462506207091663)
XLA Ops:
  40.0 298.4 %while.39 = (s32[]{:T(128)}, f32[32,3,16,256]{3,2,1,0:T(8,128)S(1)}, s32[32,3]{0,1:T(4,128)S(1)}, f32[3,32,32,128]{3,2,1,0:T(8,128)S(1)}, s32[]{:T(128)}, /*inde...) while((s32[]{:T(128)}, f32[32,3,16,256]{3,2,1,0:T(8,128)S(1)}, s32[32,3]{0,1:T(4,128)S(1)}, ...), condition=%wide.region_7.8_spmd, body=%wide.region_5.7_spmd.sunk | while | flops 12326 | bytes 344345 | solution.py:166
  419.3 22.0 %all-to-all-done.1 = f32[32,3,16,256]{3,2,1,0:T(8,128)} async-done(((f32[32,3,16,256]{3,2,1,0:T(8,128)}), f32[32,3,16,256]{3,2,1,0:T(8,128)}, u32[]{:S(2)}, u32[]{:S(2)}) %all-to-all-start.1) | async-done | bytes 1572896 | tf_op jit(solution)/shard_map/all_to_all | solution.py:191
  452.9 23.1 %while.40 = (s32[]{:T(128)}, f32[16,16,256]{2,1,0:T(8,128)S(1)}, f32[16,16,256]{2,1,0:T(8,128)}, pred[16,16,256]{2,1,0:T(8,128)(4,1)}, s32[]{:T(128)}) while((s32[]{:T(128)}, f32[16,16,256]{2,1,0:T(8,128)S(1)}, f32[16,16,256]{2,1,0:T(8,128)}, pred[16,16,256]{2,1,0:T(8,128)(4,1)}, s32[]{:T(128)}) %tuple.177), condition=%wide.region_9.10_spmd, body=%wide.region_8.9_spmd.sunk | while | flops 3611650 | bytes 6883445 | solution.py:118
  562.7 887.8 %while.41 = (s32[]{:T(128)}, f32[3,32,32,128]{3,2,1,0:T(8,128)}, s32[32,3]{0,1:T(4,128)S(1)}, f32[32,3,16,16,16]{4,3,2,1,0:T(8,128)}, s32[]{:T(128)}, /*index=5*/s32[]{:T(128)}, s32[]{:T(128)}, s32[]{:T(128)}) while((s32[]{:T(128)}, f32[3,32,32,128]{3,2,1,0:T(8,128)}, s32[32,3]{0,1:T(4,128)S(1)}, f32[32,3,16,16,16]{4,3,2,1,0:T(8,128)}, ...), condition=%wide.region_11.14_spmd, body=%wide.region_10.13_spmd.sunk | while | flops 24587 | bytes 246003 | solution.py:225
  570.4 20.0 %dynamic_update_slice.8 = f32[3,32,32,128]{3,2,1,0:T(8,128)} dynamic-update-slice(f32[3,32,32,128]{3,2,1,0:T(8,128)} %get-tuple-element.578, f32[3,16,16,16]{3,2,1,0:T(8,128)S(1)} %bitcast_add_fusion.2, s32[]{:T(128)} %constant.445.clone.1..sunk.1, s32[]{:T(128)S(6)} %select_n.609, s32[]{:T(128)S(6)} %select_n.610, s32[]{:T(128)S(6)} %select_n.611) | dynamic-update-slice | bytes 98308 | tf_op jit(solution)/shard_map/while/body/eval_jaxpr/dynamic_update_slice | solution.py:221
  598.2 20.0 %dynamic_update_slice.8 = f32[3,32,32,128]{3,2,1,0:T(8,128)} dynamic-update-slice(f32[3,32,32,128]{3,2,1,0:T(8,128)} %get-tuple-element.578, f32[3,16,16,16]{3,2,1,0:T(8,128)S(1)} %bitcast_add_fusion.2, s32[]{:T(128)} %constant.445.clone.1..sunk.1, s32[]{:T(128)S(6)} %select_n.609, s32[]{:T(128)S(6)} %select_n.610, s32[]{:T(128)S(6)} %select_n.611) | dynamic-update-slice | bytes 98308 | tf_op jit(solution)/shard_map/while/body/eval_jaxpr/dynamic_update_slice | solution.py:221
  625.9 20.0 %dynamic_update_slice.8 = f32[3,32,32,128]{3,2,1,0:T(8,128)} dynamic-update-slice(f32[3,32,32,128]{3,2,1,0:T(8,128)} %get-tuple-element.578, f32[3,16,16,16]{3,2,1,0:T(8,128)S(1)} %bitcast_add_fusion.2, s32[]{:T(128)} %constant.445.clone.1..sunk.1, s32[]{:T(128)S(6)} %select_n.609, s32[]{:T(128)S(6)} %select_n.610, s32[]{:T(128)S(6)} %select_n.611) | dynamic-update-slice | bytes 98308 | tf_op jit(solution)/shard_map/while/body/eval_jaxpr/dynamic_update_slice | solution.py:221
  653.7 20.0 %dynamic_update_slice.8 = f32[3,32,32,128]{3,2,1,0:T(8,128)} dynamic-update-slice(f32[3,32,32,128]{3,2,1,0:T(8,128)} %get-tuple-element.578, f32[3,16,16,16]{3,2,1,0:T(8,128)S(1)} %bitcast_add_fusion.2, s32[]{:T(128)} %constant.445.clone.1..sunk.1, s32[]{:T(128)S(6)} %select_n.609, s32[]{:T(128)S(6)} %select_n.610, s32[]{:T(128)S(6)} %select_n.611) | dynamic-update-slice | bytes 98308 | tf_op jit(solution)/shard_map/while/body/eval_jaxpr/dynamic_update_slice | solution.py:221
  681.4 20.0 %dynamic_update_slice.8 = f32[3,32,32,128]{3,2,1,0:T(8,128)} dynamic-update-slice(f32[3,32,32,128]{3,2,1,0:T(8,128)} %get-tuple-element.578, f32[3,16,16,16]{3,2,1,0:T(8,128)S(1)} %bitcast_add_fusion.2, s32[]{:T(128)} %constant.445.clone.1..sunk.1, s32[]{:T(128)S(6)} %select_n.609, s32[]{:T(128)S(6)} %select_n.610, s32[]{:T(128)S(6)} %select_n.611) | dynamic-update-slice | bytes 98308 | tf_op jit(solution)/shard_map/while/body/eval_jaxpr/dynamic_update_slice | solution.py:221
  709.2 20.0 %dynamic_update_slice.8 = f32[3,32,32,128]{3,2,1,0:T(8,128)} dynamic-update-slice(f32[3,32,32,128]{3,2,1,0:T(8,128)} %get-tuple-element.578, f32[3,16,16,16]{3,2,1,0:T(8,128)S(1)} %bitcast_add_fusion.2, s32[]{:T(128)} %constant.445.clone.1..sunk.1, s32[]{:T(128)S(6)} %select_n.609, s32[]{:T(128)S(6)} %select_n.610, s32[]{:T(128)S(6)} %select_n.611) | dynamic-update-slice | bytes 98308 | tf_op jit(solution)/shard_map/while/body/eval_jaxpr/dynamic_update_slice | solution.py:221
  736.9 20.0 %dynamic_update_slice.8 = f32[3,32,32,128]{3,2,1,0:T(8,128)} dynamic-update-slice(f32[3,32,32,128]{3,2,1,0:T(8,128)} %get-tuple-element.578, f32[3,16,16,16]{3,2,1,0:T(8,128)S(1)} %bitcast_add_fusion.2, s32[]{:T(128)} %constant.445.clone.1..sunk.1, s32[]{:T(128)S(6)} %select_n.609, s32[]{:T(128)S(6)} %select_n.610, s32[]{:T(128)S(6)} %select_n.611) | dynamic-update-slice | bytes 98308 | tf_op jit(solution)/shard_map/while/body/eval_jaxpr/dynamic_update_slice | solution.py:221
  764.7 20.0 %dynamic_update_slice.8 = f32[3,32,32,128]{3,2,1,0:T(8,128)} dynamic-update-slice(f32[3,32,32,128]{3,2,1,0:T(8,128)} %get-tuple-element.578, f32[3,16,16,16]{3,2,1,0:T(8,128)S(1)} %bitcast_add_fusion.2, s32[]{:T(128)} %constant.445.clone.1..sunk.1, s32[]{:T(128)S(6)} %select_n.609, s32[]{:T(128)S(6)} %select_n.610, s32[]{:T(128)S(6)} %select_n.611) | dynamic-update-slice | bytes 98308 | tf_op jit(solution)/shard_map/while/body/eval_jaxpr/dynamic_update_slice | solution.py:221
  792.4 20.0 %dynamic_update_slice.8 = f32[3,32,32,128]{3,2,1,0:T(8,128)} dynamic-update-slice(f32[3,32,32,128]{3,2,1,0:T(8,128)} %get-tuple-element.578, f32[3,16,16,16]{3,2,1,0:T(8,128)S(1)} %bitcast_add_fusion.2, s32[]{:T(128)} %constant.445.clone.1..sunk.1, s32[]{:T(128)S(6)} %select_n.609, s32[]{:T(128)S(6)} %select_n.610, s32[]{:T(128)S(6)} %select_n.611) | dynamic-update-slice | bytes 98308 | tf_op jit(solution)/shard_map/while/body/eval_jaxpr/dynamic_update_slice | solution.py:221
  820.2 20.0 %dynamic_update_slice.8 = f32[3,32,32,128]{3,2,1,0:T(8,128)} dynamic-update-slice(f32[3,32,32,128]{3,2,1,0:T(8,128)} %get-tuple-element.578, f32[3,16,16,16]{3,2,1,0:T(8,128)S(1)} %bitcast_add_fusion.2, s32[]{:T(128)} %constant.445.clone.1..sunk.1, s32[]{:T(128)S(6)} %select_n.609, s32[]{:T(128)S(6)} %select_n.610, s32[]{:T(128)S(6)} %select_n.611) | dynamic-update-slice | bytes 98308 | tf_op jit(solution)/shard_map/while/body/eval_jaxpr/dynamic_update_slice | solution.py:221
  847.9 20.0 %dynamic_update_slice.8 = f32[3,32,32,128]{3,2,1,0:T(8,128)} dynamic-update-slice(f32[3,32,32,128]{3,2,1,0:T(8,128)} %get-tuple-element.578, f32[3,16,16,16]{3,2,1,0:T(8,128)S(1)} %bitcast_add_fusion.2, s32[]{:T(128)} %constant.445.clone.1..sunk.1, s32[]{:T(128)S(6)} %select_n.609, s32[]{:T(128)S(6)} %select_n.610, s32[]{:T(128)S(6)} %select_n.611) | dynamic-update-slice | bytes 98308 | tf_op jit(solution)/shard_map/while/body/eval_jaxpr/dynamic_update_slice | solution.py:221
  875.7 20.0 %dynamic_update_slice.8 = f32[3,32,32,128]{3,2,1,0:T(8,128)} dynamic-update-slice(f32[3,32,32,128]{3,2,1,0:T(8,128)} %get-tuple-element.578, f32[3,16,16,16]{3,2,1,0:T(8,128)S(1)} %bitcast_add_fusion.2, s32[]{:T(128)} %constant.445.clone.1..sunk.1, s32[]{:T(128)S(6)} %select_n.609, s32[]{:T(128)S(6)} %select_n.610, s32[]{:T(128)S(6)} %select_n.611) | dynamic-update-slice | bytes 98308 | tf_op jit(solution)/shard_map/while/body/eval_jaxpr/dynamic_update_slice | solution.py:221
  903.4 20.0 %dynamic_update_slice.8 = f32[3,32,32,128]{3,2,1,0:T(8,128)} dynamic-update-slice(f32[3,32,32,128]{3,2,1,0:T(8,128)} %get-tuple-element.578, f32[3,16,16,16]{3,2,1,0:T(8,128)S(1)} %bitcast_add_fusion.2, s32[]{:T(128)} %constant.445.clone.1..sunk.1, s32[]{:T(128)S(6)} %select_n.609, s32[]{:T(128)S(6)} %select_n.610, s32[]{:T(128)S(6)} %select_n.611) | dynamic-update-slice | bytes 98308 | tf_op jit(solution)/shard_map/while/body/eval_jaxpr/dynamic_update_slice | solution.py:221
  931.2 20.0 %dynamic_update_slice.8 = f32[3,32,32,128]{3,2,1,0:T(8,128)} dynamic-update-slice(f32[3,32,32,128]{3,2,1,0:T(8,128)} %get-tuple-element.578, f32[3,16,16,16]{3,2,1,0:T(8,128)S(1)} %bitcast_add_fusion.2, s32[]{:T(128)} %constant.445.clone.1..sunk.1, s32[]{:T(128)S(6)} %select_n.609, s32[]{:T(128)S(6)} %select_n.610, s32[]{:T(128)S(6)} %select_n.611) | dynamic-update-slice | bytes 98308 | tf_op jit(solution)/shard_map/while/body/eval_jaxpr/dynamic_update_slice | solution.py:221
  958.9 20.0 %dynamic_update_slice.8 = f32[3,32,32,128]{3,2,1,0:T(8,128)} dynamic-update-slice(f32[3,32,32,128]{3,2,1,0:T(8,128)} %get-tuple-element.578, f32[3,16,16,16]{3,2,1,0:T(8,128)S(1)} %bitcast_add_fusion.2, s32[]{:T(128)} %constant.445.clone.1..sunk.1, s32[]{:T(128)S(6)} %select_n.609, s32[]{:T(128)S(6)} %select_n.610, s32[]{:T(128)S(6)} %select_n.611) | dynamic-update-slice | bytes 98308 | tf_op jit(solution)/shard_map/while/body/eval_jaxpr/dynamic_update_slice | solution.py:221
  986.6 20.0 %dynamic_update_slice.8 = f32[3,32,32,128]{3,2,1,0:T(8,128)} dynamic-update-slice(f32[3,32,32,128]{3,2,1,0:T(8,128)} %get-tuple-element.578, f32[3,16,16,16]{3,2,1,0:T(8,128)S(1)} %bitcast_add_fusion.2, s32[]{:T(128)} %constant.445.clone.1..sunk.1, s32[]{:T(128)S(6)} %select_n.609, s32[]{:T(128)S(6)} %select_n.610, s32[]{:T(128)S(6)} %select_n.611) | dynamic-update-slice | bytes 98308 | tf_op jit(solution)/shard_map/while/body/eval_jaxpr/dynamic_update_slice | solution.py:221
  1014.3 20.0 %dynamic_update_slice.8 = f32[3,32,32,128]{3,2,1,0:T(8,128)} dynamic-update-slice(f32[3,32,32,128]{3,2,1,0:T(8,128)} %get-tuple-element.578, f32[3,16,16,16]{3,2,1,0:T(8,128)S(1)} %bitcast_add_fusion.2, s32[]{:T(128)} %constant.445.clone.1..sunk.1, s32[]{:T(128)S(6)} %select_n.609, s32[]{:T(128)S(6)} %select_n.610, s32[]{:T(128)S(6)} %select_n.611) | dynamic-update-slice | bytes 98308 | tf_op jit(solution)/shard_map/while/body/eval_jaxpr/dynamic_update_slice | solution.py:221
  1069.8 20.0 %dynamic_update_slice.8 = f32[3,32,32,128]{3,2,1,0:T(8,128)} dynamic-update-slice(f32[3,32,32,128]{3,2,1,0:T(8,128)} %get-tuple-element.578, f32[3,16,16,16]{3,2,1,0:T(8,128)S(1)} %bitcast_add_fusion.2, s32[]{:T(128)} %constant.445.clone.1..sunk.1, s32[]{:T(128)S(6)} %select_n.609, s32[]{:T(128)S(6)} %select_n.610, s32[]{:T(128)S(6)} %select_n.611) | dynamic-update-slice | bytes 98308 | tf_op jit(solution)/shard_map/while/body/eval_jaxpr/dynamic_update_slice | solution.py:221
  1097.6 20.0 %dynamic_update_slice.8 = f32[3,32,32,128]{3,2,1,0:T(8,128)} dynamic-update-slice(f32[3,32,32,128]{3,2,1,0:T(8,128)} %get-tuple-element.578, f32[3,16,16,16]{3,2,1,0:T(8,128)S(1)} %bitcast_add_fusion.2, s32[]{:T(128)} %constant.445.clone.1..sunk.1, s32[]{:T(128)S(6)} %select_n.609, s32[]{:T(128)S(6)} %select_n.610, s32[]{:T(128)S(6)} %select_n.611) | dynamic-update-slice | bytes 98308 | tf_op jit(solution)/shard_map/while/body/eval_jaxpr/dynamic_update_slice | solution.py:221
  1125.3 20.0 %dynamic_update_slice.8 = f32[3,32,32,128]{3,2,1,0:T(8,128)} dynamic-update-slice(f32[3,32,32,128]{3,2,1,0:T(8,128)} %get-tuple-element.578, f32[3,16,16,16]{3,2,1,0:T(8,128)S(1)} %bitcast_add_fusion.2, s32[]{:T(128)} %constant.445.clone.1..sunk.1, s32[]{:T(128)S(6)} %select_n.609, s32[]{:T(128)S(6)} %select_n.610, s32[]{:T(128)S(6)} %select_n.611) | dynamic-update-slice | bytes 98308 | tf_op jit(solution)/shard_map/while/body/eval_jaxpr/dynamic_update_slice | solution.py:221
  1153.1 20.0 %dynamic_update_slice.8 = f32[3,32,32,128]{3,2,1,0:T(8,128)} dynamic-update-slice(f32[3,32,32,128]{3,2,1,0:T(8,128)} %get-tuple-element.578, f32[3,16,16,16]{3,2,1,0:T(8,128)S(1)} %bitcast_add_fusion.2, s32[]{:T(128)} %constant.445.clone.1..sunk.1, s32[]{:T(128)S(6)} %select_n.609, s32[]{:T(128)S(6)} %select_n.610, s32[]{:T(128)S(6)} %select_n.611) | dynamic-update-slice | bytes 98308 | tf_op jit(solution)/shard_map/while/body/eval_jaxpr/dynamic_update_slice | solution.py:221
  1208.6 20.0 %dynamic_update_slice.8 = f32[3,32,32,128]{3,2,1,0:T(8,128)} dynamic-update-slice(f32[3,32,32,128]{3,2,1,0:T(8,128)} %get-tuple-element.578, f32[3,16,16,16]{3,2,1,0:T(8,128)S(1)} %bitcast_add_fusion.2, s32[]{:T(128)} %constant.445.clone.1..sunk.1, s32[]{:T(128)S(6)} %select_n.609, s32[]{:T(128)S(6)} %select_n.610, s32[]{:T(128)S(6)} %select_n.611) | dynamic-update-slice | bytes 98308 | tf_op jit(solution)/shard_map/while/body/eval_jaxpr/dynamic_update_slice | solution.py:221
  1236.3 20.0 %dynamic_update_slice.8 = f32[3,32,32,128]{3,2,1,0:T(8,128)} dynamic-update-slice(f32[3,32,32,128]{3,2,1,0:T(8,128)} %get-tuple-element.578, f32[3,16,16,16]{3,2,1,0:T(8,128)S(1)} %bitcast_add_fusion.2, s32[]{:T(128)} %constant.445.clone.1..sunk.1, s32[]{:T(128)S(6)} %select_n.609, s32[]{:T(128)S(6)} %select_n.610, s32[]{:T(128)S(6)} %select_n.611) | dynamic-update-slice | bytes 98308 | tf_op jit(solution)/shard_map/while/body/eval_jaxpr/dynamic_update_slice | solution.py:221
  1264.0 20.0 %dynamic_update_slice.8 = f32[3,32,32,128]{3,2,1,0:T(8,128)} dynamic-update-slice(f32[3,32,32,128]{3,2,1,0:T(8,128)} %get-tuple-element.578, f32[3,16,16,16]{3,2,1,0:T(8,128)S(1)} %bitcast_add_fusion.2, s32[]{:T(128)} %constant.445.clone.1..sunk.1, s32[]{:T(128)S(6)} %select_n.609, s32[]{:T(128)S(6)} %select_n.610, s32[]{:T(128)S(6)} %select_n.611) | dynamic-update-slice | bytes 98308 | tf_op jit(solution)/shard_map/while/body/eval_jaxpr/dynamic_update_slice | solution.py:221
  1319.5 20.0 %dynamic_update_slice.8 = f32[3,32,32,128]{3,2,1,0:T(8,128)} dynamic-update-slice(f32[3,32,32,128]{3,2,1,0:T(8,128)} %get-tuple-element.578, f32[3,16,16,16]{3,2,1,0:T(8,128)S(1)} %bitcast_add_fusion.2, s32[]{:T(128)} %constant.445.clone.1..sunk.1, s32[]{:T(128)S(6)} %select_n.609, s32[]{:T(128)S(6)} %select_n.610, s32[]{:T(128)S(6)} %select_n.611) | dynamic-update-slice | bytes 98308 | tf_op jit(solution)/shard_map/while/body/eval_jaxpr/dynamic_update_slice | solution.py:221
  1347.3 20.0 %dynamic_update_slice.8 = f32[3,32,32,128]{3,2,1,0:T(8,128)} dynamic-update-slice(f32[3,32,32,128]{3,2,1,0:T(8,128)} %get-tuple-element.578, f32[3,16,16,16]{3,2,1,0:T(8,128)S(1)} %bitcast_add_fusion.2, s32[]{:T(128)} %constant.445.clone.1..sunk.1, s32[]{:T(128)S(6)} %select_n.609, s32[]{:T(128)S(6)} %select_n.610, s32[]{:T(128)S(6)} %select_n.611) | dynamic-update-slice | bytes 98308 | tf_op jit(solution)/shard_map/while/body/eval_jaxpr/dynamic_update_slice | solution.py:221
  1375.0 20.0 %dynamic_update_slice.8 = f32[3,32,32,128]{3,2,1,0:T(8,128)} dynamic-update-slice(f32[3,32,32,128]{3,2,1,0:T(8,128)} %get-tuple-element.578, f32[3,16,16,16]{3,2,1,0:T(8,128)S(1)} %bitcast_add_fusion.2, s32[]{:T(128)} %constant.445.clone.1..sunk.1, s32[]{:T(128)S(6)} %select_n.609, s32[]{:T(128)S(6)} %select_n.610, s32[]{:T(128)S(6)} %select_n.611) | dynamic-update-slice | bytes 98308 | tf_op jit(solution)/shard_map/while/body/eval_jaxpr/dynamic_update_slice | solution.py:221
  1402.8 20.0 %dynamic_update_slice.8 = f32[3,32,32,128]{3,2,1,0:T(8,128)} dynamic-update-slice(f32[3,32,32,128]{3,2,1,0:T(8,128)} %get-tuple-element.578, f32[3,16,16,16]{3,2,1,0:T(8,128)S(1)} %bitcast_add_fusion.2, s32[]{:T(128)} %constant.445.clone.1..sunk.1, s32[]{:T(128)S(6)} %select_n.609, s32[]{:T(128)S(6)} %select_n.610, s32[]{:T(128)S(6)} %select_n.611) | dynamic-update-slice | bytes 98308 | tf_op jit(solution)/shard_map/while/body/eval_jaxpr/dynamic_update_slice | solution.py:221
  (668 shorter events, 502.5 us)
Async XLA Ops:
  2.1 341.9 %collective-permute-start = (f32[3,1,32,128]{3,2,1,0:T(8,128)}, f32[3,1,32,128]{3,2,1,0:T(8,128)}, u32[]{:S(2)}, u32[]{:S(2)}) collective-permute-start(f32[3,1,32,128]{3,2,1,0:T(8,128)} %get-tuple-element.335), channel_id=1, source_target_pairs={{32,0},{64,32},{96,64},{128,96},{160,128},{192,160},{224,192},{0,2... | collective-permute-start | bytes 147464 | tf_op jit(solution)/shard_map/ppermute | solution.py:29
  5.3 337.7 %collective-permute-start.1 = (f32[3,1,32,128]{3,2,1,0:T(8,128)}, f32[3,1,32,128]{3,2,1,0:T(8,128)}, u32[]{:S(2)}, u32[]{:S(2)}) collective-permute-start(f32[3,1,32,128]{3,2,1,0:T(8,128)} %get-tuple-element.336), channel_id=1, source_target_pairs={{0,32},{32,64},{64,96},{96,128},{128,160},{160,192},{192,224},{224... | collective-permute-start | bytes 147464 | tf_op jit(solution)/shard_map/ppermute | solution.py:28
  6.9 25.8 %copy-start.62 = (pred[32]{0:T(512)(128)(4,1)}, pred[32]{0:T(512)(128)(4,1)S(1)}, u32[]{:S(2)}) copy-start(pred[32]{0:T(512)(128)(4,1)S(1)} %compare_and_fusion.2) | copy-start | bytes 100
  31.1 6.2 copy-start.64
  31.1 6.8 copy-start
  32.7 367.3 %all-to-all-start = ((f32[32,16,256]{2,1,0:T(8,128)}), f32[32,16,256]{2,1,0:T(8,128)}, u32[]{:S(2)}, u32[]{:S(2)}) async-start(f32[32,16,256]{2,1,0:T(8,128)} %broadcast_select_fusion.4), calls=%async_computation | async-start | bytes 1048576 | tf_op jit(solution)/shard_map/all_to_all | solution.py:190
  39.8 371.7 %copy-start.56 = (pred[16]{0:T(512)(128)(4,1)}, pred[16]{0:T(512)(128)(4,1)S(1)}, u32[]{:S(2)}) copy-start(pred[16]{0:T(512)(128)(4,1)S(1)} %compare_and_fusion.3) | copy-start | bytes 52
  344.9 4.3 collective-permute-start.3
  346.0 3.1 collective-permute-start.2
  356.9 6.3 collective-permute-start.5
  358.0 3.0 collective-permute-start.4
  359.7 49.8 %copy-start.60 = (s32[1024]{0:T(1024)}, s32[1024]{0:T(1024)S(1)}, u32[]{:S(2)}) copy-start(s32[1024]{0:T(1024)S(1)} %pad_clamp_fusion.2) | copy-start | bytes 12292
  372.0 9.6 collective-permute-start.7
  380.0 3.5 collective-permute-start.6
  380.9 31.7 %copy-start.46 = (pred[256]{0:T(512)(128)(4,1)}, pred[256]{0:T(512)(128)(4,1)S(1)}, u32[]{:S(2)}) copy-start(pred[256]{0:T(512)(128)(4,1)S(1)} %get-tuple-element.404) | copy-start | bytes 772
  381.0 33.3 %copy-start.43 = (pred[256]{0:T(512)(128)(4,1)}, pred[256]{0:T(512)(128)(4,1)S(1)}, u32[]{:S(2)}) copy-start(pred[256]{0:T(512)(128)(4,1)S(1)} %get-tuple-element.403) | copy-start | bytes 772
  381.6 6.6 copy-start.32
  383.6 4.3 collective-permute-start.9
  385.0 3.0 collective-permute-start.8
  386.6 25.4 %copy-start.52 = (pred[256]{0:T(512)(128)(4,1)}, pred[256]{0:T(512)(128)(4,1)S(1)}, u32[]{:S(2)}) copy-start(pred[256]{0:T(512)(128)(4,1)S(1)} %get-tuple-element.402) | copy-start | bytes 772
  386.6 27.3 %copy-start.49 = (pred[256]{0:T(512)(128)(4,1)}, pred[256]{0:T(512)(128)(4,1)S(1)}, u32[]{:S(2)}) copy-start(pred[256]{0:T(512)(128)(4,1)S(1)} %get-tuple-element.401) | copy-start | bytes 772
  397.3 106.8 %collective-permute-start.11 = (f32[3,34,34,1]{2,3,1,0:T(1,128)}, f32[3,34,34,1]{2,3,1,0:T(1,128)}, u32[]{:S(2)}, u32[]{:S(2)}) collective-permute-start(f32[3,34,34,1]{2,3,1,0:T(1,128)} %copy.90), channel_id=1, source_target_pairs={{0,1},{1,2},{2,3},{3,4},{4,5},{5,6},{6,7},{7,0},{8,9},{9,10},{10,1... | collective-permute-start | bytes 41624 | tf_op jit(solution)/shard_map/ppermute | solution.py:28
  398.4 102.7 %collective-permute-start.10 = (f32[3,34,34,1]{2,3,1,0:T(1,128)}, f32[3,34,34,1]{2,3,1,0:T(1,128)}, u32[]{:S(2)}, u32[]{:S(2)}) collective-permute-start(f32[3,34,34,1]{2,3,1,0:T(1,128)} %copy.89), channel_id=1, source_target_pairs={{1,0},{2,1},{3,2},{4,3},{5,4},{6,5},{7,6},{0,7},{9,8},{10,9},{11,1... | collective-permute-start | bytes 41624 | tf_op jit(solution)/shard_map/ppermute | solution.py:29
  400.0 41.3 %all-to-all-start.1 = ((f32[32,3,16,256]{3,2,1,0:T(8,128)}), f32[32,3,16,256]{3,2,1,0:T(8,128)}, u32[]{:S(2)}, u32[]{:S(2)}) async-start(f32[32,3,16,256]{3,2,1,0:T(8,128)} %broadcast_select_fusion), calls=%async_computation.1 | async-start | bytes 3145728 | tf_op jit(solution)/shard_map/all_to_all | solution.py:191
  417.5 26.8 %copy-start.40 = (f32[16,1,256]{2,1,0:T(1,128)}, f32[16,1,256]{2,1,0:T(1,128)S(1)}, u32[]{:S(2)}) copy-start(f32[16,1,256]{2,1,0:T(1,128)S(1)} %get-tuple-element.377) | copy-start | bytes 49156
  417.6 26.7 %copy-start.57 = (pred[16]{0:T(512)(128)(4,1)S(1)}, pred[16]{0:T(512)(128)(4,1)}, u32[]{:S(2)}) copy-start(pred[16]{0:T(512)(128)(4,1)} %copy-done.56) | copy-start | bytes 52
  419.3 26.4 %slice-start = ((f32[16,16,256]{2,1,0:T(8,128)}), f32[16,16,16]{2,1,0:T(8,128)S(1)}, s32[]{:S(2)}) async-start(f32[16,16,256]{2,1,0:T(8,128)} %copy-done.13), calls=%async_computation.4 | async-start | bytes 262144 | tf_op jit(solution)/shard_map/slice | solution.py:45
  489.6 24.7 %all-to-all-start.3 = ((f32[32,16,256]{2,1,0:T(8,128)}), f32[32,16,256]{2,1,0:T(8,128)}, u32[]{:S(2)}, u32[]{:S(2)}) async-start(f32[32,16,256]{2,1,0:T(8,128)} %get-tuple-element.397), calls=%async_computation.3 | async-start | bytes 1048576 | tf_op jit(solution)/shard_map/all_to_all | solution.py:205
  514.2 10.7 copy-start.58
  514.2 10.7 copy-start.59
  514.2 20.5 %all-to-all-start.2 = ((f32[32,16,256]{2,1,0:T(8,128)}), f32[32,16,256]{2,1,0:T(8,128)S(1)}, u32[]{:S(2)}, u32[]{:S(2)}) async-start(f32[32,16,256]{2,1,0:T(8,128)} %get-tuple-element.396), calls=%async_computation.2 | async-start | bytes 1048576 | tf_op jit(solution)/shard_map/all_to_all | solution.py:206
  550.2 12.5 copy-start.42
  (74 other events, 123.0 us)
where the time goes:
time: 1470 us; the launch traced here: 1450 us
  local copies, waits for them, and re-layouts  812 us (55%)
  loops' own time  364 us (25%)
  other arithmetic  163 us (11%)
  starting transfers between devices  56.8 us (4%)
  waiting for transfers between devices  33.6 us (2%)
  blocking collectives  18.6 us (1%)
    dynamic_update_slice x32, local copies, waits for them, and re-layouts, deposit_slot(): lax.dynamic_update_slice(grid_now, region + grid_step * push_boxes[slot_n...  640 us
    another operation x1, loops' own time, local(): result = lax.fori_loop(0, slot_count, deposit_slot, stepped)  182 us
    another operation x1, loops' own time, local(): lax.fori_loop(0, slot_count, cut_slot, jnp.zeros((slot_count, 3, box_edge...  180 us
    scatter x32, other arithmetic, cut_slot(): boxes_now.at[slot_no].set(region.reshape(3, box_edge, box_edge * box_edge))  44 us
    add x32, other arithmetic, deposit_slot(): region + grid_step * push_boxes[slot_no]  43.9 us
  transfers between devices with their start and end apart: 16, of which 7 were waited for; matrix products, arithmetic and copies ran while one was open for 16% of the time, Pallas kernels for 0%

commit v1 on v0

v1 whole, which is shorter than its diff:
```python
import functools
import math

import jax
import jax.numpy as jnp
from jax import lax
from jax.experimental import pallas as pl
from jax.experimental.pallas import tpu as pltpu
from jax.sharding import PartitionSpec as P

ITERS = 12
BOX = 16
LANES = 128
PER = 8

box_step = 0.25
pseudo_step = 0.3
weno_floor = 1e-06
band_width = 1.5
tension = 2.0
grid_step = 0.2
viscosity = 0.1
normal_floor = 0.5

F32 = jnp.float32
TILE = (8, LANES)


def iotas():
    row = lax.broadcasted_iota(jnp.int32, TILE, 0)
    lane = lax.broadcasted_iota(jnp.int32, TILE, 1)
    return row, lane


def block_transpose(x, row, lane):
    block = lane // BOX
    for s in (4, 2, 1):
        r_bit = (row // s) % 2
        q_bit = (block // s) % 2
        down = pltpu.roll(pltpu.roll(x, s, 0), LANES - BOX * s, 1)
        if s == 4:
            moved = down
        else:
            up = pltpu.roll(pltpu.roll(x, 8 - s, 0), BOX * s, 1)
            moved = jnp.where(r_bit == 1, down, up)
        x = jnp.where(r_bit == q_bit, x, moved)
    return x


def weno(a, b, c, e, f):
    ab, bc, ce, ef = a - b, b - c, c - e, e - f
    d1, d2, d3 = ab - bc, bc - ce, ce - ef
    bc2, ce2 = bc + bc, ce + ce
    t1, t2, t3 = d1 - bc2, bc + ce, d3 + ce2
    part = 3.0 / 13.0
    floor = weno_floor * 12.0 / 13.0
    s1 = (d1 * d1 + floor) + part * (t1 * t1)
    s2 = (d2 * d2 + floor) + part * (t2 * t2)
    s3 = (d3 * d3 + floor) + part * (t3 * t3)
    q1, q2, q3 = s1 * s1, s2 * s2, s3 * s3
    w1 = q2 * q3
    w2 = 6.0 * (q1 * q3)
    w3 = 3.0 * (q1 * q2)
    top = w1 * ((ab + ab) - 5.0 * bc) - w2 * (bc + ce2) + w3 * (ef - (ce2 + ce2))
    return c + top / (6.0 * (w1 + w2 + w3))


def upwind(speed, back_two, back_one, here, ahead_one, ahead_two, ahead_three):
    pos = speed > 0.0
    return speed * weno(
        jnp.where(pos, back_two, ahead_three),
        jnp.where(pos, back_one, ahead_two),
        jnp.where(pos, here, ahead_one),
        jnp.where(pos, ahead_one, here),
        jnp.where(pos, ahead_two, back_one),
    )


ROWS = 32


def box_body(
    groups,
    first,
    owner_ref,
    corner_ref,
    vel_ref,
    level_lo,
    level_hi,
    *rest,
):
    if first:
        (force_out, settled_out, bending_out, *scratch) = rest
    else:
        (_, force_in, _, _, force_out, settled_out, bending_out, *scratch) = rest
    (u_ref, l_ref, mi_ref, mj_ref, pa, pb, c_ref, s_ref, k_ref, turned_s, turned_b) = scratch
    row, lane = iotas()
    k = lane % BOX
    block = lane // BOX
    k_first, k_last = k == 0, k == BOX - 1
    top, bottom = row == 0, row == 7

    if first:

        @pl.loop(0, 32)
        def _(x):
            for c in range(3):
                force_out[c, x] = jnp.zeros((32, LANES), F32)
    else:

        @pl.loop(0, 32)
        def _(x):
            for c in range(3):
                force_out[c, x] = force_in[c, x]

    def next_k(v):
        return jnp.where(k_last, v, pltpu.roll(v, LANES - 1, 1))

    def prev_k(v):
        return jnp.where(k_first, v, pltpu.roll(v, 1, 1))

    def one_group(g):
        spots = [
            [corner_ref[g * PER + b, d] for d in range(3)] for b in range(PER)
        ]
        alive = jnp.zeros(TILE, F32)
        for b in range(PER):
            living = jnp.where(owner_ref[g * PER + b] >= 0, 1.0, 0.0)
            alive = jnp.where(block == b, living, alive)

        @pl.loop(0, BOX)
        def _(i):
            for jt in range(2):
                for c in range(3):
                    total = jnp.zeros(TILE, F32)
                    for b in range(PER):
                        px, py, pz = spots[b]
                        part = vel_ref[c, px + i, pl.ds(py + 8 * jt, 8), :]
                        part = pltpu.roll(part, (BOX * b + LANES - pz) % LANES, 1)
                        total = part if b == 0 else jnp.where(block == b, part, total)
                    u_ref[c, i, pl.ds(8 * jt, 8), :] = total
                level = (level_lo, level_hi)[jt]
                x = level[pl.ds(g * (PER * BOX) + i, 8, stride=BOX), :]
                l_ref[i, pl.ds(8 + 8 * jt, 8), :] = block_transpose(x, row, lane)

        mi_ref[0] = jnp.zeros((BOX, LANES), F32)
        mi_ref[1] = jnp.zeros((BOX, LANES), F32)
        mi_ref[2] = jnp.zeros((BOX, LANES), F32)

        @pl.loop(1, BOX)
        def _(i):
            for jt in range(2):
                at = pl.ds(8 + 8 * jt, 8)
                mi_ref[i + 2, pl.ds(8 * jt, 8), :] = l_ref[i, at, :] - l_ref[i - 1, at, :]

        for t in range(3):
            mi_ref[18 + t] = mi_ref[17]

        @pl.loop(0, BOX)
        def _(i):
            for jt in range(2):
                here = l_ref[i, pl.ds(8 + 8 * jt, 8), :]
                m = here - l_ref[i, pl.ds(7 + 8 * jt, 8), :]
                if jt == 0:
                    m = jnp.where(top, 0.0, m)
                    mj_ref[i, pl.ds(0, 8), :] = jnp.zeros(TILE, F32)
                else:
                    mj_ref[i, pl.ds(24, 8), :] = jnp.broadcast_to(m[7:8, :], TILE)
                mj_ref[i, pl.ds(8 + 8 * jt, 8), :] = m

        @pl.loop(0, BOX)
        def _(i):
            for jt in range(2):
                at = pl.ds(8 * jt, 8)
                padded_at = pl.ds(8 + 8 * jt, 8)
                here = l_ref[i, padded_at, :]
                change = upwind(u_ref[0, i, at, :], *[mi_ref[i + t, at, :] for t in range(6)])
                change += upwind(
                    u_ref[1, i, at, :],
                    *[mj_ref[i, pl.ds(6 + t + 8 * jt, 8), :] for t in range(6)],
                )
                m = here - prev_k(here)
                back_one = prev_k(m)
                ahead_one = next_k(m)
                ahead_two = next_k(ahead_one)
                change += upwind(
                    u_ref[2, i, at, :],
                    prev_k(back_one),
                    back_one,
                    m,
                    ahead_one,
                    ahead_two,
                    next_k(ahead_two),
                )
                advected = here - box_step * change
                pa[i, padded_at, :] = advected
                c_ref[i, at, :] = pseudo_step * advected * lax.rsqrt(advected * advected + 1.0)
                s_ref[i, at, :] = jnp.where(advected > 0.0, 1.0, -1.0)

        def sweep(src, dst):
            for jt in range(2):
                at = pl.ds(8 * jt, 8)
                behind_i = None
                cur = src[0, pl.ds(8 + 8 * jt, 8), :]
                for i in range(BOX):
                    s = s_ref[i, at, :]
                    terms = []
                    if i < BOX - 1:
                        nxt = src[i + 1, pl.ds(8 + 8 * jt, 8), :]
                        down_i = cur - nxt
                    else:
                        nxt = down_i = None
                    if behind_i is None:
                        terms.append(jnp.maximum(s * down_i, 0.0))
                    elif down_i is None:
                        terms.append(jnp.maximum(-(s * behind_i), 0.0))
                    else:
                        terms.append(
                            jnp.maximum(jnp.maximum(s * down_i, -(s * behind_i)), 0.0)
                        )
                    below = cur - src[i, pl.ds(7 + 8 * jt, 8), :]
                    above = cur - src[i, pl.ds(9 + 8 * jt, 8), :]
                    if jt == 0:
                        below = jnp.where(top, 0.0, below)
                    else:
                        above = jnp.where(bottom, 0.0, above)
                    terms.append(jnp.maximum(jnp.maximum(s * below, s * above), 0.0))
                    down_k = jnp.where(k_last, 0.0, cur - pltpu.roll(cur, LANES - 1, 1))
                    up_k = pltpu.roll(down_k, 1, 1)
                    terms.append(jnp.maximum(jnp.maximum(s * down_k, -(s * up_k)), 0.0))
                    squared = terms[0] * terms[0] + terms[1] * terms[1] + terms[2] * terms[2]
                    root = squared * lax.rsqrt(jnp.maximum(squared, 1e-37))
                    dst[i, pl.ds(8 + 8 * jt, 8), :] = cur - c_ref[i, at, :] * (root - 1.0)
                    behind_i, cur = down_i, nxt

        @pl.loop(0, ITERS // 2)
        def _(_):
            sweep(pa, pb)
            sweep(pb, pa)

        def central(i, jt):
            at = pl.ds(8 + 8 * jt, 8)
            cur = pa[i, at, :]
            c0 = 0.5 * (pa[jnp.minimum(i + 1, BOX - 1), at, :] - pa[jnp.maximum(i - 1, 0), at, :])
            lower = pa[i, pl.ds(7 + 8 * jt, 8), :]
            upper = pa[i, pl.ds(9 + 8 * jt, 8), :]
            if jt == 0:
                lower = jnp.where(top, cur, lower)
            else:
                upper = jnp.where(bottom, cur, upper)
            c1 = 0.5 * (upper - lower)
            c2 = 0.5 * (next_k(cur) - prev_k(cur))
            return cur, c0, c1, c2

        @pl.loop(0, BOX)
        def _(i):
            for jt in range(2):
                cur, c0, c1, c2 = central(i, jt)
                size = c0 * c0 + c1 * c1 + c2 * c2
                inverse = jnp.minimum(lax.rsqrt(size), 1.0 / normal_floor)
                at = pl.ds(8 * jt, 8)
                mi_ref[i, at, :] = c0 * inverse
                mj_ref[i, pl.ds(8 + 8 * jt, 8), :] = c1 * inverse
                n3 = c2 * inverse
                k_ref[i, at, :] = next_k(n3) - prev_k(n3)
                scaled = cur * (1.0 / band_width)
                band = jnp.exp(-(scaled * scaled)) * (
                    grid_step * tension / (band_width * math.sqrt(math.pi))
                )
                band = band * alive
                u_ref[0, i, at, :] = band * c0
                u_ref[1, i, at, :] = band * c1
                u_ref[2, i, at, :] = band * c2
                y = block_transpose(cur * alive, row, lane)
                turned_s[pl.ds(jt * (PER * BOX) + i, 8, stride=BOX), :] = y

        @pl.loop(0, BOX)
        def _(i):
            for jt in range(2):
                at = pl.ds(8 * jt, 8)
                padded_at = pl.ds(8 + 8 * jt, 8)
                d1 = mi_ref[jnp.minimum(i + 1, BOX - 1), at, :] - mi_ref[jnp.maximum(i - 1, 0), at, :]
                lower = mj_ref[i, pl.ds(7 + 8 * jt, 8), :]
                upper = mj_ref[i, pl.ds(9 + 8 * jt, 8), :]
                if jt == 0:
                    lower = jnp.where(top, mj_ref[i, padded_at, :], lower)
                else:
                    upper = jnp.where(bottom, mj_ref[i, padded_at, :], upper)
                kappa = 0.5 * (d1 + (upper - lower) + k_ref[i, at, :])
                for c in range(3):
                    u_ref[c, i, at, :] = u_ref[c, i, at, :] * kappa
                y = block_transpose(kappa * alive, row, lane)
                turned_b[pl.ds(jt * (PER * BOX) + i, 8, stride=BOX), :] = y

        for jt in range(2):
            here = pl.ds(jt * (PER * BOX), PER * BOX)
            there = pl.ds(pl.multiple_of(g * (PER * BOX), PER * BOX), PER * BOX)
            settled_out[there, pl.ds(LANES * jt, LANES)] = turned_s[here, :]
            bending_out[there, pl.ds(LANES * jt, LANES)] = turned_b[here, :]

        for b in range(PER):
            px, py, pz = spots[b]
            inside = (lane >= pz) & (lane < pz + BOX)
            turn = (pz + LANES - BOX * b) % LANES

            @pl.loop(0, 3 * BOX // 8)
            def _(step):
                c = step // 2
                i0 = (step % 2) * 8
                sums = []
                for i in range(8):
                    for jt in range(2):
                        old = force_out[c, px + i0 + i, pl.ds(py + 8 * jt, 8), :]
                        push = pltpu.roll(u_ref[c, i0 + i, pl.ds(8 * jt, 8), :], turn, 1)
                        sums.append(old + jnp.where(inside, push, 0.0))
                for i in range(8):
                    for jt in range(2):
                        force_out[c, px + i0 + i, pl.ds(py + 8 * jt, 8), :] = sums[2 * i + jt]

    @pl.loop(groups[0], groups[1])
    def _(g):
        one_group(g)


def boxes(groups, owner, corners, velocity, level_rows, carried=None):
    first = carried is None
    smem = pl.BlockSpec(memory_space=pltpu.SMEM)
    vmem = pl.BlockSpec(memory_space=pltpu.VMEM)
    halves = [
        pl.BlockSpec((level_rows.shape[0], LANES), functools.partial(lambda h, s: (0, h), h))
        for h in range(2)
    ]
    whole = pl.BlockSpec(velocity.shape, lambda s: (0, 0, 0, 0))
    rows = pl.BlockSpec(level_rows.shape, lambda s: (0, 0))
    any_ = pl.BlockSpec(memory_space=pl.ANY)
    specs = [smem, smem, whole, *halves]
    operands = [owner, corners, velocity, level_rows, level_rows]
    plane = lambda *lead: pltpu.VMEM((*lead, LANES), F32)
    return pl.pallas_call(
        functools.partial(box_body, groups, first),
        grid=(1,),
        out_shape=(
            jax.ShapeDtypeStruct(velocity.shape, F32),
            jax.ShapeDtypeStruct(level_rows.shape, F32),
            jax.ShapeDtypeStruct(level_rows.shape, F32),
        ),
        in_specs=specs,
        out_specs=(whole, rows, rows),
        scratch_shapes=[
            plane(3, BOX, BOX),
            plane(BOX, ROWS),
            plane(BOX + 5, BOX),
            plane(BOX, ROWS),
            plane(BOX, ROWS),
            plane(BOX, ROWS),
            plane(BOX, BOX),
            plane(BOX, BOX),
            plane(BOX, BOX),
            plane(2 * PER * BOX),
            plane(2 * PER * BOX),
        ],
        compiler_params=pltpu.CompilerParams(vmem_limit_bytes=32 * 2**20),
        cost_estimate=pl.CostEstimate(flops=60_000_000, bytes_accessed=5_000_000, transcendentals=0),
        name="boxes",
    )(*operands)


PLANE = 48


def take_faces(load, faces):
    xlo, xhi, ylo, yhi, zlo, zhi = faces
    row, lane = iotas()

    def one(x, packed):
        out = []
        for c in range(3):
            lo, hi = packed[2 * c], packed[2 * c + 1]
            for yt in range(4):
                n = x * 4 + yt
                turned = pltpu.roll(load(c, x, yt), n, 1)
                lo = jnp.where(lane == n, turned, lo)
                hi = jnp.where(lane == (n + LANES - 1) % LANES, turned, hi)
            out += [lo, hi]
        return tuple(out)

    packed = lax.fori_loop(0, 32, one, (jnp.zeros(TILE, F32),) * 6)
    for c in range(3):
        zlo[c] = packed[2 * c]
        zhi[c] = packed[2 * c + 1]


def faces_body(vel_ref, *faces):
    xlo, xhi, ylo, yhi, _, _ = faces
    for c in range(3):
        xlo[c] = vel_ref[pl.ds(c * 1024, 32), :]
        xhi[c] = vel_ref[pl.ds(c * 1024 + 31 * 32, 32), :]
        ylo[c] = vel_ref[pl.ds(c * 1024, 32, stride=32), :]
        yhi[c] = vel_ref[pl.ds(c * 1024 + 31, 32, stride=32), :]
    take_faces(
        lambda c, x, yt: vel_ref[pl.ds(pl.multiple_of(c * 1024 + x * 32 + 8 * yt, 8), 8), :],
        faces,
    )


FACES = tuple([(3, 32, LANES)] * 4 + [(3, 8, LANES)] * 2)


def faces_of(rows):
    vmem = pl.BlockSpec(memory_space=pltpu.VMEM)
    return pl.pallas_call(
        faces_body,
        out_shape=tuple(jax.ShapeDtypeStruct(s, F32) for s in FACES),
        in_specs=[vmem],
        out_specs=(vmem,) * 6,
        compiler_params=pltpu.CompilerParams(vmem_limit_bytes=16 * 2**20),
        name="faces",
    )(rows)


def exchange(faces):
    halos = []
    for d, axis in enumerate(("gx", "gy", "gz")):
        size = lax.axis_size(axis)
        up = [(i, (i + 1) % size) for i in range(size)]
        down = [(j, i) for i, j in up]
        halos.append(lax.ppermute(faces[2 * d + 1], axis, up))
        halos.append(lax.ppermute(faces[2 * d], axis, down))
    return halos


def fill_padded(src_ref, halos, ext):
    xlo, xhi, ylo, yhi, _, _ = halos
    for c in range(3):
        base = c * 34 * PLANE
        ext[pl.ds(base + 8, 32), :] = xlo[c]
        ext[pl.ds(base + 33 * PLANE + 8, 32), :] = xhi[c]
        ext[pl.ds(base + PLANE + 7, 32, stride=PLANE), :] = ylo[c]
        ext[pl.ds(base + PLANE + 40, 32, stride=PLANE), :] = yhi[c]

    @pl.loop(0, 32)
    def _(x):
        for c in range(3):
            at = pl.multiple_of(c * 34 * PLANE + (x + 1) * PLANE + 8, 8)
            ext[pl.ds(at, 32), :] = src_ref[pl.ds(pl.multiple_of(c * 1024 + x * 32, 8), 32), :]


def tendencies(ext, zlo, zhi, x, yt, lane):
    n = x * 4 + yt
    at = [
        pl.multiple_of(c * 34 * PLANE + (x + 1) * PLANE + 8 + 8 * yt, 8) for c in range(3)
    ]
    centre = [ext[pl.ds(at[c], 8), :] for c in range(3)]
    out = []
    for c in range(3):
        v = centre[c]
        up0 = ext[pl.ds(at[c] + PLANE, 8), :]
        lo0 = ext[pl.ds(at[c] - PLANE, 8), :]
        up1 = ext[pl.ds(at[c] + 1, 8), :]
        lo1 = ext[pl.ds(at[c] - 1, 8), :]
        lo2 = jnp.where(
            lane == 0, pltpu.roll(zlo[c], (LANES + 1 - n) % LANES, 1), pltpu.roll(v, 1, 1)
        )
        up2 = jnp.where(
            lane == LANES - 1,
            pltpu.roll(zhi[c], LANES - 1 - n, 1),
            pltpu.roll(v, LANES - 1, 1),
        )
        advect = centre[0] * (up0 - lo0) + centre[1] * (up1 - lo1) + centre[2] * (up2 - lo2)
        spread = (up0 + lo0) + (up1 + lo1) + (up2 + lo2) - 6.0 * v
        out.append(viscosity * spread - 0.5 * advect)
    return centre, out


def predictor_body(vel_ref, *refs):
    halos, out_ref, faces, ext = refs[:6], refs[6], refs[7:13], refs[13]
    fill_padded(vel_ref, halos, ext)
    row, lane = iotas()
    zlo, zhi = halos[4], halos[5]

    @pl.loop(0, 32)
    def _(x):
        zl = [zlo[c] for c in range(3)]
        zh = [zhi[c] for c in range(3)]
        for yt in range(4):
            centre, f = tendencies(ext, zl, zh, x, yt, lane)
            for c in range(3):
                out_ref[pl.ds(pl.multiple_of(c * 1024 + x * 32 + 8 * yt, 8), 8), :] = (
                    centre[c] + grid_step * f[c]
                )

    faces_body(out_ref, *faces)


def predictor_of(rows, halos):
    vmem = pl.BlockSpec(memory_space=pltpu.VMEM)
    return pl.pallas_call(
        predictor_body,
        out_shape=(
            jax.ShapeDtypeStruct(rows.shape, F32),
            *(jax.ShapeDtypeStruct(s, F32) for s in FACES),
        ),
        in_specs=[vmem] * 7,
        out_specs=(vmem,) * 7,
        scratch_shapes=[pltpu.VMEM((3 * 34 * PLANE, LANES), F32)],
        compiler_params=pltpu.CompilerParams(vmem_limit_bytes=24 * 2**20),
        name="predictor",
    )(rows, *halos)


def final_body(vel_ref, pred_ref, force_ref, *refs):
    halos, out_ref, ext = refs[:6], refs[6], refs[7]
    fill_padded(pred_ref, halos, ext)
    row, lane = iotas()
    zlo, zhi = halos[4], halos[5]

    @pl.loop(0, 32)
    def _(x):
        zl = [zlo[c] for c in range(3)]
        zh = [zhi[c] for c in range(3)]
        for yt in range(4):
            centre, f = tendencies(ext, zl, zh, x, yt, lane)
            for c in range(3):
                at = pl.ds(pl.multiple_of(c * 1024 + x * 32 + 8 * yt, 8), 8)
                second = centre[c] + grid_step * f[c]
                out_ref[at, :] = 0.5 * (vel_ref[at, :] + second) + force_ref[at, :]


def final_of(rows, predictor, force, halos):
    vmem = pl.BlockSpec(memory_space=pltpu.VMEM)
    return pl.pallas_call(
        final_body,
        out_shape=jax.ShapeDtypeStruct(rows.shape, F32),
        in_specs=[vmem] * 9,
        out_specs=vmem,
        scratch_shapes=[pltpu.VMEM((3 * 34 * PLANE, LANES), F32)],
        compiler_params=pltpu.CompilerParams(vmem_limit_bytes=24 * 2**20),
        name="final",
    )(rows, predictor, force, *halos)


def local(velocity, box_level, corners, owner_list):
    slots = box_level.shape[0]
    rows = velocity.reshape(-1, LANES)
    level_rows = box_level.reshape(slots * BOX, BOX * BOX)
    halos = exchange(faces_of(rows))
    force, settled, bending = boxes((0, slots // PER), owner_list, corners, velocity, level_rows)
    predictor, *faces = predictor_of(rows, halos)
    halos = exchange(faces)
    result = final_of(rows, predictor, force.reshape(rows.shape), halos)
    return (
        result.reshape(velocity.shape),
        settled.reshape(box_level.shape),
        bending.reshape(box_level.shape),
    )


def solution(mesh):
    placed = (
        P(None, "gx", "gy", "gz"),
        P(("gx", "gy", "gz"), None, None),
        P(("gx", "gy", "gz"), None),
        P(("gx", "gy", "gz")),
    )
    return jax.shard_map(
        local,
        mesh=mesh,
        in_specs=placed,
        out_specs=(
            P(None, "gx", "gy", "gz"),
            P(("gx", "gy", "gz"), None, None),
            P(("gx", "gy", "gz"), None, None),
        ),
        check_vma=False,
    )
```

time: 1470 us -> 139 us (0.09); the launches traced: 1450 us -> 137 us
  local copies, waits for them, and re-layouts: 812 us -> 2.64 us
  loops' own time: 364 us -> 0 us
  other arithmetic: 163 us -> 0 us
  Pallas kernels: 0 us -> 107 us
  starting transfers between devices: 56.8 us -> 16.7 us
  waiting for transfers between devices: 33.6 us -> 10.4 us
  blocking collectives: 18.6 us -> 0 us
    dynamic_update_slice x32 -> x0, local copies, waits for them, and re-layouts: 640 us -> none  [deposit_slot(): lax.dynamic_update_slice(grid_now, region + grid_step * push_boxes[slot_n...]
    another operation x3 -> x0, loops' own time: 364 us -> none  [the longest x1 182 us: local(): result = lax.fori_loop(0, slot_count, deposit_slot, stepped)]
    pallas_call x0 -> x4, Pallas kernels: none -> 107 us  [the longest x1 91.2 us: boxes(): pl.pallas_call(functools.partial(box_body, groups, first), grid=(1,), out...]
    add x34 -> x0, other arithmetic: 52.5 us -> none  [the longest x32 43.9 us: deposit_slot(): region + grid_step * push_boxes[slot_no]]
    dynamic_slice x96 -> x0, local copies, waits for them, and re-layouts: 47.1 us -> none  [the longest x32 21.6 us: deposit_slot(): corners[slot_no, 2]]
    scatter x32 -> x0, other arithmetic: 44 us -> none  [cut_slot(): boxes_now.at[slot_no].set(region.reshape(3, box_edge, box_edge * box_edge))]
    all_to_all x4 -> x0, starting transfers between devices: 33.5 us -> none  [the longest x1 10.4 us: local(): lax.all_to_all(replies[0], ('gy', 'gz'), split_axis=0, concat_axis=0, til...]
    another operation x35 -> x0, other arithmetic: 29 us -> none
  transfers between devices with their start and end apart: 16 -> 12, of which waited for: 7 -> 3; matrix products, arithmetic and copies ran while one was open for 16% -> 0% of each run, Pallas kernels for 0% -> 67%
where the time goes in v1:
time: 139 us; the launch traced here: 137 us
  Pallas kernels  107 us (77%)
  starting transfers between devices  16.7 us (12%)
  waiting for transfers between devices  10.4 us (7%)
  local copies, waits for them, and re-layouts  2.64 us (2%)
    pallas_call x1, Pallas kernels, boxes(): pl.pallas_call(functools.partial(box_body, groups, first), grid=(1,), out...  91.2 us
    ppermute x6, waiting for transfers between devices, exchange(): halos.append(lax.ppermute(faces[2 * d + 1], axis, up))  9.06 us
    ppermute x6, starting transfers between devices, exchange(): halos.append(lax.ppermute(faces[2 * d + 1], axis, up))  8.46 us
    ppermute x6, starting transfers between devices, exchange(): halos.append(lax.ppermute(faces[2 * d], axis, down))  8.25 us
    pallas_call x1, Pallas kernels, predictor_of(): pl.pallas_call(predictor_body, out_shape=(jax.ShapeDtypeStruct(rows.shape...  7.03 us
    pallas_call x1, Pallas kernels, final_of(): pl.pallas_call(final_body, out_shape=jax.ShapeDtypeStruct(rows.shape, F32...  5.65 us
  transfers between devices with their start and end apart: 12, of which 3 were waited for; matrix products, arithmetic and copies ran while one was open for 0% of the time, Pallas kernels for 67%

profile of v1, /device:TPU:1, one launch (start us, length us, event | category | flops | bytes accessed | tf_op | source)
XLA Modules:
  0.0 137.0 jit_solution(8707202389677872122)
XLA Ops:
  0.6 1.4 %copy-done = f32[3,32,32,128]{3,2,1,0:T(8,128)S(1)} copy-done((f32[3,32,32,128]{3,2,1,0:T(8,128)S(1)}, f32[3,32,32,128]{3,2,1,0:T(8,128)}, u32[]{:S(2)}) %copy-start) | copy-done | bytes 1572888
  2.1 2.6 %faces.1 = (f32[3,32,128]{2,1,0:T(8,128)S(1)}, f32[3,32,128]{2,1,0:T(8,128)S(1)}, f32[3,32,128]{2,1,0:T(8,128)S(1)}, f32[3,32,128]{2,1,0:T(8,128)S(1)}, f32[3,8,...) custom-call(f32[3072,128]{1,0:T(8,128)S(1)} %bitcast.6), custom_call_target="tpu_custom_call" | custom-call | tf_op jit(solution)/shard_map/faces/pallas_call | solution.py:411
  4.7 2.7 %collective-permute-start = (f32[3,32,128]{2,1,0:T(8,128)S(1)}, f32[3,32,128]{2,1,0:T(8,128)S(1)}, u32[]{:S(2)}, u32[]{:S(2)}) collective-permute-start(f32[3,32,128]{2,1,0:T(8,128)S(1)} %get-tuple-element.19), channel_id=1, source_target_pairs={{0,32},{32,64},{64,96},{96,128},{128,160},{160,192},{192,224},{224... | collective-permute-start | bytes 147464 | tf_op jit(solution)/shard_map/ppermute | solution.py:427
  7.4 0.6 collective-permute-start.1
  8.0 0.6 collective-permute-start.2
  8.6 2.0 %collective-permute-start.3 = (f32[3,32,128]{2,1,0:T(8,128)S(1)}, f32[3,32,128]{2,1,0:T(8,128)S(1)}, u32[]{:S(2)}, u32[]{:S(2)}) collective-permute-start(f32[3,32,128]{2,1,0:T(8,128)S(1)} %get-tuple-element.22), channel_id=1, source_target_pairs={{8,0},{16,8},{24,16},{0,24},{9,1},{17,9},{25,17},{1,25},{10,2},{18... | collective-permute-start | bytes 147464 | tf_op jit(solution)/shard_map/ppermute | solution.py:428
  10.7 1.1 collective-permute-start.4
  11.7 5.0 %collective-permute-done.4.refs_4_ = f32[3,8,128]{2,1,0:T(8,128)S(1)} collective-permute-done((f32[3,8,128]{2,1,0:T(8,128)S(1)}, f32[3,8,128]{2,1,0:T(8,128)S(1)}, u32[]{:S(2)}, u32[]{:S(2)}) %collective-permute-start.4) | collective-permute-done | bytes 12320 | tf_op jit(solution)/shard_map/ppermute | solution.py:427
  16.7 1.5 %collective-permute-start.5 = (f32[3,8,128]{2,1,0:T(8,128)S(1)}, f32[3,8,128]{2,1,0:T(8,128)S(1)}, u32[]{:S(2)}, u32[]{:S(2)}) collective-permute-start(f32[3,8,128]{2,1,0:T(8,128)S(1)} %get-tuple-element.24), channel_id=1, source_target_pairs={{1,0},{2,1},{3,2},{4,3},{5,4},{6,5},{7,6},{0,7},{9,8},{10,9},{11,1... | collective-permute-start | bytes 36872 | tf_op jit(solution)/shard_map/ppermute | solution.py:428
  18.2 1.3 collective-permute-done.5.refs_5_
  19.5 0.0 collective-permute-done.refs_0_
  19.5 0.0 collective-permute-done.1.refs_1_
  19.5 0.0 collective-permute-done.2.refs_2_
  19.6 0.0 collective-permute-done.3.refs_3_
  19.6 7.0 %predictor.1 = (f32[3072,128]{1,0:T(8,128)S(1)}, f32[3,32,128]{2,1,0:T(8,128)S(1)}, f32[3,32,128]{2,1,0:T(8,128)S(1)}, f32[3,32,128]{2,1,0:T(8,128)S(1)}, f32[3,...) custom-call(f32[3072,128]{1,0:T(8,128)S(1)} %bitcast.7, ...), custom_call_target="tpu_custom_call" | custom-call | tf_op jit(solution)/shard_map/predictor/pallas_call | solution.py:497
  26.6 0.0 copy-start.3
  26.6 1.1 copy-done.3
  27.8 4.1 %collective-permute-start.6 = (f32[3,32,128]{2,1,0:T(8,128)S(1)}, f32[3,32,128]{2,1,0:T(8,128)S(1)}, u32[]{:S(2)}, u32[]{:S(2)}) collective-permute-start(f32[3,32,128]{2,1,0:T(8,128)S(1)} %get-tuple-element.27), channel_id=1, source_target_pairs={{0,32},{32,64},{64,96},{96,128},{128,160},{160,192},{192,224},{224... | collective-permute-start | bytes 147464 | tf_op jit(solution)/shard_map/ppermute | solution.py:427
  31.8 0.0 collective-permute-start.7
  31.8 0.0 collective-permute-start.8
  31.9 2.7 %collective-permute-start.9 = (f32[3,32,128]{2,1,0:T(8,128)S(1)}, f32[3,32,128]{2,1,0:T(8,128)S(1)}, u32[]{:S(2)}, u32[]{:S(2)}) collective-permute-start(f32[3,32,128]{2,1,0:T(8,128)S(1)} %get-tuple-element.30), channel_id=1, source_target_pairs={{8,0},{16,8},{24,16},{0,24},{9,1},{17,9},{25,17},{1,25},{10,2},{18... | collective-permute-start | bytes 147464 | tf_op jit(solution)/shard_map/ppermute | solution.py:428
  34.5 0.0 collective-permute-start.10
  34.5 4.0 %collective-permute-done.10.refs_4_ = f32[3,8,128]{2,1,0:T(8,128)S(1)} collective-permute-done((f32[3,8,128]{2,1,0:T(8,128)S(1)}, f32[3,8,128]{2,1,0:T(8,128)S(1)}, u32[]{:S(2)}, u32[]{:S(2)}) %collective-permute-start.10) | collective-permute-done | bytes 12320 | tf_op jit(solution)/shard_map/ppermute | solution.py:427
  38.6 1.5 %collective-permute-start.11 = (f32[3,8,128]{2,1,0:T(8,128)S(1)}, f32[3,8,128]{2,1,0:T(8,128)S(1)}, u32[]{:S(2)}, u32[]{:S(2)}) collective-permute-start(f32[3,8,128]{2,1,0:T(8,128)S(1)} %get-tuple-element.32), channel_id=1, source_target_pairs={{1,0},{2,1},{3,2},{4,3},{5,4},{6,5},{7,6},{0,7},{9,8},{10,9},{11,1... | collective-permute-start | bytes 36872 | tf_op jit(solution)/shard_map/ppermute | solution.py:428
  40.0 0.1 copy.7.corner_ref
  40.1 91.2 %boxes.1 = (f32[3,32,32,128]{3,2,1,0:T(8,128)S(1)}, f32[512,256]{1,0:T(8,128)}, f32[512,256]{1,0:T(8,128)}) custom-call(s32[32]{0:T(128)S(1)} %copy-done.5, s32[32,3]{1,0:T(8,128)S(1)} %copy.7.corner_ref, f32[3,32,32,128]{3,2,1,0:T(8,128)S(1)} %copy-done.1, f32[512,256]{1,0:T(8,128)S(1)} %bitcast.9, f32[512,256]{1,0:T(8,128)S(1)} %bitcast.10), custom_call_target="tpu_custom_call" | custom-call | flops 60000000 | bytes 5000000 | tf_op jit(solution)/shard_map/boxes/pallas_call | solution.py:339
  131.3 0.0 collective-permute-done.11.refs_5_
  131.3 0.0 collective-permute-done.6.refs_0_
  131.3 0.0 collective-permute-done.7.refs_1_
  131.3 0.0 collective-permute-done.8.refs_2_
  131.3 0.0 collective-permute-done.9.refs_3_
  131.4 5.6 %final.1 = f32[3072,128]{1,0:T(8,128)} custom-call(f32[3072,128]{1,0:T(8,128)S(1)} %bitcast.8, f32[3072,128]{1,0:T(8,128)S(1)} %copy-done.4, f32[3072,128]{1,0:T(8,128)S(1)} %bitcast.11, f32[3,32,128]{2,1,0:T(8,128)S(1)} %collective-permute-done.6.refs_0_, f32[3,32,128]{2,1,0:T(8,128)S(1)} %collective-permute-done.7.refs_1_, ...), custom_call_target="tpu_custom_call" | custom-call | tf_op jit(solution)/shard_map/final/pallas_call | solution.py:531
  (11 shorter events, 0.0 us)
Async XLA Ops:
  0.6 1.4 %copy-start = (f32[3,32,32,128]{3,2,1,0:T(8,128)S(1)}, f32[3,32,32,128]{3,2,1,0:T(8,128)}, u32[]{:S(2)}) copy-start(f32[3,32,32,128]{3,2,1,0:T(8,128)} %vel_ref.1) | copy-start | bytes 4718596
  2.0 17.5 %copy-start.1 = (f32[3,32,32,128]{3,2,1,0:T(8,128)S(1)}, f32[3,32,32,128]{3,2,1,0:T(8,128)}, u32[]{:S(2)}) copy-start(f32[3,32,32,128]{3,2,1,0:T(8,128)} %vel_ref.1) | copy-start | bytes 4718596
  2.0 38.0 %copy-start.6 = (s32[32,3]{0,1:T(4,128)S(1)}, s32[32,3]{0,1:T(4,128)}, u32[]{:S(2)}) copy-start(s32[32,3]{0,1:T(4,128)} %param.6) | copy-start | bytes 1156
  2.0 38.1 %copy-start.2 = (f32[32,16,256]{2,1,0:T(8,128)S(1)}, f32[32,16,256]{2,1,0:T(8,128)}, u32[]{:S(2)}) copy-start(f32[32,16,256]{2,1,0:T(8,128)} %param.5) | copy-start | bytes 1572868
  2.0 38.1 %copy-start.5 = (s32[32]{0:T(128)S(1)}, s32[32]{0:T(128)}, u32[]{:S(2)}) copy-start(s32[32]{0:T(128)} %owner_ref.1) | copy-start | bytes 388
  4.7 14.8 %collective-permute-start = (f32[3,32,128]{2,1,0:T(8,128)S(1)}, f32[3,32,128]{2,1,0:T(8,128)S(1)}, u32[]{:S(2)}, u32[]{:S(2)}) collective-permute-start(f32[3,32,128]{2,1,0:T(8,128)S(1)} %get-tuple-element.19), channel_id=1, source_target_pairs={{0,32},{32,64},{64,96},{96,128},{128,160},{160,192},{192,224},{224... | collective-permute-start | bytes 147464 | tf_op jit(solution)/shard_map/ppermute | solution.py:427
  7.4 12.2 %collective-permute-start.1 = (f32[3,32,128]{2,1,0:T(8,128)S(1)}, f32[3,32,128]{2,1,0:T(8,128)S(1)}, u32[]{:S(2)}, u32[]{:S(2)}) collective-permute-start(f32[3,32,128]{2,1,0:T(8,128)S(1)} %get-tuple-element.20), channel_id=1, source_target_pairs={{32,0},{64,32},{96,64},{128,96},{160,128},{192,160},{224,192},{0,2... | collective-permute-start | bytes 147464 | tf_op jit(solution)/shard_map/ppermute | solution.py:428
  8.0 11.6 %collective-permute-start.2 = (f32[3,32,128]{2,1,0:T(8,128)S(1)}, f32[3,32,128]{2,1,0:T(8,128)S(1)}, u32[]{:S(2)}, u32[]{:S(2)}) collective-permute-start(f32[3,32,128]{2,1,0:T(8,128)S(1)} %get-tuple-element.21), channel_id=1, source_target_pairs={{0,8},{8,16},{16,24},{24,0},{1,9},{9,17},{17,25},{25,1},{2,10},{10... | collective-permute-start | bytes 147464 | tf_op jit(solution)/shard_map/ppermute | solution.py:427
  8.6 10.9 %collective-permute-start.3 = (f32[3,32,128]{2,1,0:T(8,128)S(1)}, f32[3,32,128]{2,1,0:T(8,128)S(1)}, u32[]{:S(2)}, u32[]{:S(2)}) collective-permute-start(f32[3,32,128]{2,1,0:T(8,128)S(1)} %get-tuple-element.22), channel_id=1, source_target_pairs={{8,0},{16,8},{24,16},{0,24},{9,1},{17,9},{25,17},{1,25},{10,2},{18... | collective-permute-start | bytes 147464 | tf_op jit(solution)/shard_map/ppermute | solution.py:428
  10.7 6.1 %collective-permute-start.4 = (f32[3,8,128]{2,1,0:T(8,128)S(1)}, f32[3,8,128]{2,1,0:T(8,128)S(1)}, u32[]{:S(2)}, u32[]{:S(2)}) collective-permute-start(f32[3,8,128]{2,1,0:T(8,128)S(1)} %get-tuple-element.23), channel_id=1, source_target_pairs={{0,1},{1,2},{2,3},{3,4},{4,5},{5,6},{6,7},{7,0},{8,9},{9,10},{10,1... | collective-permute-start | bytes 36872 | tf_op jit(solution)/shard_map/ppermute | solution.py:427
  16.7 2.8 %collective-permute-start.5 = (f32[3,8,128]{2,1,0:T(8,128)S(1)}, f32[3,8,128]{2,1,0:T(8,128)S(1)}, u32[]{:S(2)}, u32[]{:S(2)}) collective-permute-start(f32[3,8,128]{2,1,0:T(8,128)S(1)} %get-tuple-element.24), channel_id=1, source_target_pairs={{1,0},{2,1},{3,2},{4,3},{5,4},{6,5},{7,6},{0,7},{9,8},{10,9},{11,1... | collective-permute-start | bytes 36872 | tf_op jit(solution)/shard_map/ppermute | solution.py:428
  26.6 1.1 copy-start.3
  27.8 103.6 %collective-permute-start.6 = (f32[3,32,128]{2,1,0:T(8,128)S(1)}, f32[3,32,128]{2,1,0:T(8,128)S(1)}, u32[]{:S(2)}, u32[]{:S(2)}) collective-permute-start(f32[3,32,128]{2,1,0:T(8,128)S(1)} %get-tuple-element.27), channel_id=1, source_target_pairs={{0,32},{32,64},{64,96},{96,128},{128,160},{160,192},{192,224},{224... | collective-permute-start | bytes 147464 | tf_op jit(solution)/shard_map/ppermute | solution.py:427
  31.8 99.5 %collective-permute-start.7 = (f32[3,32,128]{2,1,0:T(8,128)S(1)}, f32[3,32,128]{2,1,0:T(8,128)S(1)}, u32[]{:S(2)}, u32[]{:S(2)}) collective-permute-start(f32[3,32,128]{2,1,0:T(8,128)S(1)} %get-tuple-element.28), channel_id=1, source_target_pairs={{32,0},{64,32},{96,64},{128,96},{160,128},{192,160},{224,192},{0,2... | collective-permute-start | bytes 147464 | tf_op jit(solution)/shard_map/ppermute | solution.py:428
  31.8 99.5 %collective-permute-start.8 = (f32[3,32,128]{2,1,0:T(8,128)S(1)}, f32[3,32,128]{2,1,0:T(8,128)S(1)}, u32[]{:S(2)}, u32[]{:S(2)}) collective-permute-start(f32[3,32,128]{2,1,0:T(8,128)S(1)} %get-tuple-element.29), channel_id=1, source_target_pairs={{0,8},{8,16},{16,24},{24,0},{1,9},{9,17},{17,25},{25,1},{2,10},{10... | collective-permute-start | bytes 147464 | tf_op jit(solution)/shard_map/ppermute | solution.py:427
  31.9 99.5 %collective-permute-start.9 = (f32[3,32,128]{2,1,0:T(8,128)S(1)}, f32[3,32,128]{2,1,0:T(8,128)S(1)}, u32[]{:S(2)}, u32[]{:S(2)}) collective-permute-start(f32[3,32,128]{2,1,0:T(8,128)S(1)} %get-tuple-element.30), channel_id=1, source_target_pairs={{8,0},{16,8},{24,16},{0,24},{9,1},{17,9},{25,17},{1,25},{10,2},{18... | collective-permute-start | bytes 147464 | tf_op jit(solution)/shard_map/ppermute | solution.py:428
  34.5 4.0 %collective-permute-start.10 = (f32[3,8,128]{2,1,0:T(8,128)S(1)}, f32[3,8,128]{2,1,0:T(8,128)S(1)}, u32[]{:S(2)}, u32[]{:S(2)}) collective-permute-start(f32[3,8,128]{2,1,0:T(8,128)S(1)} %get-tuple-element.31), channel_id=1, source_target_pairs={{0,1},{1,2},{2,3},{3,4},{4,5},{5,6},{6,7},{7,0},{8,9},{9,10},{10,1... | collective-permute-start | bytes 36872 | tf_op jit(solution)/shard_map/ppermute | solution.py:427
  38.6 92.8 %collective-permute-start.11 = (f32[3,8,128]{2,1,0:T(8,128)S(1)}, f32[3,8,128]{2,1,0:T(8,128)S(1)}, u32[]{:S(2)}, u32[]{:S(2)}) collective-permute-start(f32[3,8,128]{2,1,0:T(8,128)S(1)} %get-tuple-element.32), channel_id=1, source_target_pairs={{1,0},{2,1},{3,2},{4,3},{5,4},{6,5},{7,6},{0,7},{9,8},{10,9},{11,1... | collective-permute-start | bytes 36872 | tf_op jit(solution)/shard_map/ppermute | solution.py:428
  40.1 91.2 %copy-start.4 = (f32[3072,128]{1,0:T(8,128)S(1)}, f32[3072,128]{1,0:T(8,128)}, u32[]{:S(2)}) copy-start(f32[3072,128]{1,0:T(8,128)} %copy-done.3) | copy-start | bytes 4718596

commit v2 on v1

--- a/solution.py
+++ b/solution.py
@@ -12,6 +12,8 @@
 BOX = 16
 LANES = 128
 PER = 8
+
+CUT, LEVEL, MI, MJ, WENO, CENTRAL, KAPPA, DEPOSIT, PLANES = 6, 8, 5, 4, 8, 8, 8, 6, 4
 
 box_step = 0.25
 pseudo_step = 0.3
@@ -34,17 +36,9 @@
 
 def block_transpose(x, row, lane):
     block = lane // BOX
-    for s in (4, 2, 1):
-        r_bit = (row // s) % 2
-        q_bit = (block // s) % 2
-        down = pltpu.roll(pltpu.roll(x, s, 0), LANES - BOX * s, 1)
-        if s == 4:
-            moved = down
-        else:
-            up = pltpu.roll(pltpu.roll(x, 8 - s, 0), BOX * s, 1)
-            moved = jnp.where(r_bit == 1, down, up)
-        x = jnp.where(r_bit == q_bit, x, moved)
-    return x
+    x = jnp.take_along_axis(x, (lane - BOX * row) % LANES, axis=1)
+    x = jnp.take_along_axis(x, (block - row) % 8, axis=0)
+    return jnp.take_along_axis(x, (lane + BOX * row) % LANES, axis=1)
 
 
 def weno(a, b, c, e, f):
@@ -79,75 +73,60 @@
 ROWS = 32
 
 
-def box_body(
-    groups,
-    first,
-    owner_ref,
-    corner_ref,
-    vel_ref,
-    level_lo,
-    level_hi,
-    *rest,
-):
-    if first:
-        (force_out, settled_out, bending_out, *scratch) = rest
-    else:
-        (_, force_in, _, _, force_out, settled_out, bending_out, *scratch) = rest
-    (u_ref, l_ref, mi_ref, mj_ref, pa, pb, c_ref, s_ref, k_ref, turned_s, turned_b) = scratch
+def box_body(first_group, count, owner_ref, corner_ref, vel_ref, level_lo, level_hi, *rest):
+    (force_out, settled_out, bending_out, *scratch) = rest[-15:]
+    (u_ref, l_ref, mi_ref, mj_ref, pa, pb, c_ref, s_ref, k_ref) = scratch[:9]
+    turned, turned_kappa, sems = scratch[9], scratch[10], scratch[11]
     row, lane = iotas()
     k = lane % BOX
     block = lane // BOX
     k_first, k_last = k == 0, k == BOX - 1
     top, bottom = row == 0, row == 7
 
-    if first:
-
-        @pl.loop(0, 32)
-        def _(x):
-            for c in range(3):
-                force_out[c, x] = jnp.zeros((32, LANES), F32)
-    else:
-
-        @pl.loop(0, 32)
-        def _(x):
-            for c in range(3):
-                force_out[c, x] = force_in[c, x]
-
     def next_k(v):
         return jnp.where(k_last, v, pltpu.roll(v, LANES - 1, 1))
 
     def prev_k(v):
         return jnp.where(k_first, v, pltpu.roll(v, 1, 1))
 
-    def one_group(g):
-        spots = [
-            [corner_ref[g * PER + b, d] for d in range(3)] for b in range(PER)
-        ]
+    def one_group(own):
+        g = first_group + own
+        spots = [[corner_ref[g * PER + b, d] for d in range(3)] for b in range(PER)]
         alive = jnp.zeros(TILE, F32)
         for b in range(PER):
             living = jnp.where(owner_ref[g * PER + b] >= 0, 1.0, 0.0)
             alive = jnp.where(block == b, living, alive)
 
-        @pl.loop(0, BOX)
+        for b in range(PER):
+            px, py, pz = spots[b]
+            turn = (BOX * b + LANES - pz) % LANES
+            here = block == b
+
+            @pl.loop(0, 6, unroll=CUT)
+            def _(step):
+                c = step // 2
+                i0 = (step % 2) * 8
+                for i in range(8):
+                    for jt in range(2):
+                        part = vel_ref[c, px + i0 + i, pl.ds(py + 8 * jt, 8), :]
+                        pltpu.store(
+                            u_ref.at[c, i0 + i, pl.ds(8 * jt, 8), :],
+                            pltpu.roll(part, turn, 1),
+                            mask=here,
+                        )
+
+        @pl.loop(0, BOX, unroll=LEVEL)
         def _(i):
             for jt in range(2):
-                for c in range(3):
-                    total = jnp.zeros(TILE, F32)
-                    for b in range(PER):
-                        px, py, pz = spots[b]
-                        part = vel_ref[c, px + i, pl.ds(py + 8 * jt, 8), :]
-                        part = pltpu.roll(part, (BOX * b + LANES - pz) % LANES, 1)
-                        total = part if b == 0 else jnp.where(block == b, part, total)
-                    u_ref[c, i, pl.ds(8 * jt, 8), :] = total
                 level = (level_lo, level_hi)[jt]
-                x = level[pl.ds(g * (PER * BOX) + i, 8, stride=BOX), :]
+                x = level[pl.ds(own * (PER * BOX) + i, 8, stride=BOX), :]
                 l_ref[i, pl.ds(8 + 8 * jt, 8), :] = block_transpose(x, row, lane)
 
         mi_ref[0] = jnp.zeros((BOX, LANES), F32)
         mi_ref[1] = jnp.zeros((BOX, LANES), F32)
         mi_ref[2] = jnp.zeros((BOX, LANES), F32)
 
-        @pl.loop(1, BOX)
+        @pl.loop(1, BOX, unroll=MI)
         def _(i):
             for jt in range(2):
                 at = pl.ds(8 + 8 * jt, 8)
@@ -156,7 +135,7 @@
         for t in range(3):
             mi_ref[18 + t] = mi_ref[17]
 
-        @pl.loop(0, BOX)
+        @pl.loop(0, BOX, unroll=MJ)
         def _(i):
             for jt in range(2):
                 here = l_ref[i, pl.ds(8 + 8 * jt, 8), :]
@@ -168,7 +147,7 @@
                     mj_ref[i, pl.ds(24, 8), :] = jnp.broadcast_to(m[7:8, :], TILE)
                 mj_ref[i, pl.ds(8 + 8 * jt, 8), :] = m
 
-        @pl.loop(0, BOX)
+        @pl.loop(0, BOX, unroll=WENO)
         def _(i):
             for jt in range(2):
                 at = pl.ds(8 * jt, 8)
@@ -252,7 +231,7 @@
             c2 = 0.5 * (next_k(cur) - prev_k(cur))
             return cur, c0, c1, c2
 
-        @pl.loop(0, BOX)
+        @pl.loop(0, BOX, unroll=CENTRAL)
         def _(i):
             for jt in range(2):
                 cur, c0, c1, c2 = central(i, jt)
@@ -268,13 +247,12 @@
                     grid_step * tension / (band_width * math.sqrt(math.pi))
                 )
                 band = band * alive
-                u_ref[0, i, at, :] = band * c0
-                u_ref[1, i, at, :] = band * c1
-                u_ref[2, i, at, :] = band * c2
+                for c, slope in enumerate((c0, c1, c2)):
+                    force_out[own, c, i, at, :] = band * slope
                 y = block_transpose(cur * alive, row, lane)
-                turned_s[pl.ds(jt * (PER * BOX) + i, 8, stride=BOX), :] = y
-
-        @pl.loop(0, BOX)
+                turned[pl.ds((own * 2 + jt) * (PER * BOX) + i, 8, stride=BOX), :] = y
+
+        @pl.loop(0, BOX, unroll=KAPPA)
         def _(i):
             for jt in range(2):
                 at = pl.ds(8 * jt, 8)
@@ -288,64 +266,62 @@
                     upper = jnp.where(bottom, mj_ref[i, padded_at, :], upper)
                 kappa = 0.5 * (d1 + (upper - lower) + k_ref[i, at, :])
                 for c in range(3):
-                    u_ref[c, i, at, :] = u_ref[c, i, at, :] * kappa
+                    force_out[own, c, i, at, :] = force_out[own, c, i, at, :] * kappa
                 y = block_transpose(kappa * alive, row, lane)
-                turned_b[pl.ds(jt * (PER * BOX) + i, 8, stride=BOX), :] = y
-
-        for jt in range(2):
-            here = pl.ds(jt * (PER * BOX), PER * BOX)
-            there = pl.ds(pl.multiple_of(g * (PER * BOX), PER * BOX), PER * BOX)
-            settled_out[there, pl.ds(LANES * jt, LANES)] = turned_s[here, :]
-            bending_out[there, pl.ds(LANES * jt, LANES)] = turned_b[here, :]
-
-        for b in range(PER):
-            px, py, pz = spots[b]
-            inside = (lane >= pz) & (lane < pz + BOX)
-            turn = (pz + LANES - BOX * b) % LANES
-
-            @pl.loop(0, 3 * BOX // 8)
-            def _(step):
-                c = step // 2
-                i0 = (step % 2) * 8
-                sums = []
-                for i in range(8):
-                    for jt in range(2):
-                        old = force_out[c, px + i0 + i, pl.ds(py + 8 * jt, 8), :]
-                        push = pltpu.roll(u_ref[c, i0 + i, pl.ds(8 * jt, 8), :], turn, 1)
-                        sums.append(old + jnp.where(inside, push, 0.0))
-                for i in range(8):
-                    for jt in range(2):
-                        force_out[c, px + i0 + i, pl.ds(py + 8 * jt, 8), :] = sums[2 * i + jt]
-
-    @pl.loop(groups[0], groups[1])
-    def _(g):
-        one_group(g)
-
-
-def boxes(groups, owner, corners, velocity, level_rows, carried=None):
-    first = carried is None
+                turned_kappa[pl.ds((own * 2 + jt) * (PER * BOX) + i, 8, stride=BOX), :] = y
+
+        for copy in sent(own):
+            copy.start()
+
+    def sent(own):
+        copies = []
+        for n, (src, dst) in enumerate(((turned, settled_out), (turned_kappa, bending_out))):
+            for jt in range(2):
+                rows = (first_group + own) * (PER * BOX)
+                copies.append(
+                    pltpu.make_async_copy(
+                        src.at[pl.ds((own * 2 + jt) * (PER * BOX), PER * BOX), :],
+                        dst.at[pl.ds(rows, PER * BOX), pl.ds(LANES * jt, LANES)],
+                        sems.at[own, 2 * n + jt],
+                    )
+                )
+        return copies
+
+    @pl.loop(0, count)
+    def _(own):
+        one_group(own)
+
+    for own in range(count):
+        for copy in sent(own):
+            copy.wait()
+
+
+def boxes(first_group, count, owner, corners, velocity, level_rows, after, carried=()):
     smem = pl.BlockSpec(memory_space=pltpu.SMEM)
+    any_ = pl.BlockSpec(memory_space=pl.ANY)
     vmem = pl.BlockSpec(memory_space=pltpu.VMEM)
     halves = [
-        pl.BlockSpec((level_rows.shape[0], LANES), functools.partial(lambda h, s: (0, h), h))
+        pl.BlockSpec(
+            (count * PER * BOX, LANES),
+            functools.partial(lambda h, s: (first_group // count, h), h),
+        )
         for h in range(2)
     ]
     whole = pl.BlockSpec(velocity.shape, lambda s: (0, 0, 0, 0))
-    rows = pl.BlockSpec(level_rows.shape, lambda s: (0, 0))
-    any_ = pl.BlockSpec(memory_space=pl.ANY)
-    specs = [smem, smem, whole, *halves]
-    operands = [owner, corners, velocity, level_rows, level_rows]
     plane = lambda *lead: pltpu.VMEM((*lead, LANES), F32)
+    force = (count, 3, BOX, BOX, LANES)
+    operands = [owner, corners, velocity, level_rows, level_rows, after, *carried]
     return pl.pallas_call(
-        functools.partial(box_body, groups, first),
+        functools.partial(box_body, first_group, count),
         grid=(1,),
         out_shape=(
-            jax.ShapeDtypeStruct(velocity.shape, F32),
+            jax.ShapeDtypeStruct(force, F32),
             jax.ShapeDtypeStruct(level_rows.shape, F32),
             jax.ShapeDtypeStruct(level_rows.shape, F32),
         ),
-        in_specs=specs,
-        out_specs=(whole, rows, rows),
+        in_specs=[smem, smem, whole, *halves, any_] + [any_] * len(carried),
+        out_specs=(pl.BlockSpec(force, lambda s: (0,) * 5), any_, any_),
+        input_output_aliases={6: 1, 7: 2} if carried else {},
         scratch_shapes=[
             plane(3, BOX, BOX),
             plane(BOX, ROWS),
@@ -356,21 +332,68 @@
             plane(BOX, BOX),
             plane(BOX, BOX),
             plane(BOX, BOX),
-            plane(2 * PER * BOX),
-            plane(2 * PER * BOX),
+            plane(count * 2 * PER * BOX),
+            plane(count * 2 * PER * BOX),
+            pltpu.SemaphoreType.DMA((count, 4)),
         ],
-        compiler_params=pltpu.CompilerParams(vmem_limit_bytes=32 * 2**20),
-        cost_estimate=pl.CostEstimate(flops=60_000_000, bytes_accessed=5_000_000, transcendentals=0),
+        compiler_params=pltpu.CompilerParams(vmem_limit_bytes=20 * 2**20),
+        cost_estimate=pl.CostEstimate(
+            flops=30_000_000, bytes_accessed=5_000_000, transcendentals=0
+        ),
         name="boxes",
     )(*operands)
 
 
+def deposit(force_refs, corner_ref, grid_ref):
+    _, lane = iotas()
+
+    def one_group(ref, own, g):
+        for b in range(PER):
+            px, py, pz = [corner_ref[g * PER + b, d] for d in range(3)]
+            inside = (lane >= pz) & (lane < pz + BOX)
+            turn = (pz + LANES - BOX * b) % LANES
+            base = px * 32 + py
+
+            @pl.loop(0, 6, unroll=DEPOSIT)
+            def _(step):
+                c = step // 2
+                i0 = (step % 2) * 8
+                sums = []
+                for i in range(8):
+                    for jt in range(2):
+                        old = grid_ref[pl.ds(base + c * 1024 + (i0 + i) * 32 + 8 * jt, 8), :]
+                        push = pltpu.roll(ref[own, c, i0 + i, pl.ds(8 * jt, 8), :], turn, 1)
+                        sums.append(old + jnp.where(inside, push, 0.0))
+                for i in range(8):
+                    for jt in range(2):
+                        grid_ref[pl.ds(base + c * 1024 + (i0 + i) * 32 + 8 * jt, 8), :] = sums[
+                            2 * i + jt
+                        ]
+
+    done = 0
+    for ref in force_refs:
+        count = ref.shape[0]
+
+        @pl.loop(0, count)
+        def _(own):
+            one_group(ref, own, done + own)
+
+        done += count
+
+
 PLANE = 48
 
 
-def take_faces(load, faces):
-    xlo, xhi, ylo, yhi, zlo, zhi = faces
-    row, lane = iotas()
+def side_faces(rows_ref, xlo, xhi, ylo, yhi):
+    for c in range(3):
+        xlo[c] = rows_ref[pl.ds(c * 1024, 32), :]
+        xhi[c] = rows_ref[pl.ds(c * 1024 + 31 * 32, 32), :]
+        ylo[c] = rows_ref[pl.ds(c * 1024, 32, stride=32), :]
+        yhi[c] = rows_ref[pl.ds(c * 1024 + 31, 32, stride=32), :]
+
+
+def end_faces_body(rows_ref, zlo, zhi):
+    _, lane = iotas()
 
     def one(x, packed):
         out = []
@@ -378,49 +401,39 @@
             lo, hi = packed[2 * c], packed[2 * c + 1]
             for yt in range(4):
                 n = x * 4 + yt
-                turned = pltpu.roll(load(c, x, yt), n, 1)
+                at = pl.multiple_of(c * 1024 + x * 32 + 8 * yt, 8)
+                turned = pltpu.roll(rows_ref[pl.ds(at, 8), :], n, 1)
                 lo = jnp.where(lane == n, turned, lo)
                 hi = jnp.where(lane == (n + LANES - 1) % LANES, turned, hi)
             out += [lo, hi]
         return tuple(out)
 
-    packed = lax.fori_loop(0, 32, one, (jnp.zeros(TILE, F32),) * 6)
+    packed = lax.fori_loop(0, 32, one, (jnp.zeros(TILE, F32),) * 6, unroll=PLANES)
     for c in range(3):
         zlo[c] = packed[2 * c]
         zhi[c] = packed[2 * c + 1]
 
 
-def faces_body(vel_ref, *faces):
-    xlo, xhi, ylo, yhi, _, _ = faces
-    for c in range(3):
-        xlo[c] = vel_ref[pl.ds(c * 1024, 32), :]
-        xhi[c] = vel_ref[pl.ds(c * 1024 + 31 * 32, 32), :]
-        ylo[c] = vel_ref[pl.ds(c * 1024, 32, stride=32), :]
-        yhi[c] = vel_ref[pl.ds(c * 1024 + 31, 32, stride=32), :]
-    take_faces(
-        lambda c, x, yt: vel_ref[pl.ds(pl.multiple_of(c * 1024 + x * 32 + 8 * yt, 8), 8), :],
-        faces,
-    )
-
-
-FACES = tuple([(3, 32, LANES)] * 4 + [(3, 8, LANES)] * 2)
-
-
-def faces_of(rows):
+SIDES = jax.ShapeDtypeStruct((3, 32, LANES), F32)
+ENDS = jax.ShapeDtypeStruct((3, 8, LANES), F32)
+
+
+def in_vmem(body, out_shape, operands, scratch=(), limit=16, name=None, smem=0):
     vmem = pl.BlockSpec(memory_space=pltpu.VMEM)
     return pl.pallas_call(
-        faces_body,
-        out_shape=tuple(jax.ShapeDtypeStruct(s, F32) for s in FACES),
-        in_specs=[vmem],
-        out_specs=(vmem,) * 6,
-        compiler_params=pltpu.CompilerParams(vmem_limit_bytes=16 * 2**20),
-        name="faces",
-    )(rows)
-
-
-def exchange(faces):
+        body,
+        out_shape=out_shape,
+        in_specs=[vmem] * (len(operands) - smem) + [pl.BlockSpec(memory_space=pltpu.SMEM)] * smem,
+        out_specs=jax.tree.map(lambda _: vmem, out_shape),
+        scratch_shapes=scratch,
+        compiler_params=pltpu.CompilerParams(vmem_limit_bytes=limit * 2**20),
+        name=name,
+    )(*operands)
+
+
+def exchange(faces, axes):
     halos = []
-    for d, axis in enumerate(("gx", "gy", "gz")):
+    for d, axis in enumerate(axes):
         size = lax.axis_size(axis)
         up = [(i, (i + 1) % size) for i in range(size)]
         down = [(j, i) for i, j in up]
@@ -472,49 +485,15 @@
     return centre, out
 
 
-def predictor_body(vel_ref, *refs):
-    halos, out_ref, faces, ext = refs[:6], refs[6], refs[7:13], refs[13]
-    fill_padded(vel_ref, halos, ext)
-    row, lane = iotas()
+PADDED = [pltpu.VMEM((3 * 34 * PLANE, LANES), F32)]
+
+
+def stage(src_ref, halos, ext, write):
+    fill_padded(src_ref, halos, ext)
+    _, lane = iotas()
     zlo, zhi = halos[4], halos[5]
 
-    @pl.loop(0, 32)
-    def _(x):
-        zl = [zlo[c] for c in range(3)]
-        zh = [zhi[c] for c in range(3)]
-        for yt in range(4):
-            centre, f = tendencies(ext, zl, zh, x, yt, lane)
-            for c in range(3):
-                out_ref[pl.ds(pl.multiple_of(c * 1024 + x * 32 + 8 * yt, 8), 8), :] = (
-                    centre[c] + grid_step * f[c]
-                )
-
-    faces_body(out_ref, *faces)
-
-
-def predictor_of(rows, halos):
-    vmem = pl.BlockSpec(memory_space=pltpu.VMEM)
-    return pl.pallas_call(
-        predictor_body,
-        out_shape=(
-            jax.ShapeDtypeStruct(rows.shape, F32),
-            *(jax.ShapeDtypeStruct(s, F32) for s in FACES),
-        ),
-        in_specs=[vmem] * 7,
-        out_specs=(vmem,) * 7,
-        scratch_shapes=[pltpu.VMEM((3 * 34 * PLANE, LANES), F32)],
-        compiler_params=pltpu.CompilerParams(vmem_limit_bytes=24 * 2**20),
-        name="predictor",
-    )(rows, *halos)
-
-
-def final_body(vel_ref, pred_ref, force_ref, *refs):
-    halos, out_ref, ext = refs[:6], refs[6], refs[7]
-    fill_padded(pred_ref, halos, ext)
-    row, lane = iotas()
-    zlo, zhi = halos[4], halos[5]
-
-    @pl.loop(0, 32)
+    @pl.loop(0, 32, unroll=PLANES)
     def _(x):
         zl = [zlo[c] for c in range(3)]
         zh = [zhi[c] for c in range(3)]
@@ -522,32 +501,64 @@
             centre, f = tendencies(ext, zl, zh, x, yt, lane)
             for c in range(3):
                 at = pl.ds(pl.multiple_of(c * 1024 + x * 32 + 8 * yt, 8), 8)
-                second = centre[c] + grid_step * f[c]
-                out_ref[at, :] = 0.5 * (vel_ref[at, :] + second) + force_ref[at, :]
-
-
-def final_of(rows, predictor, force, halos):
-    vmem = pl.BlockSpec(memory_space=pltpu.VMEM)
-    return pl.pallas_call(
-        final_body,
-        out_shape=jax.ShapeDtypeStruct(rows.shape, F32),
-        in_specs=[vmem] * 9,
-        out_specs=vmem,
-        scratch_shapes=[pltpu.VMEM((3 * 34 * PLANE, LANES), F32)],
-        compiler_params=pltpu.CompilerParams(vmem_limit_bytes=24 * 2**20),
-        name="final",
-    )(rows, predictor, force, *halos)
+                write(at, centre[c] + grid_step * f[c])
+
+
+def predictor_body(vel_ref, *refs):
+    halos, out_ref, sides, ext = refs[:6], refs[-6], refs[-5:-1], refs[-1]
+
+    def write(at, value):
+        out_ref[at, :] = value
+
+    stage(vel_ref, halos, ext, write)
+    side_faces(out_ref, *sides)
+
+
+def final_body(vel_ref, pred_ref, *refs):
+    halos, forces, corner_ref, out_ref, ext = refs[:6], refs[6:-3], refs[-3], refs[-2], refs[-1]
+
+    def write(at, value):
+        out_ref[at, :] = 0.5 * (vel_ref[at, :] + value)
+
+    stage(pred_ref, halos, ext, write)
+    deposit(forces, corner_ref, out_ref)
 
 
 def local(velocity, box_level, corners, owner_list):
     slots = box_level.shape[0]
     rows = velocity.reshape(-1, LANES)
     level_rows = box_level.reshape(slots * BOX, BOX * BOX)
-    halos = exchange(faces_of(rows))
-    force, settled, bending = boxes((0, slots // PER), owner_list, corners, velocity, level_rows)
-    predictor, *faces = predictor_of(rows, halos)
-    halos = exchange(faces)
-    result = final_of(rows, predictor, force.reshape(rows.shape), halos)
+    half = slots // PER // 2
+    sides = in_vmem(side_faces, (SIDES,) * 4, [rows], name="side_faces")
+    halos = exchange(sides, ("gx", "gy"))
+    ends = in_vmem(end_faces_body, (ENDS,) * 2, [rows], name="end_faces")
+    halos += exchange(ends, ("gz",))
+    force_a, settled, bending = boxes(
+        0, half, owner_list, corners, velocity, level_rows, ends[0]
+    )
+    predictor, *sides = in_vmem(
+        predictor_body,
+        (jax.ShapeDtypeStruct(rows.shape, F32), *(SIDES,) * 4),
+        [rows, *halos, force_a[0, 0, 0]],
+        PADDED,
+        24,
+        "predictor",
+    )
+    halos = exchange(sides, ("gx", "gy"))
+    ends = in_vmem(end_faces_body, (ENDS,) * 2, [predictor], name="end_faces")
+    halos += exchange(ends, ("gz",))
+    force_b, settled, bending = boxes(
+        half, half, owner_list, corners, velocity, level_rows, ends[0], (settled, bending)
+    )
+    result = in_vmem(
+        final_body,
+        jax.ShapeDtypeStruct(rows.shape, F32),
+        [rows, predictor, *halos, force_a, force_b, corners],
+        PADDED,
+        32,
+        "final",
+        smem=1,
+    )
     return (
         result.reshape(velocity.shape),
         settled.reshape(box_level.shape),

time: 139 us -> 66.5 us (0.48)
  the two profiles are of different devices: /device:TPU:1 before, /device:TPU:32 now
where the time goes in v2:
time: 66.5 us; the launch traced here: 66.4 us
  Pallas kernels  38.2 us (57%)
  starting transfers between devices  19.8 us (30%)
  waiting for transfers between devices  6.12 us (9%)
  local copies, waits for them, and re-layouts  1.5 us (2%)
  between operations  0.76 us (1%)
    pallas_call x2, Pallas kernels, boxes(): pl.pallas_call(functools.partial(box_body, first_group, count), grid=(1,)...  25.6 us
    ppermute x6, starting transfers between devices, exchange(): halos.append(lax.ppermute(faces[2 * d], axis, down))  12.8 us
    pallas_call x5, Pallas kernels, in_vmem(): pl.pallas_call(body, out_shape=out_shape, in_specs=[vmem] * (len(operands...  12.6 us
    ppermute x6, starting transfers between devices, exchange(): halos.append(lax.ppermute(faces[2 * d + 1], axis, up))  7 us
    ppermute x6, waiting for transfers between devices, exchange(): halos.append(lax.ppermute(faces[2 * d + 1], axis, up))  3.8 us
    ppermute x6, waiting for transfers between devices, exchange(): halos.append(lax.ppermute(faces[2 * d], axis, down))  2.33 us
    unnamed x11, local copies, waits for them, and re-layouts  1.5 us
  transfers between devices with their start and end apart: 12, of which 2 were waited for; matrix products, arithmetic and copies ran while one was open for 0% of the time, Pallas kernels for 40%

profile of v2, /device:TPU:32, one launch (start us, length us, event | category | flops | bytes accessed | tf_op | source)
XLA Modules:
  0.0 66.4 jit_solution(7920436103105731656)
XLA Ops:
  0.6 1.4 %copy-done = f32[3,32,32,128]{3,2,1,0:T(8,128)S(1)} copy-done((f32[3,32,32,128]{3,2,1,0:T(8,128)S(1)}, f32[3,32,32,128]{3,2,1,0:T(8,128)}, u32[]{:S(2)}) %copy-start) | copy-done | bytes 1572888
  2.1 0.9 %end_faces.2 = (f32[3,8,128]{2,1,0:T(8,128)S(1)}, f32[3,8,128]{2,1,0:T(8,128)S(1)}) custom-call(f32[3072,128]{1,0:T(8,128)S(1)} %bitcast.7), custom_call_target="tpu_custom_call" | custom-call | tf_op jit(solution)/shard_map/end_faces/pallas_call | solution.py:423
  3.0 2.0 %collective-permute-start.4 = (f32[3,8,128]{2,1,0:T(8,128)S(1)}, f32[3,8,128]{2,1,0:T(8,128)S(1)}, u32[]{:S(2)}, u32[]{:S(2)}) collective-permute-start(f32[3,8,128]{2,1,0:T(8,128)S(1)} %get-tuple-element.26), channel_id=1, source_target_pairs={{0,1},{1,2},{2,3},{3,4},{4,5},{5,6},{6,7},{7,0},{8,9},{9,10},{10,1... | collective-permute-start | bytes 36872 | tf_op jit(solution)/shard_map/ppermute | solution.py:440
  5.0 0.1 collective-permute-start.5
  5.1 0.1 side_faces.1
  5.2 0.0 collective-permute-start
  5.2 2.9 %collective-permute-start.1 = (f32[3,32,128]{2,1,0:T(8,128)S(1)}, f32[3,32,128]{2,1,0:T(8,128)S(1)}, u32[]{:S(2)}, u32[]{:S(2)}) collective-permute-start(f32[3,32,128]{2,1,0:T(8,128)S(1)} %get-tuple-element.23), channel_id=1, source_target_pairs={{32,0},{64,32},{96,64},{128,96},{160,128},{192,160},{224,192},{0,2... | collective-permute-start | bytes 147464 | tf_op jit(solution)/shard_map/ppermute | solution.py:441
  8.1 1.5 %collective-permute-start.2 = (f32[3,32,128]{2,1,0:T(8,128)S(1)}, f32[3,32,128]{2,1,0:T(8,128)S(1)}, u32[]{:S(2)}, u32[]{:S(2)}) collective-permute-start(f32[3,32,128]{2,1,0:T(8,128)S(1)} %get-tuple-element.24), channel_id=1, source_target_pairs={{0,8},{8,16},{16,24},{24,0},{1,9},{9,17},{17,25},{25,1},{2,10},{10... | collective-permute-start | bytes 147464 | tf_op jit(solution)/shard_map/ppermute | solution.py:440
  9.6 0.1 copy.9.corner_ref.refs_8_
  9.7 12.8 %boxes.2 = (f32[2,3,16,16,128]{4,3,2,1,0:T(8,128)S(1)}, f32[512,256]{1,0:T(8,128)}, f32[512,256]{1,0:T(8,128)}) custom-call(s32[32]{0:T(128)S(1)} %copy-done.3, s32[32,3]{1,0:T(8,128)S(1)} %copy.9.corner_ref.refs_8_, f32[3,32,32,128]{3,2,1,0:T(8,128)S(1)} %copy-done.1, f32[512,256]{1,0:T(8,128)S(1)} %bitcast.11, f32[512,256]{1,0:T(8,128)S(1)} %bitcast.12, ...), custom_call_target="tpu_custom_call" | custom-call | flops 30000000 | bytes 5000000 | tf_op jit(solution)/shard_map/boxes/pallas_call | solution.py:314
  22.5 0.0 collective-permute-done.4.refs_4_
  22.6 1.8 %collective-permute-start.3 = (f32[3,32,128]{2,1,0:T(8,128)S(1)}, f32[3,32,128]{2,1,0:T(8,128)S(1)}, u32[]{:S(2)}, u32[]{:S(2)}) collective-permute-start(f32[3,32,128]{2,1,0:T(8,128)S(1)} %get-tuple-element.25), channel_id=1, source_target_pairs={{8,0},{16,8},{24,16},{0,24},{9,1},{17,9},{25,17},{1,25},{10,2},{18... | collective-permute-start | bytes 147464 | tf_op jit(solution)/shard_map/ppermute | solution.py:441
  24.4 0.0 collective-permute-done.5.refs_5_
  24.4 0.0 collective-permute-done.refs_0_
  24.4 0.0 collective-permute-done.1.refs_1_
  24.4 0.0 collective-permute-done.2.refs_2_
  24.4 2.3 %collective-permute-done.3.refs_3_ = f32[3,32,128]{2,1,0:T(8,128)S(1)} collective-permute-done((f32[3,32,128]{2,1,0:T(8,128)S(1)}, f32[3,32,128]{2,1,0:T(8,128)S(1)}, u32[]{:S(2)}, u32[]{:S(2)}) %collective-permute-start.3) | collective-permute-done | bytes 49184 | tf_op jit(solution)/shard_map/ppermute | solution.py:441
  26.7 2.6 %predictor.1 = (f32[3072,128]{1,0:T(8,128)S(1)}, f32[3,32,128]{2,1,0:T(8,128)S(1)}, f32[3,32,128]{2,1,0:T(8,128)S(1)}, f32[3,32,128]{2,1,0:T(8,128)S(1)}, f32[3,32,128]{2,1,0:T(8,128)S(1)}) custom-call(f32[3072,128]{1,0:T(8,128)S(1)} %bitcast.9, f32[3,32,128]{2,1,0:T(8,128)S(1)} %collective-permute-done.refs_0_, ...), custom_call_target="tpu_custom_call" | custom-call | tf_op jit(solution)/shard_map/predictor/pallas_call | solution.py:423
  29.3 0.0 collective-permute-start.6
  29.3 2.9 %collective-permute-start.7 = (f32[3,32,128]{2,1,0:T(8,128)S(1)}, f32[3,32,128]{2,1,0:T(8,128)S(1)}, u32[]{:S(2)}, u32[]{:S(2)}) collective-permute-start(f32[3,32,128]{2,1,0:T(8,128)S(1)} %get-tuple-element.31), channel_id=1, source_target_pairs={{32,0},{64,32},{96,64},{128,96},{160,128},{192,160},{224,192},{0,2... | collective-permute-start | bytes 147464 | tf_op jit(solution)/shard_map/ppermute | solution.py:441
  32.3 1.5 %collective-permute-start.8 = (f32[3,32,128]{2,1,0:T(8,128)S(1)}, f32[3,32,128]{2,1,0:T(8,128)S(1)}, u32[]{:S(2)}, u32[]{:S(2)}) collective-permute-start(f32[3,32,128]{2,1,0:T(8,128)S(1)} %get-tuple-element.32), channel_id=1, source_target_pairs={{0,8},{8,16},{16,24},{24,0},{1,9},{9,17},{17,25},{25,1},{2,10},{10... | collective-permute-start | bytes 147464 | tf_op jit(solution)/shard_map/ppermute | solution.py:440
  33.8 1.7 %collective-permute-start.9 = (f32[3,32,128]{2,1,0:T(8,128)S(1)}, f32[3,32,128]{2,1,0:T(8,128)S(1)}, u32[]{:S(2)}, u32[]{:S(2)}) collective-permute-start(f32[3,32,128]{2,1,0:T(8,128)S(1)} %get-tuple-element.33), channel_id=1, source_target_pairs={{8,0},{16,8},{24,16},{0,24},{9,1},{17,9},{25,17},{1,25},{10,2},{18... | collective-permute-start | bytes 147464 | tf_op jit(solution)/shard_map/ppermute | solution.py:441
  35.5 0.9 %end_faces.3 = (f32[3,8,128]{2,1,0:T(8,128)S(1)}, f32[3,8,128]{2,1,0:T(8,128)S(1)}) custom-call(f32[3072,128]{1,0:T(8,128)S(1)} %get-tuple-element.29.rows_ref.pred_ref), custom_call_target="tpu_custom_call" | custom-call | tf_op jit(solution)/shard_map/end_faces/pallas_call | solution.py:423
  36.4 2.0 %collective-permute-start.10 = (f32[3,8,128]{2,1,0:T(8,128)S(1)}, f32[3,8,128]{2,1,0:T(8,128)S(1)}, u32[]{:S(2)}, u32[]{:S(2)}) collective-permute-start(f32[3,8,128]{2,1,0:T(8,128)S(1)} %get-tuple-element.34), channel_id=1, source_target_pairs={{0,1},{1,2},{2,3},{3,4},{4,5},{5,6},{6,7},{7,0},{8,9},{9,10},{10,1... | collective-permute-start | bytes 36872 | tf_op jit(solution)/shard_map/ppermute | solution.py:440
  38.4 3.8 %collective-permute-done.10.refs_4_ = f32[3,8,128]{2,1,0:T(8,128)S(1)} collective-permute-done((f32[3,8,128]{2,1,0:T(8,128)S(1)}, f32[3,8,128]{2,1,0:T(8,128)S(1)}, u32[]{:S(2)}, u32[]{:S(2)}) %collective-permute-start.10) | collective-permute-done | bytes 12320 | tf_op jit(solution)/shard_map/ppermute | solution.py:440
  42.2 3.2 %collective-permute-start.11 = (f32[3,8,128]{2,1,0:T(8,128)S(1)}, f32[3,8,128]{2,1,0:T(8,128)S(1)}, u32[]{:S(2)}, u32[]{:S(2)}) collective-permute-start(f32[3,8,128]{2,1,0:T(8,128)S(1)} %get-tuple-element.35.rest_0_), channel_id=1, source_target_pairs={{1,0},{2,1},{3,2},{4,3},{5,4},{6,5},{7,6},{0,7},{9,8},{10,9},{11,1... | collective-permute-start | bytes 36872 | tf_op jit(solution)/shard_map/ppermute | solution.py:441
  45.5 12.8 %boxes.3 = (f32[2,3,16,16,128]{4,3,2,1,0:T(8,128)S(1)}, f32[512,256]{1,0:T(8,128)}, f32[512,256]{1,0:T(8,128)}) custom-call(s32[32]{0:T(128)S(1)} %copy-done.3, s32[32,3]{1,0:T(8,128)S(1)} %copy.9.corner_ref.refs_8_, f32[3,32,32,128]{3,2,1,0:T(8,128)S(1)} %copy-done.1, f32[512,256]{1,0:T(8,128)S(1)} %bitcast.13, ...), custom_call_target="tpu_custom_call", output_to_operand_aliasing={{1}: (6, {}), {2}: (7, {})} | custom-call | flops 30000000 | bytes 5000000 | tf_op jit(solution)/shard_map/boxes/pallas_call | solution.py:314
  58.3 0.0 collective-permute-done.11.refs_5_
  58.3 0.0 collective-permute-done.6.refs_0_
  58.3 0.0 collective-permute-done.7.refs_1_
  58.3 0.0 collective-permute-done.9.refs_3_
  58.3 8.0 %final.1 = f32[3072,128]{1,0:T(8,128)} custom-call(f32[3072,128]{1,0:T(8,128)S(1)} %bitcast.10, f32[3072,128]{1,0:T(8,128)S(1)} %get-tuple-element.29.rows_ref.pred_ref, f32[3,32,128]{2,1,0:T(8,128)S(1)} %collective-permute-done.6.refs_0_, f32[3,32,128]{2,1,0:T(8,128)S(1)} %collective-permute-done.7.refs_1_, ...), custom_call_target="tpu_custom_call" | custom-call | tf_op jit(solution)/shard_map/final/pallas_call | solution.py:423
  (11 shorter events, 0.0 us)
Async XLA Ops:
  0.6 1.4 %copy-start = (f32[3,32,32,128]{3,2,1,0:T(8,128)S(1)}, f32[3,32,32,128]{3,2,1,0:T(8,128)}, u32[]{:S(2)}) copy-start(f32[3,32,32,128]{3,2,1,0:T(8,128)} %vel_ref.3) | copy-start | bytes 4718596
  2.0 7.6 %copy-start.4 = (s32[32,3]{0,1:T(4,128)S(1)}, s32[32,3]{0,1:T(4,128)}, u32[]{:S(2)}) copy-start(s32[32,3]{0,1:T(4,128)} %param.6) | copy-start | bytes 1156
  2.0 7.7 %copy-start.1 = (f32[3,32,32,128]{3,2,1,0:T(8,128)S(1)}, f32[3,32,32,128]{3,2,1,0:T(8,128)}, u32[]{:S(2)}) copy-start(f32[3,32,32,128]{3,2,1,0:T(8,128)} %vel_ref.3) | copy-start | bytes 4718596
  2.0 7.7 %copy-start.2 = (f32[32,16,256]{2,1,0:T(8,128)S(1)}, f32[32,16,256]{2,1,0:T(8,128)}, u32[]{:S(2)}) copy-start(f32[32,16,256]{2,1,0:T(8,128)} %param.5) | copy-start | bytes 1572868
  2.0 7.7 %copy-start.3 = (s32[32]{0:T(128)S(1)}, s32[32]{0:T(128)}, u32[]{:S(2)}) copy-start(s32[32]{0:T(128)} %owner_ref.3) | copy-start | bytes 388
  3.0 19.5 %collective-permute-start.4 = (f32[3,8,128]{2,1,0:T(8,128)S(1)}, f32[3,8,128]{2,1,0:T(8,128)S(1)}, u32[]{:S(2)}, u32[]{:S(2)}) collective-permute-start(f32[3,8,128]{2,1,0:T(8,128)S(1)} %get-tuple-element.26), channel_id=1, source_target_pairs={{0,1},{1,2},{2,3},{3,4},{4,5},{5,6},{6,7},{7,0},{8,9},{9,10},{10,1... | collective-permute-start | bytes 36872 | tf_op jit(solution)/shard_map/ppermute | solution.py:440
  5.0 19.4 %collective-permute-start.5 = (f32[3,8,128]{2,1,0:T(8,128)S(1)}, f32[3,8,128]{2,1,0:T(8,128)S(1)}, u32[]{:S(2)}, u32[]{:S(2)}) collective-permute-start(f32[3,8,128]{2,1,0:T(8,128)S(1)} %get-tuple-element.27.rest_0_), channel_id=1, source_target_pairs={{1,0},{2,1},{3,2},{4,3},{5,4},{6,5},{7,6},{0,7},{9,8},{10,9},{11,1... | collective-permute-start | bytes 36872 | tf_op jit(solution)/shard_map/ppermute | solution.py:441
  5.2 19.2 %collective-permute-start = (f32[3,32,128]{2,1,0:T(8,128)S(1)}, f32[3,32,128]{2,1,0:T(8,128)S(1)}, u32[]{:S(2)}, u32[]{:S(2)}) collective-permute-start(f32[3,32,128]{2,1,0:T(8,128)S(1)} %get-tuple-element.22), channel_id=1, source_target_pairs={{0,32},{32,64},{64,96},{96,128},{128,160},{160,192},{192,224},{224... | collective-permute-start | bytes 147464 | tf_op jit(solution)/shard_map/ppermute | solution.py:440
  5.2 19.2 %collective-permute-start.1 = (f32[3,32,128]{2,1,0:T(8,128)S(1)}, f32[3,32,128]{2,1,0:T(8,128)S(1)}, u32[]{:S(2)}, u32[]{:S(2)}) collective-permute-start(f32[3,32,128]{2,1,0:T(8,128)S(1)} %get-tuple-element.23), channel_id=1, source_target_pairs={{32,0},{64,32},{96,64},{128,96},{160,128},{192,160},{224,192},{0,2... | collective-permute-start | bytes 147464 | tf_op jit(solution)/shard_map/ppermute | solution.py:441
  8.1 16.3 %collective-permute-start.2 = (f32[3,32,128]{2,1,0:T(8,128)S(1)}, f32[3,32,128]{2,1,0:T(8,128)S(1)}, u32[]{:S(2)}, u32[]{:S(2)}) collective-permute-start(f32[3,32,128]{2,1,0:T(8,128)S(1)} %get-tuple-element.24), channel_id=1, source_target_pairs={{0,8},{8,16},{16,24},{24,0},{1,9},{9,17},{17,25},{25,1},{2,10},{10... | collective-permute-start | bytes 147464 | tf_op jit(solution)/shard_map/ppermute | solution.py:440
  22.6 4.2 %collective-permute-start.3 = (f32[3,32,128]{2,1,0:T(8,128)S(1)}, f32[3,32,128]{2,1,0:T(8,128)S(1)}, u32[]{:S(2)}, u32[]{:S(2)}) collective-permute-start(f32[3,32,128]{2,1,0:T(8,128)S(1)} %get-tuple-element.25), channel_id=1, source_target_pairs={{8,0},{16,8},{24,16},{0,24},{9,1},{17,9},{25,17},{1,25},{10,2},{18... | collective-permute-start | bytes 147464 | tf_op jit(solution)/shard_map/ppermute | solution.py:441
  29.3 29.0 %collective-permute-start.6 = (f32[3,32,128]{2,1,0:T(8,128)S(1)}, f32[3,32,128]{2,1,0:T(8,128)S(1)}, u32[]{:S(2)}, u32[]{:S(2)}) collective-permute-start(f32[3,32,128]{2,1,0:T(8,128)S(1)} %get-tuple-element.30), channel_id=1, source_target_pairs={{0,32},{32,64},{64,96},{96,128},{128,160},{160,192},{192,224},{224... | collective-permute-start | bytes 147464 | tf_op jit(solution)/shard_map/ppermute | solution.py:440
  29.3 29.0 %collective-permute-start.7 = (f32[3,32,128]{2,1,0:T(8,128)S(1)}, f32[3,32,128]{2,1,0:T(8,128)S(1)}, u32[]{:S(2)}, u32[]{:S(2)}) collective-permute-start(f32[3,32,128]{2,1,0:T(8,128)S(1)} %get-tuple-element.31), channel_id=1, source_target_pairs={{32,0},{64,32},{96,64},{128,96},{160,128},{192,160},{224,192},{0,2... | collective-permute-start | bytes 147464 | tf_op jit(solution)/shard_map/ppermute | solution.py:441
  32.3 26.0 %collective-permute-start.8 = (f32[3,32,128]{2,1,0:T(8,128)S(1)}, f32[3,32,128]{2,1,0:T(8,128)S(1)}, u32[]{:S(2)}, u32[]{:S(2)}) collective-permute-start(f32[3,32,128]{2,1,0:T(8,128)S(1)} %get-tuple-element.32), channel_id=1, source_target_pairs={{0,8},{8,16},{16,24},{24,0},{1,9},{9,17},{17,25},{25,1},{2,10},{10... | collective-permute-start | bytes 147464 | tf_op jit(solution)/shard_map/ppermute | solution.py:440
  33.8 24.6 %collective-permute-start.9 = (f32[3,32,128]{2,1,0:T(8,128)S(1)}, f32[3,32,128]{2,1,0:T(8,128)S(1)}, u32[]{:S(2)}, u32[]{:S(2)}) collective-permute-start(f32[3,32,128]{2,1,0:T(8,128)S(1)} %get-tuple-element.33), channel_id=1, source_target_pairs={{8,0},{16,8},{24,16},{0,24},{9,1},{17,9},{25,17},{1,25},{10,2},{18... | collective-permute-start | bytes 147464 | tf_op jit(solution)/shard_map/ppermute | solution.py:441
  36.4 5.8 %collective-permute-start.10 = (f32[3,8,128]{2,1,0:T(8,128)S(1)}, f32[3,8,128]{2,1,0:T(8,128)S(1)}, u32[]{:S(2)}, u32[]{:S(2)}) collective-permute-start(f32[3,8,128]{2,1,0:T(8,128)S(1)} %get-tuple-element.34), channel_id=1, source_target_pairs={{0,1},{1,2},{2,3},{3,4},{4,5},{5,6},{6,7},{7,0},{8,9},{9,10},{10,1... | collective-permute-start | bytes 36872 | tf_op jit(solution)/shard_map/ppermute | solution.py:440
  42.2 16.0 %collective-permute-start.11 = (f32[3,8,128]{2,1,0:T(8,128)S(1)}, f32[3,8,128]{2,1,0:T(8,128)S(1)}, u32[]{:S(2)}, u32[]{:S(2)}) collective-permute-start(f32[3,8,128]{2,1,0:T(8,128)S(1)} %get-tuple-element.35.rest_0_), channel_id=1, source_target_pairs={{1,0},{2,1},{3,2},{4,3},{5,4},{6,5},{7,6},{0,7},{9,8},{10,9},{11,1... | collective-permute-start | bytes 36872 | tf_op jit(solution)/shard_map/ppermute | solution.py:441

commit v3 on v2

--- a/solution.py
+++ b/solution.py
@@ -13,7 +13,7 @@
 LANES = 128
 PER = 8
 
-CUT, LEVEL, MI, MJ, WENO, CENTRAL, KAPPA, DEPOSIT, PLANES = 6, 8, 5, 4, 8, 8, 8, 6, 4
+CUT, LEVEL, MI, MJ, WENO, CENTRAL, KAPPA, DEPOSIT, PLANES = 6, 8, 5, 4, 16, 8, 16, 6, 4
 
 box_step = 0.25
 pseudo_step = 0.3
@@ -73,10 +73,10 @@
 ROWS = 32
 
 
-def box_body(first_group, count, owner_ref, corner_ref, vel_ref, level_lo, level_hi, *rest):
-    (force_out, settled_out, bending_out, *scratch) = rest[-15:]
+def box_body(first_group, count, owner_ref, corner_ref, vel_ref, level_ref, *rest):
+    (force_out, settled_out, bending_out, *scratch) = rest[-17:]
     (u_ref, l_ref, mi_ref, mj_ref, pa, pb, c_ref, s_ref, k_ref) = scratch[:9]
-    turned, turned_kappa, sems = scratch[9], scratch[10], scratch[11]
+    turned, turned_kappa, levels, sems, level_sems = scratch[9:]
     row, lane = iotas()
     k = lane % BOX
     block = lane // BOX
@@ -115,11 +115,13 @@
                             mask=here,
                         )
 
+        for jt in range(2):
+            come(own, jt).wait()
+
         @pl.loop(0, BOX, unroll=LEVEL)
         def _(i):
             for jt in range(2):
-                level = (level_lo, level_hi)[jt]
-                x = level[pl.ds(own * (PER * BOX) + i, 8, stride=BOX), :]
+                x = levels[pl.ds((own + count * jt) * (PER * BOX) + i, 8, stride=BOX), :]
                 l_ref[i, pl.ds(8 + 8 * jt, 8), :] = block_transpose(x, row, lane)
 
         mi_ref[0] = jnp.zeros((BOX, LANES), F32)
@@ -273,6 +275,15 @@
         for copy in sent(own):
             copy.start()
 
+    def come(own, jt):
+        return pltpu.make_async_copy(
+            level_ref.at[
+                pl.ds((first_group + own) * (PER * BOX), PER * BOX), pl.ds(LANES * jt, LANES)
+            ],
+            levels.at[pl.ds((own + count * jt) * (PER * BOX), PER * BOX), :],
+            level_sems.at[own, jt],
+        )
+
     def sent(own):
         copies = []
         for n, (src, dst) in enumerate(((turned, settled_out), (turned_kappa, bending_out))):
@@ -287,6 +298,10 @@
                 )
         return copies
 
+    for own in range(count):
+        for jt in range(2):
+            come(own, jt).start()
+
     @pl.loop(0, count)
     def _(own):
         one_group(own)
@@ -300,28 +315,19 @@
     smem = pl.BlockSpec(memory_space=pltpu.SMEM)
     any_ = pl.BlockSpec(memory_space=pl.ANY)
     vmem = pl.BlockSpec(memory_space=pltpu.VMEM)
-    halves = [
-        pl.BlockSpec(
-            (count * PER * BOX, LANES),
-            functools.partial(lambda h, s: (first_group // count, h), h),
-        )
-        for h in range(2)
-    ]
-    whole = pl.BlockSpec(velocity.shape, lambda s: (0, 0, 0, 0))
     plane = lambda *lead: pltpu.VMEM((*lead, LANES), F32)
     force = (count, 3, BOX, BOX, LANES)
-    operands = [owner, corners, velocity, level_rows, level_rows, after, *carried]
+    operands = [owner, corners, velocity, level_rows, after, *carried]
     return pl.pallas_call(
         functools.partial(box_body, first_group, count),
-        grid=(1,),
         out_shape=(
             jax.ShapeDtypeStruct(force, F32),
             jax.ShapeDtypeStruct(level_rows.shape, F32),
             jax.ShapeDtypeStruct(level_rows.shape, F32),
         ),
-        in_specs=[smem, smem, whole, *halves, any_] + [any_] * len(carried),
-        out_specs=(pl.BlockSpec(force, lambda s: (0,) * 5), any_, any_),
-        input_output_aliases={6: 1, 7: 2} if carried else {},
+        in_specs=[smem, smem, vmem, any_, any_] + [any_] * len(carried),
+        out_specs=(vmem, any_, any_),
+        input_output_aliases={5: 1, 6: 2} if carried else {},
         scratch_shapes=[
             plane(3, BOX, BOX),
             plane(BOX, ROWS),
@@ -334,7 +340,9 @@
             plane(BOX, BOX),
             plane(count * 2 * PER * BOX),
             plane(count * 2 * PER * BOX),
+            plane(count * 2 * PER * BOX),
             pltpu.SemaphoreType.DMA((count, 4)),
+            pltpu.SemaphoreType.DMA((count, 2)),
         ],
         compiler_params=pltpu.CompilerParams(vmem_limit_bytes=20 * 2**20),
         cost_estimate=pl.CostEstimate(
@@ -384,46 +392,230 @@
 PLANE = 48
 
 
-def side_faces(rows_ref, xlo, xhi, ylo, yhi):
-    for c in range(3):
-        xlo[c] = rows_ref[pl.ds(c * 1024, 32), :]
-        xhi[c] = rows_ref[pl.ds(c * 1024 + 31 * 32, 32), :]
-        ylo[c] = rows_ref[pl.ds(c * 1024, 32, stride=32), :]
-        yhi[c] = rows_ref[pl.ds(c * 1024 + 31, 32, stride=32), :]
-
-
-def end_faces_body(rows_ref, zlo, zhi):
+PACKED = jax.ShapeDtypeStruct((2, 3, 8, LANES), F32)
+Y_ROWS = 80
+X_ROWS = 88
+
+
+def z_faces(rows_ref, lo_ref, hi_ref):
     _, lane = iotas()
 
     def one(x, packed):
         out = []
         for c in range(3):
-            lo, hi = packed[2 * c], packed[2 * c + 1]
+            parts = packed[4 * c : 4 * c + 4]
             for yt in range(4):
                 n = x * 4 + yt
                 at = pl.multiple_of(c * 1024 + x * 32 + 8 * yt, 8)
                 turned = pltpu.roll(rows_ref[pl.ds(at, 8), :], n, 1)
-                lo = jnp.where(lane == n, turned, lo)
-                hi = jnp.where(lane == (n + LANES - 1) % LANES, turned, hi)
-            out += [lo, hi]
+                parts = [
+                    jnp.where(lane == (n + shift + LANES) % LANES, turned, part)
+                    for shift, part in zip((0, 1, -1, -2), parts)
+                ]
+            out += parts
         return tuple(out)
 
-    packed = lax.fori_loop(0, 32, one, (jnp.zeros(TILE, F32),) * 6, unroll=PLANES)
+    packed = lax.fori_loop(0, 32, one, (jnp.zeros(TILE, F32),) * 12, unroll=PLANES)
     for c in range(3):
-        zlo[c] = packed[2 * c]
-        zhi[c] = packed[2 * c + 1]
-
-
-SIDES = jax.ShapeDtypeStruct((3, 32, LANES), F32)
-ENDS = jax.ShapeDtypeStruct((3, 8, LANES), F32)
-
-
-def in_vmem(body, out_shape, operands, scratch=(), limit=16, name=None, smem=0):
+        first, second, last, before = packed[4 * c : 4 * c + 4]
+        lo_ref[0, c] = first
+        lo_ref[1, c] = pltpu.roll(second, LANES - 1, 1)
+        hi_ref[0, c] = pltpu.roll(last, 1, 1)
+        hi_ref[1, c] = pltpu.roll(before, 2, 1)
+
+
+def y_faces(rows_ref, below_ref, above_ref, _, lo_ref, hi_ref):
+    for c in range(3):
+        for out, layers in ((lo_ref, (0, 1)), (hi_ref, (31, 30))):
+            for n, y in enumerate(layers):
+                out[c, pl.ds(32 * n, 32), :] = rows_ref[pl.ds(c * 1024 + y, 32, stride=32), :]
+            out[c, pl.ds(64, 8), :] = below_ref[0, c]
+            out[c, pl.ds(72, 8), :] = above_ref[0, c]
+
+
+def x_faces(rows_ref, below_ref, above_ref, left_ref, right_ref, _, lo_ref, hi_ref):
+    for c in range(3):
+        for out, layers in ((lo_ref, (0, 1)), (hi_ref, (31, 30))):
+            for n, x in enumerate(layers):
+                out[c, pl.ds(32 * n, 32), :] = rows_ref[pl.ds(c * 1024 + 32 * x, 32), :]
+            out[c, pl.ds(64, 8), :] = jnp.zeros(TILE, F32)
+            out[c, pl.ds(64, 1), :] = left_ref[c, pl.ds(layers[0], 1), :]
+            out[c, pl.ds(65, 1), :] = right_ref[c, pl.ds(layers[0], 1), :]
+            out[c, pl.ds(72, 8), :] = below_ref[0, c]
+            out[c, pl.ds(80, 8), :] = above_ref[0, c]
+
+
+def exchange(lo, hi, axis):
+    size = lax.axis_size(axis)
+    up = [(i, (i + 1) % size) for i in range(size)]
+    down = [(j, i) for i, j in up]
+    return lax.ppermute(hi, axis, up), lax.ppermute(lo, axis, down)
+
+
+def slopes_to_f(centre, v, lower, upper):
+    advect = sum(centre[d] * (upper[d] - lower[d]) for d in range(3))
+    spread = (upper[0] + lower[0]) + (upper[1] + lower[1]) + (upper[2] + lower[2]) - 6.0 * v
+    return viscosity * spread - 0.5 * advect
+
+
+def along_z(v, before, after, lane):
+    lower = jnp.where(lane == 0, before, pltpu.roll(v, 1, 1))
+    upper = jnp.where(lane == LANES - 1, after, pltpu.roll(v, LANES - 1, 1))
+    return lower, upper
+
+
+def tile_step(ext, planes, plane, yt, below, above, n, lane):
+    at = [
+        pl.multiple_of((c * planes + plane) * PLANE + 8 + 8 * yt, 8) for c in range(3)
+    ]
+    centre = [ext[pl.ds(at[c], 8), :] for c in range(3)]
+    out = []
+    for c in range(3):
+        v = centre[c]
+        lower2, upper2 = along_z(
+            v,
+            pltpu.roll(below[c], (LANES - n) % LANES, 1),
+            pltpu.roll(above[c], LANES - 1 - n, 1),
+            lane,
+        )
+        lower = (ext[pl.ds(at[c] - PLANE, 8), :], ext[pl.ds(at[c] - 1, 8), :], lower2)
+        upper = (ext[pl.ds(at[c] + PLANE, 8), :], ext[pl.ds(at[c] + 1, 8), :], upper2)
+        out.append(v + grid_step * slopes_to_f(centre, v, lower, upper))
+    return out
+
+
+def packed_step(own, beyond, inner, x_sides, y_sides, outward, row, lane):
+    out = []
+    for c in range(3):
+        v = own[c]
+        x_lower = jnp.where(lane < 4, pltpu.roll(x_sides[0][c], 4, 1), pltpu.roll(v, 4, 1))
+        x_upper = jnp.where(
+            lane >= LANES - 4,
+            pltpu.roll(x_sides[1][c], LANES - 4, 1),
+            pltpu.roll(v, LANES - 4, 1),
+        )
+        down = pltpu.roll(v, 1, 0)
+        down_side = pltpu.roll(pltpu.roll(y_sides[0][c], 1, 0), LANES - 3, 1)
+        y_lower = jnp.where(
+            row == 0, jnp.where(lane % 4 == 0, down_side, pltpu.roll(down, 1, 1)), down
+        )
+        up = pltpu.roll(v, 7, 0)
+        up_side = pltpu.roll(pltpu.roll(y_sides[1][c], 7, 0), 3, 1)
+        y_upper = jnp.where(
+            row == 7, jnp.where(lane % 4 == 3, up_side, pltpu.roll(up, LANES - 1, 1)), up
+        )
+        pair = (inner[c], beyond[c]) if outward else (beyond[c], inner[c])
+        f = slopes_to_f(own, v, (x_lower, y_lower, pair[0]), (x_upper, y_upper, pair[1]))
+        out.append(v + grid_step * f)
+    return out
+
+
+def momentum_body(
+    vel_ref, z_lo, z_hi, below, above, left, right, front, back, force_a, force_b, force_c,
+    corner_ref, out_ref, ext, later, sides, packed,
+):
+    row, lane = iotas()
+    for c in range(3):
+        base = c * 36 * PLANE
+        for plane, halo, layer in ((1, front, 0), (0, front, 1), (34, back, 0), (35, back, 1)):
+            ext[pl.ds(base + plane * PLANE + 8, 32), :] = halo[c, pl.ds(32 * layer, 32), :]
+        for plane, halo in ((1, front), (34, back)):
+            ext[pl.ds(base + plane * PLANE + 7, 1), :] = halo[c, pl.ds(64, 1), :]
+            ext[pl.ds(base + plane * PLANE + 40, 1), :] = halo[c, pl.ds(65, 1), :]
+        ext[pl.ds(base + 2 * PLANE + 7, 32, stride=PLANE), :] = left[c, pl.ds(0, 32), :]
+        ext[pl.ds(base + 2 * PLANE + 40, 32, stride=PLANE), :] = right[c, pl.ds(0, 32), :]
+
+    @pl.loop(0, 32)
+    def _(x):
+        for c in range(3):
+            at = pl.multiple_of((c * 36 + x + 2) * PLANE + 8, 8)
+            ext[pl.ds(at, 32), :] = vel_ref[pl.ds(pl.multiple_of(c * 1024 + x * 32, 8), 32), :]
+
+    @pl.loop(0, 32, unroll=PLANES)
+    def _(x):
+        lo = [below[0, c] for c in range(3)]
+        hi = [above[0, c] for c in range(3)]
+        for yt in range(4):
+            new = tile_step(ext, 36, x + 2, yt, lo, hi, x * 4 + yt, lane)
+            for c in range(3):
+                at = pl.multiple_of((c * 34 + x + 1) * PLANE + 8 + 8 * yt, 8)
+                later[pl.ds(at, 8), :] = new[c]
+
+    for halo, plane, x in ((front, 1, 31), (back, 34, 0)):
+        lo = [halo[c, pl.ds(72, 8), :] for c in range(3)]
+        hi = [halo[c, pl.ds(80, 8), :] for c in range(3)]
+        for yt in range(4):
+            new = tile_step(ext, 36, plane, yt, lo, hi, x * 4 + yt, lane)
+            for c in range(3):
+                later[pl.ds((c * 34 + plane - 1) * PLANE + 8 + 8 * yt, 8), :] = new[c]
+
+    for halo, out_row, y, inside in ((left, 7, 31, 0), (right, 40, 0, 31)):
+        for c in range(3):
+            sides[c, pl.ds(8, 32), :] = halo[c, pl.ds(0, 32), :]
+            for at, end in ((7, front), (40, back)):
+                sides[c, pl.ds(at, 1), :] = end[c, pl.ds(64 if out_row == 7 else 65, 1), :]
+        for t in range(4):
+            at = pl.ds(8 + 8 * t, 8)
+            centre = [sides[c, at, :] for c in range(3)]
+            where_x = 4 * (8 * t + row) + y // 8
+            for c in range(3):
+                v = centre[c]
+                ends = [
+                    jnp.take_along_axis(
+                        jnp.broadcast_to(halo[c, pl.ds(64 + 8 * e + y % 8, 1), :], TILE),
+                        where_x,
+                        axis=1,
+                    )
+                    for e in range(2)
+                ]
+                lower2, upper2 = along_z(v, *ends, lane)
+                beyond = halo[c, pl.ds(32 + 8 * t, 8), :]
+                inner = vel_ref[pl.ds(c * 1024 + 8 * t * 32 + inside, 8, stride=32), :]
+                pair = (beyond, inner) if out_row == 7 else (inner, beyond)
+                lower = (sides[c, pl.ds(7 + 8 * t, 8), :], pair[0], lower2)
+                upper = (sides[c, pl.ds(9 + 8 * t, 8), :], pair[1], upper2)
+                new = v + grid_step * slopes_to_f(centre, v, lower, upper)
+                rows = pl.ds((c * 34 + 8 * t + 1) * PLANE + out_row, 8, stride=PLANE)
+                later[rows, :] = new
+
+    for outward, halo, own_face in ((0, below, z_lo), (1, above, z_hi)):
+        x_at, y_at = pl.ds(72 + 8 * outward, 8), pl.ds(64 + 8 * outward, 8)
+        new = packed_step(
+            [halo[0, c] for c in range(3)],
+            [halo[1, c] for c in range(3)],
+            [own_face[0, c] for c in range(3)],
+            [[side[c, x_at, :] for c in range(3)] for side in (front, back)],
+            [[side[c, y_at, :] for c in range(3)] for side in (left, right)],
+            outward,
+            row,
+            lane,
+        )
+        for c in range(3):
+            packed[outward, c] = new[c]
+
+    @pl.loop(0, 32, unroll=PLANES)
+    def _(x):
+        lo = [packed[0, c] for c in range(3)]
+        hi = [packed[1, c] for c in range(3)]
+        for yt in range(4):
+            new = tile_step(later, 34, x + 1, yt, lo, hi, x * 4 + yt, lane)
+            for c in range(3):
+                at = pl.ds(pl.multiple_of(c * 1024 + x * 32 + 8 * yt, 8), 8)
+                out_ref[at, :] = 0.5 * (vel_ref[at, :] + new[c])
+
+    deposit((force_a, force_b, force_c), corner_ref, out_ref)
+
+
+def call(body, out_shape, operands, name, unread=0, corners=None, scratch=(), limit=16):
     vmem = pl.BlockSpec(memory_space=pltpu.VMEM)
+    specs = [vmem] * (len(operands) - unread) + [pl.BlockSpec(memory_space=pl.ANY)] * unread
+    if corners is not None:
+        operands = [*operands, corners]
+        specs.append(pl.BlockSpec(memory_space=pltpu.SMEM))
     return pl.pallas_call(
         body,
         out_shape=out_shape,
-        in_specs=[vmem] * (len(operands) - smem) + [pl.BlockSpec(memory_space=pltpu.SMEM)] * smem,
+        in_specs=specs,
         out_specs=jax.tree.map(lambda _: vmem, out_shape),
         scratch_shapes=scratch,
         compiler_params=pltpu.CompilerParams(vmem_limit_bytes=limit * 2**20),
@@ -431,133 +623,37 @@
     )(*operands)
 
 
-def exchange(faces, axes):
-    halos = []
-    for d, axis in enumerate(axes):
-        size = lax.axis_size(axis)
-        up = [(i, (i + 1) % size) for i in range(size)]
-        down = [(j, i) for i, j in up]
-        halos.append(lax.ppermute(faces[2 * d + 1], axis, up))
-        halos.append(lax.ppermute(faces[2 * d], axis, down))
-    return halos
-
-
-def fill_padded(src_ref, halos, ext):
-    xlo, xhi, ylo, yhi, _, _ = halos
-    for c in range(3):
-        base = c * 34 * PLANE
-        ext[pl.ds(base + 8, 32), :] = xlo[c]
-        ext[pl.ds(base + 33 * PLANE + 8, 32), :] = xhi[c]
-        ext[pl.ds(base + PLANE + 7, 32, stride=PLANE), :] = ylo[c]
-        ext[pl.ds(base + PLANE + 40, 32, stride=PLANE), :] = yhi[c]
-
-    @pl.loop(0, 32)
-    def _(x):
-        for c in range(3):
-            at = pl.multiple_of(c * 34 * PLANE + (x + 1) * PLANE + 8, 8)
-            ext[pl.ds(at, 32), :] = src_ref[pl.ds(pl.multiple_of(c * 1024 + x * 32, 8), 32), :]
-
-
-def tendencies(ext, zlo, zhi, x, yt, lane):
-    n = x * 4 + yt
-    at = [
-        pl.multiple_of(c * 34 * PLANE + (x + 1) * PLANE + 8 + 8 * yt, 8) for c in range(3)
-    ]
-    centre = [ext[pl.ds(at[c], 8), :] for c in range(3)]
-    out = []
-    for c in range(3):
-        v = centre[c]
-        up0 = ext[pl.ds(at[c] + PLANE, 8), :]
-        lo0 = ext[pl.ds(at[c] - PLANE, 8), :]
-        up1 = ext[pl.ds(at[c] + 1, 8), :]
-        lo1 = ext[pl.ds(at[c] - 1, 8), :]
-        lo2 = jnp.where(
-            lane == 0, pltpu.roll(zlo[c], (LANES + 1 - n) % LANES, 1), pltpu.roll(v, 1, 1)
-        )
-        up2 = jnp.where(
-            lane == LANES - 1,
-            pltpu.roll(zhi[c], LANES - 1 - n, 1),
-            pltpu.roll(v, LANES - 1, 1),
-        )
-        advect = centre[0] * (up0 - lo0) + centre[1] * (up1 - lo1) + centre[2] * (up2 - lo2)
-        spread = (up0 + lo0) + (up1 + lo1) + (up2 + lo2) - 6.0 * v
-        out.append(viscosity * spread - 0.5 * advect)
-    return centre, out
-
-
-PADDED = [pltpu.VMEM((3 * 34 * PLANE, LANES), F32)]
-
-
-def stage(src_ref, halos, ext, write):
-    fill_padded(src_ref, halos, ext)
-    _, lane = iotas()
-    zlo, zhi = halos[4], halos[5]
-
-    @pl.loop(0, 32, unroll=PLANES)
-    def _(x):
-        zl = [zlo[c] for c in range(3)]
-        zh = [zhi[c] for c in range(3)]
-        for yt in range(4):
-            centre, f = tendencies(ext, zl, zh, x, yt, lane)
-            for c in range(3):
-                at = pl.ds(pl.multiple_of(c * 1024 + x * 32 + 8 * yt, 8), 8)
-                write(at, centre[c] + grid_step * f[c])
-
-
-def predictor_body(vel_ref, *refs):
-    halos, out_ref, sides, ext = refs[:6], refs[-6], refs[-5:-1], refs[-1]
-
-    def write(at, value):
-        out_ref[at, :] = value
-
-    stage(vel_ref, halos, ext, write)
-    side_faces(out_ref, *sides)
-
-
-def final_body(vel_ref, pred_ref, *refs):
-    halos, forces, corner_ref, out_ref, ext = refs[:6], refs[6:-3], refs[-3], refs[-2], refs[-1]
-
-    def write(at, value):
-        out_ref[at, :] = 0.5 * (vel_ref[at, :] + value)
-
-    stage(pred_ref, halos, ext, write)
-    deposit(forces, corner_ref, out_ref)
-
-
 def local(velocity, box_level, corners, owner_list):
     slots = box_level.shape[0]
     rows = velocity.reshape(-1, LANES)
     level_rows = box_level.reshape(slots * BOX, BOX * BOX)
-    half = slots // PER // 2
-    sides = in_vmem(side_faces, (SIDES,) * 4, [rows], name="side_faces")
-    halos = exchange(sides, ("gx", "gy"))
-    ends = in_vmem(end_faces_body, (ENDS,) * 2, [rows], name="end_faces")
-    halos += exchange(ends, ("gz",))
-    force_a, settled, bending = boxes(
-        0, half, owner_list, corners, velocity, level_rows, ends[0]
+    work = functools.partial(boxes, owner=owner_list, corners=corners, velocity=velocity, level_rows=level_rows)
+    z_lo, z_hi = call(z_faces, (PACKED,) * 2, [rows], "z_faces")
+    below, above = exchange(z_lo, z_hi, "gz")
+    force_a, *done = work(0, 1, after=z_lo)
+    sent = jax.ShapeDtypeStruct((3, Y_ROWS, LANES), F32)
+    faces = call(y_faces, (sent,) * 2, [rows, below, above, force_a], "y_faces", unread=1)
+    left, right = exchange(*faces, "gy")
+    force_b, *done = work(1, 1, after=faces[0], carried=done)
+    sent = jax.ShapeDtypeStruct((3, X_ROWS, LANES), F32)
+    faces = call(
+        x_faces, (sent,) * 2, [rows, below, above, left, right, force_b], "x_faces", unread=1
     )
-    predictor, *sides = in_vmem(
-        predictor_body,
-        (jax.ShapeDtypeStruct(rows.shape, F32), *(SIDES,) * 4),
-        [rows, *halos, force_a[0, 0, 0]],
-        PADDED,
-        24,
-        "predictor",
-    )
-    halos = exchange(sides, ("gx", "gy"))
-    ends = in_vmem(end_faces_body, (ENDS,) * 2, [predictor], name="end_faces")
-    halos += exchange(ends, ("gz",))
-    force_b, settled, bending = boxes(
-        half, half, owner_list, corners, velocity, level_rows, ends[0], (settled, bending)
-    )
-    result = in_vmem(
-        final_body,
+    front, back = exchange(*faces, "gx")
+    force_c, settled, bending = work(2, slots // PER - 2, after=faces[0], carried=done)
+    result = call(
+        momentum_body,
         jax.ShapeDtypeStruct(rows.shape, F32),
-        [rows, predictor, *halos, force_a, force_b, corners],
-        PADDED,
-        32,
-        "final",
-        smem=1,
+        [rows, z_lo, z_hi, below, above, left, right, front, back, force_a, force_b, force_c],
+        "momentum",
+        corners=corners,
+        scratch=[
+            pltpu.VMEM((3 * 36 * PLANE, LANES), F32),
+            pltpu.VMEM((3 * 34 * PLANE, LANES), F32),
+            pltpu.VMEM((3, PLANE, LANES), F32),
+            pltpu.VMEM((2, 3, 8, LANES), F32),
+        ],
+        limit=32,
     )
     return (
         result.reshape(velocity.shape),

time: 66.5 us -> 52.9 us (0.80)
  the two profiles are of different devices: /device:TPU:32 before, /device:TPU:1 now
where the time goes in v3:
time: 52.9 us; the launch traced here: 52.8 us
  Pallas kernels  37.5 us (71%)
  starting transfers between devices  12 us (23%)
  local copies, waits for them, and re-layouts  2.55 us (5%)
  between operations  0.74 us (1%)
    pallas_call x3, Pallas kernels, boxes(): pl.pallas_call(functools.partial(box_body, first_group, count), out_shape...  25.7 us
    ppermute x6, starting transfers between devices, exchange(): return (lax.ppermute(hi, axis, up), lax.ppermute(lo, axis, down))  12 us
    pallas_call x4, Pallas kernels, call(): pl.pallas_call(body, out_shape=out_shape, in_specs=specs, out_specs=jax.t...  11.8 us
    unnamed x13, local copies, waits for them, and re-layouts  2.55 us
  transfers between devices with their start and end apart: 6, of which 0 were waited for; matrix products, arithmetic and copies ran while one was open for 0% of the time, Pallas kernels for 49%

profile of v3, /device:TPU:1, one launch (start us, length us, event | category | flops | bytes accessed | tf_op | source)
XLA Modules:
  0.0 52.8 jit_solution(2809199367109211788)
XLA Ops:
  0.6 0.0 copy-start.4
  0.6 0.0 copy-start
  0.7 1.4 %copy-done = f32[3,32,32,128]{3,2,1,0:T(8,128)S(1)} copy-done((f32[3,32,32,128]{3,2,1,0:T(8,128)S(1)}, f32[3,32,32,128]{3,2,1,0:T(8,128)}, u32[]{:S(2)}) %copy-start) | copy-done | bytes 1572888
  2.1 0.0 copy-start.5
  2.1 0.0 copy-start.1
  2.1 1.0 %z_faces.1 = (f32[2,3,8,128]{3,2,1,0:T(8,128)S(1)}, f32[2,3,8,128]{3,2,1,0:T(8,128)S(1)}) custom-call(f32[3072,128]{1,0:T(8,128)S(1)} %bitcast.5), custom_call_target="tpu_custom_call" | custom-call | tf_op jit(solution)/shard_map/z_faces/pallas_call | solution.py:615
  3.1 2.5 %collective-permute-start = (f32[2,3,8,128]{3,2,1,0:T(8,128)S(1)}, f32[2,3,8,128]{3,2,1,0:T(8,128)S(1)}, u32[]{:S(2)}, u32[]{:S(2)}) collective-permute-start(f32[2,3,8,128]{3,2,1,0:T(8,128)S(1)} %get-tuple-element.19.z_hi), channel_id=1, source_target_pairs={{0,1},{1,2},{2,3},{3,4},{4,5},{5,6},{6,7},{7,0},{8,9},{9,10},{10,1... | collective-permute-start | bytes 73736 | tf_op jit(solution)/shard_map/ppermute | solution.py:452
  5.6 4.0 %collective-permute-start.1 = (f32[2,3,8,128]{3,2,1,0:T(8,128)S(1)}, f32[2,3,8,128]{3,2,1,0:T(8,128)S(1)}, u32[]{:S(2)}, u32[]{:S(2)}) collective-permute-start(f32[2,3,8,128]{3,2,1,0:T(8,128)S(1)} %get-tuple-element.18.rest_0_.z_lo), channel_id=1, source_target_pairs={{1,0},{2,1},{3,2},{4,3},{5,4},{6,5},{7,6},{0,7},{9,8},{10,9},{11,1... | collective-permute-start | bytes 73736 | tf_op jit(solution)/shard_map/ppermute | solution.py:452
  9.6 0.0 copy-done.5
  9.6 0.1 copy.11.corner_ref
  9.7 0.0 copy-done.4
  9.7 0.0 copy-done.1
  9.7 0.0 copy-start.2
  9.7 1.0 %copy-done.2 = f32[32,16,256]{2,1,0:T(8,128)S(1)} copy-done((f32[32,16,256]{2,1,0:T(8,128)S(1)}, f32[32,16,256]{2,1,0:T(8,128)}, u32[]{:S(2)}) %copy-start.2) | copy-done | bytes 524312
  10.7 0.0 copy-start.3
  10.7 6.8 %boxes.3 = (f32[1,3,16,16,128]{4,3,2,1,0:T(8,128)S(1)}, f32[512,256]{1,0:T(8,128)}, f32[512,256]{1,0:T(8,128)}) custom-call(s32[32]{0:T(128)S(1)} %copy-done.4, s32[32,3]{1,0:T(8,128)S(1)} %copy.11.corner_ref, f32[3,32,32,128]{3,2,1,0:T(8,128)S(1)} %copy-done.1, f32[512,256]{1,0:T(8,128)S(1)} %bitcast.9, f32[2,3,8,128]{3,2,1,0:T(8,128)S(1)} %get-tuple-element.18.rest_0_.z_lo), custom_call_target="tpu_custom_call" | custom-call | flops 30000000 | bytes 5000000 | tf_op jit(solution)/shard_map/boxes/pallas_call | solution.py:321
  17.5 0.0 collective-permute-done.below_ref.below
  17.6 0.0 collective-permute-done.1.above_ref.above
  17.6 0.1 y_faces.1
  17.7 1.3 %collective-permute-start.2 = (f32[3,80,128]{2,1,0:T(8,128)S(1)}, f32[3,80,128]{2,1,0:T(8,128)S(1)}, u32[]{:S(2)}, u32[]{:S(2)}) collective-permute-start(f32[3,80,128]{2,1,0:T(8,128)S(1)} %get-tuple-element.21), channel_id=1, source_target_pairs={{0,8},{8,16},{16,24},{24,0},{1,9},{9,17},{17,25},{25,1},{2,10},{10... | collective-permute-start | bytes 368648 | tf_op jit(solution)/shard_map/ppermute | solution.py:452
  19.0 1.5 %collective-permute-start.3 = (f32[3,80,128]{2,1,0:T(8,128)S(1)}, f32[3,80,128]{2,1,0:T(8,128)S(1)}, u32[]{:S(2)}, u32[]{:S(2)}) collective-permute-start(f32[3,80,128]{2,1,0:T(8,128)S(1)} %get-tuple-element.22.rest_0_), channel_id=1, source_target_pairs={{8,0},{16,8},{24,16},{0,24},{9,1},{17,9},{25,17},{1,25},{10,2},{18... | collective-permute-start | bytes 368648 | tf_op jit(solution)/shard_map/ppermute | solution.py:452
  20.5 0.0 copy-done.3
  20.5 6.8 %boxes.4 = (f32[1,3,16,16,128]{4,3,2,1,0:T(8,128)S(1)}, f32[512,256]{1,0:T(8,128)}, f32[512,256]{1,0:T(8,128)}) custom-call(s32[32]{0:T(128)S(1)} %copy-done.4, s32[32,3]{1,0:T(8,128)S(1)} %copy.11.corner_ref, f32[3,32,32,128]{3,2,1,0:T(8,128)S(1)} %copy-done.1, f32[512,256]{1,0:T(8,128)S(1)} %bitcast.10, ...), custom_call_target="tpu_custom_call", output_to_operand_aliasing={{1}: (5, {}), {2}: (6, {})} | custom-call | flops 30000000 | bytes 5000000 | tf_op jit(solution)/shard_map/boxes/pallas_call | solution.py:321
  27.3 0.0 collective-permute-done.2.left_ref.left
  27.3 0.0 collective-permute-done.3.right_ref.right
  27.4 2.6 %collective-permute-start.4 = (f32[3,88,128]{2,1,0:T(8,128)S(1)}, f32[3,88,128]{2,1,0:T(8,128)S(1)}, u32[]{:S(2)}, u32[]{:S(2)}) collective-permute-start(f32[3,88,128]{2,1,0:T(8,128)S(1)} %get-tuple-element.26), channel_id=1, source_target_pairs={{0,32},{32,64},{64,96},{96,128},{128,160},{160,192},{192,224},{224... | collective-permute-start | bytes 405512 | tf_op jit(solution)/shard_map/ppermute | solution.py:452
  30.0 0.0 collective-permute-start.5
  30.0 12.1 %boxes.5 = (f32[2,3,16,16,128]{4,3,2,1,0:T(8,128)S(1)}, f32[512,256]{1,0:T(8,128)}, f32[512,256]{1,0:T(8,128)}) custom-call(s32[32]{0:T(128)S(1)} %copy-done.4, s32[32,3]{1,0:T(8,128)S(1)} %copy.11.corner_ref, f32[3,32,32,128]{3,2,1,0:T(8,128)S(1)} %copy-done.1, f32[512,256]{1,0:T(8,128)S(1)} %bitcast.11, ...), custom_call_target="tpu_custom_call", output_to_operand_aliasing={{1}: (5, {}), {2}: (6, {})} | custom-call | flops 30000000 | bytes 5000000 | tf_op jit(solution)/shard_map/boxes/pallas_call | solution.py:321
  42.2 0.0 collective-permute-done.4.front
  42.2 0.0 collective-permute-done.5.back
  42.2 10.6 %momentum.1 = f32[3072,128]{1,0:T(8,128)} custom-call(f32[3072,128]{1,0:T(8,128)S(1)} %bitcast.8, f32[2,3,8,128]{3,2,1,0:T(8,128)S(1)} %get-tuple-element.18.rest_0_.z_lo, f32[2,3,8,128]{3,2,1,0:T(8,128)S(1)} %get-tuple-element.19.z_hi, f32[2,3,8,128]{3,2,1,0:T(8,128)S(1)} %collective-permute-done.below_ref.below, ...), custom_call_target="tpu_custom_call" | custom-call | tf_op jit(solution)/shard_map/momentum/pallas_call | solution.py:615
  (1 shorter events, 0.0 us)
Async XLA Ops:
  0.6 9.1 %copy-start.4 = (s32[32]{0:T(128)S(1)}, s32[32]{0:T(128)}, u32[]{:S(2)}) copy-start(s32[32]{0:T(128)} %owner_ref.5) | copy-start | bytes 388
  0.6 1.4 %copy-start = (f32[3,32,32,128]{3,2,1,0:T(8,128)S(1)}, f32[3,32,32,128]{3,2,1,0:T(8,128)}, u32[]{:S(2)}) copy-start(f32[3,32,32,128]{3,2,1,0:T(8,128)} %vel_ref.5) | copy-start | bytes 4718596
  2.1 7.5 %copy-start.5 = (s32[32,3]{0,1:T(4,128)S(1)}, s32[32,3]{0,1:T(4,128)}, u32[]{:S(2)}) copy-start(s32[32,3]{0,1:T(4,128)} %param.6) | copy-start | bytes 1156
  2.1 7.6 %copy-start.1 = (f32[3,32,32,128]{3,2,1,0:T(8,128)S(1)}, f32[3,32,32,128]{3,2,1,0:T(8,128)}, u32[]{:S(2)}) copy-start(f32[3,32,32,128]{3,2,1,0:T(8,128)} %vel_ref.5) | copy-start | bytes 4718596
  3.1 14.5 %collective-permute-start = (f32[2,3,8,128]{3,2,1,0:T(8,128)S(1)}, f32[2,3,8,128]{3,2,1,0:T(8,128)S(1)}, u32[]{:S(2)}, u32[]{:S(2)}) collective-permute-start(f32[2,3,8,128]{3,2,1,0:T(8,128)S(1)} %get-tuple-element.19.z_hi), channel_id=1, source_target_pairs={{0,1},{1,2},{2,3},{3,4},{4,5},{5,6},{6,7},{7,0},{8,9},{9,10},{10,1... | collective-permute-start | bytes 73736 | tf_op jit(solution)/shard_map/ppermute | solution.py:452
  5.6 12.0 %collective-permute-start.1 = (f32[2,3,8,128]{3,2,1,0:T(8,128)S(1)}, f32[2,3,8,128]{3,2,1,0:T(8,128)S(1)}, u32[]{:S(2)}, u32[]{:S(2)}) collective-permute-start(f32[2,3,8,128]{3,2,1,0:T(8,128)S(1)} %get-tuple-element.18.rest_0_.z_lo), channel_id=1, source_target_pairs={{1,0},{2,1},{3,2},{4,3},{5,4},{6,5},{7,6},{0,7},{9,8},{10,9},{11,1... | collective-permute-start | bytes 73736 | tf_op jit(solution)/shard_map/ppermute | solution.py:452
  9.7 1.0 %copy-start.2 = (f32[32,16,256]{2,1,0:T(8,128)S(1)}, f32[32,16,256]{2,1,0:T(8,128)}, u32[]{:S(2)}) copy-start(f32[32,16,256]{2,1,0:T(8,128)} %param.5) | copy-start | bytes 1572868
  10.7 9.8 %copy-start.3 = (f32[32,16,256]{2,1,0:T(8,128)S(1)}, f32[32,16,256]{2,1,0:T(8,128)}, u32[]{:S(2)}) copy-start(f32[32,16,256]{2,1,0:T(8,128)} %param.5) | copy-start | bytes 1572868
  17.7 9.6 %collective-permute-start.2 = (f32[3,80,128]{2,1,0:T(8,128)S(1)}, f32[3,80,128]{2,1,0:T(8,128)S(1)}, u32[]{:S(2)}, u32[]{:S(2)}) collective-permute-start(f32[3,80,128]{2,1,0:T(8,128)S(1)} %get-tuple-element.21), channel_id=1, source_target_pairs={{0,8},{8,16},{16,24},{24,0},{1,9},{9,17},{17,25},{25,1},{2,10},{10... | collective-permute-start | bytes 368648 | tf_op jit(solution)/shard_map/ppermute | solution.py:452
  19.0 8.4 %collective-permute-start.3 = (f32[3,80,128]{2,1,0:T(8,128)S(1)}, f32[3,80,128]{2,1,0:T(8,128)S(1)}, u32[]{:S(2)}, u32[]{:S(2)}) collective-permute-start(f32[3,80,128]{2,1,0:T(8,128)S(1)} %get-tuple-element.22.rest_0_), channel_id=1, source_target_pairs={{8,0},{16,8},{24,16},{0,24},{9,1},{17,9},{25,17},{1,25},{10,2},{18... | collective-permute-start | bytes 368648 | tf_op jit(solution)/shard_map/ppermute | solution.py:452
  27.4 14.8 %collective-permute-start.4 = (f32[3,88,128]{2,1,0:T(8,128)S(1)}, f32[3,88,128]{2,1,0:T(8,128)S(1)}, u32[]{:S(2)}, u32[]{:S(2)}) collective-permute-start(f32[3,88,128]{2,1,0:T(8,128)S(1)} %get-tuple-element.26), channel_id=1, source_target_pairs={{0,32},{32,64},{64,96},{96,128},{128,160},{160,192},{192,224},{224... | collective-permute-start | bytes 405512 | tf_op jit(solution)/shard_map/ppermute | solution.py:452
  30.0 12.2 %collective-permute-start.5 = (f32[3,88,128]{2,1,0:T(8,128)S(1)}, f32[3,88,128]{2,1,0:T(8,128)S(1)}, u32[]{:S(2)}, u32[]{:S(2)}) collective-permute-start(f32[3,88,128]{2,1,0:T(8,128)S(1)} %get-tuple-element.27.rest_0_), channel_id=1, source_target_pairs={{32,0},{64,32},{96,64},{128,96},{160,128},{192,160},{224,192},{0,2... | collective-permute-start | bytes 405512 | tf_op jit(solution)/shard_map/ppermute | solution.py:452

commit v4 on v3

--- a/solution.py
+++ b/solution.py
@@ -13,7 +13,7 @@
 LANES = 128
 PER = 8
 
-CUT, LEVEL, MI, MJ, WENO, CENTRAL, KAPPA, DEPOSIT, PLANES = 6, 8, 5, 4, 16, 8, 16, 6, 4
+CUT, LEVEL, MI, MJ, WENO, CENTRAL, KAPPA, PLANES = 6, 8, 5, 4, 16, 8, 16, 4
 
 box_step = 0.25
 pseudo_step = 0.3
@@ -74,9 +74,9 @@
 
 
 def box_body(first_group, count, owner_ref, corner_ref, vel_ref, level_ref, *rest):
-    (force_out, settled_out, bending_out, *scratch) = rest[-17:]
+    (force_out, turned, turned_kappa, *scratch) = rest[-14:]
     (u_ref, l_ref, mi_ref, mj_ref, pa, pb, c_ref, s_ref, k_ref) = scratch[:9]
-    turned, turned_kappa, levels, sems, level_sems = scratch[9:]
+    levels, level_sems = scratch[9:]
     row, lane = iotas()
     k = lane % BOX
     block = lane // BOX
@@ -101,6 +101,7 @@
             px, py, pz = spots[b]
             turn = (BOX * b + LANES - pz) % LANES
             here = block == b
+            base = px * 32 + py
 
             @pl.loop(0, 6, unroll=CUT)
             def _(step):
@@ -108,7 +109,7 @@
                 i0 = (step % 2) * 8
                 for i in range(8):
                     for jt in range(2):
-                        part = vel_ref[c, px + i0 + i, pl.ds(py + 8 * jt, 8), :]
+                        part = vel_ref[pl.ds(base + c * 1024 + (i0 + i) * 32 + 8 * jt, 8), :]
                         pltpu.store(
                             u_ref.at[c, i0 + i, pl.ds(8 * jt, 8), :],
                             pltpu.roll(part, turn, 1),
@@ -272,9 +273,6 @@
                 y = block_transpose(kappa * alive, row, lane)
                 turned_kappa[pl.ds((own * 2 + jt) * (PER * BOX) + i, 8, stride=BOX), :] = y
 
-        for copy in sent(own):
-            copy.start()
-
     def come(own, jt):
         return pltpu.make_async_copy(
             level_ref.at[
@@ -284,20 +282,6 @@
             level_sems.at[own, jt],
         )
 
-    def sent(own):
-        copies = []
-        for n, (src, dst) in enumerate(((turned, settled_out), (turned_kappa, bending_out))):
-            for jt in range(2):
-                rows = (first_group + own) * (PER * BOX)
-                copies.append(
-                    pltpu.make_async_copy(
-                        src.at[pl.ds((own * 2 + jt) * (PER * BOX), PER * BOX), :],
-                        dst.at[pl.ds(rows, PER * BOX), pl.ds(LANES * jt, LANES)],
-                        sems.at[own, 2 * n + jt],
-                    )
-                )
-        return copies
-
     for own in range(count):
         for jt in range(2):
             come(own, jt).start()
@@ -306,28 +290,19 @@
     def _(own):
         one_group(own)
 
-    for own in range(count):
-        for copy in sent(own):
-            copy.wait()
-
-
-def boxes(first_group, count, owner, corners, velocity, level_rows, after, carried=()):
+
+def boxes(first_group, count, owner, corners, rows, level_rows, after):
     smem = pl.BlockSpec(memory_space=pltpu.SMEM)
+    hbm = pl.BlockSpec(memory_space=pltpu.HBM)
+    vmem = pl.BlockSpec(memory_space=pltpu.VMEM)
     any_ = pl.BlockSpec(memory_space=pl.ANY)
-    vmem = pl.BlockSpec(memory_space=pltpu.VMEM)
     plane = lambda *lead: pltpu.VMEM((*lead, LANES), F32)
-    force = (count, 3, BOX, BOX, LANES)
-    operands = [owner, corners, velocity, level_rows, after, *carried]
+    turned = jax.ShapeDtypeStruct((count * 2 * PER * BOX, LANES), F32)
     return pl.pallas_call(
         functools.partial(box_body, first_group, count),
-        out_shape=(
-            jax.ShapeDtypeStruct(force, F32),
-            jax.ShapeDtypeStruct(level_rows.shape, F32),
-            jax.ShapeDtypeStruct(level_rows.shape, F32),
-        ),
-        in_specs=[smem, smem, vmem, any_, any_] + [any_] * len(carried),
-        out_specs=(vmem, any_, any_),
-        input_output_aliases={5: 1, 6: 2} if carried else {},
+        out_shape=(jax.ShapeDtypeStruct((count, 3, BOX, BOX, LANES), F32), turned, turned),
+        in_specs=[smem, smem, vmem, hbm, any_],
+        out_specs=(vmem,) * 3,
         scratch_shapes=[
             plane(3, BOX, BOX),
             plane(BOX, ROWS),
@@ -339,20 +314,17 @@
             plane(BOX, BOX),
             plane(BOX, BOX),
             plane(count * 2 * PER * BOX),
-            plane(count * 2 * PER * BOX),
-            plane(count * 2 * PER * BOX),
-            pltpu.SemaphoreType.DMA((count, 4)),
             pltpu.SemaphoreType.DMA((count, 2)),
         ],
-        compiler_params=pltpu.CompilerParams(vmem_limit_bytes=20 * 2**20),
+        compiler_params=pltpu.CompilerParams(vmem_limit_bytes=16 * 2**20),
         cost_estimate=pl.CostEstimate(
             flops=30_000_000, bytes_accessed=5_000_000, transcendentals=0
         ),
         name="boxes",
-    )(*operands)
-
-
-def deposit(force_refs, corner_ref, grid_ref):
+    )(owner, corners, rows, level_rows, after)
+
+
+def deposit(force_refs, corner_ref, grid_ref, c):
     _, lane = iotas()
 
     def one_group(ref, own, g):
@@ -360,23 +332,17 @@
             px, py, pz = [corner_ref[g * PER + b, d] for d in range(3)]
             inside = (lane >= pz) & (lane < pz + BOX)
             turn = (pz + LANES - BOX * b) % LANES
-            base = px * 32 + py
-
-            @pl.loop(0, 6, unroll=DEPOSIT)
-            def _(step):
-                c = step // 2
-                i0 = (step % 2) * 8
+            base = c * 1024 + px * 32 + py
+            for i0 in (0, 8):
                 sums = []
                 for i in range(8):
                     for jt in range(2):
-                        old = grid_ref[pl.ds(base + c * 1024 + (i0 + i) * 32 + 8 * jt, 8), :]
+                        old = grid_ref[pl.ds(base + (i0 + i) * 32 + 8 * jt, 8), :]
                         push = pltpu.roll(ref[own, c, i0 + i, pl.ds(8 * jt, 8), :], turn, 1)
                         sums.append(old + jnp.where(inside, push, 0.0))
                 for i in range(8):
                     for jt in range(2):
-                        grid_ref[pl.ds(base + c * 1024 + (i0 + i) * 32 + 8 * jt, 8), :] = sums[
-                            2 * i + jt
-                        ]
+                        grid_ref[pl.ds(base + (i0 + i) * 32 + 8 * jt, 8), :] = sums[2 * i + jt]
 
     done = 0
     for ref in force_refs:
@@ -397,27 +363,26 @@
 X_ROWS = 88
 
 
-def z_faces(rows_ref, lo_ref, hi_ref):
+def z_faces(rows_ref, kept_ref, lo_ref, hi_ref):
     _, lane = iotas()
-
-    def one(x, packed):
-        out = []
-        for c in range(3):
-            parts = packed[4 * c : 4 * c + 4]
+    for c in range(3):
+
+        def one(x, parts):
             for yt in range(4):
                 n = x * 4 + yt
                 at = pl.multiple_of(c * 1024 + x * 32 + 8 * yt, 8)
-                turned = pltpu.roll(rows_ref[pl.ds(at, 8), :], n, 1)
-                parts = [
+                tile = rows_ref[pl.ds(at, 8), :]
+                kept_ref[pl.ds(at, 8), :] = tile
+                turned = pltpu.roll(tile, n, 1)
+                parts = tuple(
                     jnp.where(lane == (n + shift + LANES) % LANES, turned, part)
                     for shift, part in zip((0, 1, -1, -2), parts)
-                ]
-            out += parts
-        return tuple(out)
-
-    packed = lax.fori_loop(0, 32, one, (jnp.zeros(TILE, F32),) * 12, unroll=PLANES)
-    for c in range(3):
-        first, second, last, before = packed[4 * c : 4 * c + 4]
+                )
+            return parts
+
+        first, second, last, before = lax.fori_loop(
+            0, 32, one, (jnp.zeros(TILE, F32),) * 4, unroll=2 * PLANES
+        )
         lo_ref[0, c] = first
         lo_ref[1, c] = pltpu.roll(second, LANES - 1, 1)
         hi_ref[0, c] = pltpu.roll(last, 1, 1)
@@ -511,10 +476,31 @@
 
 
 def momentum_body(
-    vel_ref, z_lo, z_hi, below, above, left, right, front, back, force_a, force_b, force_c,
-    corner_ref, out_ref, ext, later, sides, packed,
+    vel_ref, z_lo, z_hi, below, above, left, right, front, back, *refs,
 ):
+    forces, settled, bending, corner_ref = refs[:3], refs[3:6], refs[6:9], refs[9]
+    new_out, settled_out, bending_out, ext, later, sides, packed, out_ref, sems, grid_sems = refs[10:]
     row, lane = iotas()
+
+    leaving = []
+    for n, (parts, out) in enumerate(((settled, settled_out), (bending, bending_out))):
+        group = 0
+        for part in parts:
+            for own in range(part.shape[0] // (2 * PER * BOX)):
+                for jt in range(2):
+                    leaving.append(
+                        pltpu.make_async_copy(
+                            part.at[pl.ds((own * 2 + jt) * (PER * BOX), PER * BOX), :],
+                            out.at[
+                                pl.ds(group * (PER * BOX), PER * BOX), pl.ds(LANES * jt, LANES)
+                            ],
+                            sems.at[n, group, jt],
+                        )
+                    )
+                group += 1
+    for copy in leaving:
+        copy.start()
+
     for c in range(3):
         base = c * 36 * PLANE
         for plane, halo, layer in ((1, front, 0), (0, front, 1), (34, back, 0), (35, back, 1)):
@@ -603,58 +589,73 @@
                 at = pl.ds(pl.multiple_of(c * 1024 + x * 32 + 8 * yt, 8), 8)
                 out_ref[at, :] = 0.5 * (vel_ref[at, :] + new[c])
 
-    deposit((force_a, force_b, force_c), corner_ref, out_ref)
-
-
-def call(body, out_shape, operands, name, unread=0, corners=None, scratch=(), limit=16):
+    for c in range(3):
+        deposit(forces, corner_ref, out_ref, c)
+        at = pl.ds(c * 1024, 1024)
+        leaving.append(
+            pltpu.make_async_copy(out_ref.at[at, :], new_out.at[at, :], grid_sems.at[c])
+        )
+        leaving[-1].start()
+    for copy in leaving:
+        copy.wait()
+
+
+def call(body, out_shape, operands, name, unread=0):
     vmem = pl.BlockSpec(memory_space=pltpu.VMEM)
     specs = [vmem] * (len(operands) - unread) + [pl.BlockSpec(memory_space=pl.ANY)] * unread
-    if corners is not None:
-        operands = [*operands, corners]
-        specs.append(pl.BlockSpec(memory_space=pltpu.SMEM))
     return pl.pallas_call(
         body,
         out_shape=out_shape,
         in_specs=specs,
         out_specs=jax.tree.map(lambda _: vmem, out_shape),
-        scratch_shapes=scratch,
-        compiler_params=pltpu.CompilerParams(vmem_limit_bytes=limit * 2**20),
+        compiler_params=pltpu.CompilerParams(vmem_limit_bytes=8 * 2**20),
         name=name,
     )(*operands)
 
 
 def local(velocity, box_level, corners, owner_list):
     slots = box_level.shape[0]
+    level_rows = box_level.reshape(slots * BOX, BOX * BOX)
     rows = velocity.reshape(-1, LANES)
-    level_rows = box_level.reshape(slots * BOX, BOX * BOX)
-    work = functools.partial(boxes, owner=owner_list, corners=corners, velocity=velocity, level_rows=level_rows)
-    z_lo, z_hi = call(z_faces, (PACKED,) * 2, [rows], "z_faces")
+    kept = jax.ShapeDtypeStruct(rows.shape, F32)
+    rows, z_lo, z_hi = call(z_faces, (kept, PACKED, PACKED), [rows], "z_faces")
     below, above = exchange(z_lo, z_hi, "gz")
-    force_a, *done = work(0, 1, after=z_lo)
+    work = functools.partial(
+        boxes, owner=owner_list, corners=corners, rows=rows, level_rows=level_rows
+    )
+    first = work(0, 1, after=z_lo)
     sent = jax.ShapeDtypeStruct((3, Y_ROWS, LANES), F32)
-    faces = call(y_faces, (sent,) * 2, [rows, below, above, force_a], "y_faces", unread=1)
+    faces = call(y_faces, (sent,) * 2, [rows, below, above, first[0]], "y_faces", unread=1)
     left, right = exchange(*faces, "gy")
-    force_b, *done = work(1, 1, after=faces[0], carried=done)
+    second = work(1, 1, after=faces[0])
     sent = jax.ShapeDtypeStruct((3, X_ROWS, LANES), F32)
     faces = call(
-        x_faces, (sent,) * 2, [rows, below, above, left, right, force_b], "x_faces", unread=1
+        x_faces, (sent,) * 2, [rows, below, above, left, right, second[0]], "x_faces", unread=1
     )
     front, back = exchange(*faces, "gx")
-    force_c, settled, bending = work(2, slots // PER - 2, after=faces[0], carried=done)
-    result = call(
+    third = work(2, slots // PER - 2, after=faces[0])
+    parts = [part for kind in zip(first, second, third) for part in kind]
+    operands = [rows, z_lo, z_hi, below, above, left, right, front, back, *parts]
+    hbm = pl.BlockSpec(memory_space=pltpu.HBM)
+    boxed = jax.ShapeDtypeStruct(level_rows.shape, F32)
+    result, settled, bending = pl.pallas_call(
         momentum_body,
-        jax.ShapeDtypeStruct(rows.shape, F32),
-        [rows, z_lo, z_hi, below, above, left, right, front, back, force_a, force_b, force_c],
-        "momentum",
-        corners=corners,
-        scratch=[
+        out_shape=(jax.ShapeDtypeStruct(rows.shape, F32), boxed, boxed),
+        in_specs=[pl.BlockSpec(memory_space=pltpu.VMEM)] * len(operands)
+        + [pl.BlockSpec(memory_space=pltpu.SMEM)],
+        out_specs=(hbm,) * 3,
+        scratch_shapes=[
             pltpu.VMEM((3 * 36 * PLANE, LANES), F32),
             pltpu.VMEM((3 * 34 * PLANE, LANES), F32),
             pltpu.VMEM((3, PLANE, LANES), F32),
             pltpu.VMEM((2, 3, 8, LANES), F32),
+            pltpu.VMEM(rows.shape, F32),
+            pltpu.SemaphoreType.DMA((2, slots // PER, 2)),
+            pltpu.SemaphoreType.DMA((3,)),
         ],
-        limit=32,
-    )
+        compiler_params=pltpu.CompilerParams(vmem_limit_bytes=24 * 2**20),
+        name="momentum",
+    )(*operands, corners)
     return (
         result.reshape(velocity.shape),
         settled.reshape(box_level.shape),

time: 52.9 us -> 51.7 us (0.977)
  local copies, waits for them, and re-layouts: 2.55 us -> 1.56 us
    pallas_call x0 -> x1, Pallas kernels: none -> 10.9 us  [local(): pl.pallas_call(momentum_body, out_shape=(jax.ShapeDtypeStruct(rows.shape,...]
    pallas_call x4 -> x3, Pallas kernels: 11.8 us -> 2.56 us  [call(): pl.pallas_call(body, out_shape=out_shape, in_specs=specs, out_specs=jax.t...]
    pallas_call x3, Pallas kernels: 25.7 us -> 23.6 us  [boxes(): pl.pallas_call(functools.partial(box_body, first_group, count), out_shape...]
    unnamed x13 -> x9, local copies, waits for them, and re-layouts: 2.55 us -> 1.56 us
  transfers between devices with their start and end apart: 6 -> 6, of which waited for: 0 -> 0; matrix products, arithmetic and copies ran while one was open for 0% -> 0% of each run, Pallas kernels for 49% -> 46%
where the time goes in v4:
time: 51.7 us; the launch traced here: 51.6 us
  Pallas kernels  37.1 us (72%)
  starting transfers between devices  12 us (23%)
  local copies, waits for them, and re-layouts  1.56 us (3%)
  between operations  0.9 us (2%)
    pallas_call x3, Pallas kernels, boxes(): pl.pallas_call(functools.partial(box_body, first_group, count), out_shape...  23.6 us
    ppermute x6, starting transfers between devices, exchange(): return (lax.ppermute(hi, axis, up), lax.ppermute(lo, axis, down))  12 us
    pallas_call x1, Pallas kernels, local(): pl.pallas_call(momentum_body, out_shape=(jax.ShapeDtypeStruct(rows.shape,...  10.9 us
    pallas_call x3, Pallas kernels, call(): pl.pallas_call(body, out_shape=out_shape, in_specs=specs, out_specs=jax.t...  2.56 us
    unnamed x9, local copies, waits for them, and re-layouts  1.56 us
  transfers between devices with their start and end apart: 6, of which 0 were waited for; matrix products, arithmetic and copies ran while one was open for 0% of the time, Pallas kernels for 46%

profile of v4, /device:TPU:1, one launch (start us, length us, event | category | flops | bytes accessed | tf_op | source)
XLA Modules:
  0.0 51.6 jit_solution(9275558643285776032)
XLA Ops:
  0.6 0.0 copy-start
  0.6 0.0 copy-start.1
  0.7 1.5 %copy-done.1 = f32[3,32,32,128]{3,2,1,0:T(8,128)S(1)} copy-done((f32[3,32,32,128]{3,2,1,0:T(8,128)S(1)}, f32[3,32,32,128]{3,2,1,0:T(8,128)}, u32[]{:S(2)}) %copy-start.1) | copy-done | bytes 1572888
  2.1 0.0 copy-start.3
  2.1 0.0 copy-start.2
  2.1 2.4 %z_faces.1 = (f32[3072,128]{1,0:T(8,128)S(1)}, f32[2,3,8,128]{3,2,1,0:T(8,128)S(1)}, f32[2,3,8,128]{3,2,1,0:T(8,128)S(1)}) custom-call(f32[3072,128]{1,0:T(8,128)S(1)} %bitcast.8), custom_call_target="tpu_custom_call" | custom-call | tf_op jit(solution)/shard_map/z_faces/pallas_call | solution.py:606
  4.5 2.5 %collective-permute-start = (f32[2,3,8,128]{3,2,1,0:T(8,128)S(1)}, f32[2,3,8,128]{3,2,1,0:T(8,128)S(1)}, u32[]{:S(2)}, u32[]{:S(2)}) collective-permute-start(f32[2,3,8,128]{3,2,1,0:T(8,128)S(1)} %get-tuple-element.24.z_hi), channel_id=1, source_target_pairs={{0,1},{1,2},{2,3},{3,4},{4,5},{5,6},{6,7},{7,0},{8,9},{9,10},{10,1... | collective-permute-start | bytes 73736 | tf_op jit(solution)/shard_map/ppermute | solution.py:417
  7.0 4.0 %collective-permute-start.1 = (f32[2,3,8,128]{3,2,1,0:T(8,128)S(1)}, f32[2,3,8,128]{3,2,1,0:T(8,128)S(1)}, u32[]{:S(2)}, u32[]{:S(2)}) collective-permute-start(f32[2,3,8,128]{3,2,1,0:T(8,128)S(1)} %get-tuple-element.23.rest_0_.z_lo), channel_id=1, source_target_pairs={{1,0},{2,1},{3,2},{4,3},{5,4},{6,5},{7,6},{0,7},{9,8},{10,9},{11,1... | collective-permute-start | bytes 73736 | tf_op jit(solution)/shard_map/ppermute | solution.py:417
  11.0 0.0 copy-done.3
  11.0 0.1 copy.7.corner_ref.refs_9_
  11.1 0.0 copy-done
  11.1 0.0 copy-done.2
  11.1 6.1 %boxes.3 = (f32[1,3,16,16,128]{4,3,2,1,0:T(8,128)S(1)}, f32[256,128]{1,0:T(8,128)S(1)}, f32[256,128]{1,0:T(8,128)S(1)}) custom-call(s32[32]{0:T(128)S(1)} %copy-done.2, s32[32,3]{1,0:T(8,128)S(1)} %copy.7.corner_ref.refs_9_, f32[3072,128]{1,0:T(8,128)S(1)} %get-tuple-element.22.vel_ref.rows_ref, f32[512,256]{1,0:T(8,128)S(1)} %bitcast.5, ...), custom_call_target="tpu_custom_call" | custom-call | flops 30000000 | bytes 5000000 | tf_op jit(solution)/shard_map/boxes/pallas_call | solution.py:301
  17.3 0.0 collective-permute-done.below_ref.below
  17.3 0.0 collective-permute-done.1.above_ref.above
  17.3 0.1 y_faces.1
  17.4 1.3 %collective-permute-start.2 = (f32[3,80,128]{2,1,0:T(8,128)S(1)}, f32[3,80,128]{2,1,0:T(8,128)S(1)}, u32[]{:S(2)}, u32[]{:S(2)}) collective-permute-start(f32[3,80,128]{2,1,0:T(8,128)S(1)} %get-tuple-element.26), channel_id=1, source_target_pairs={{0,8},{8,16},{16,24},{24,0},{1,9},{9,17},{17,25},{25,1},{2,10},{10... | collective-permute-start | bytes 368648 | tf_op jit(solution)/shard_map/ppermute | solution.py:417
  18.7 1.5 %collective-permute-start.3 = (f32[3,80,128]{2,1,0:T(8,128)S(1)}, f32[3,80,128]{2,1,0:T(8,128)S(1)}, u32[]{:S(2)}, u32[]{:S(2)}) collective-permute-start(f32[3,80,128]{2,1,0:T(8,128)S(1)} %get-tuple-element.27.rest_0_), channel_id=1, source_target_pairs={{8,0},{16,8},{24,16},{0,24},{9,1},{17,9},{25,17},{1,25},{10,2},{18... | collective-permute-start | bytes 368648 | tf_op jit(solution)/shard_map/ppermute | solution.py:417
  20.2 6.1 %boxes.4 = (f32[1,3,16,16,128]{4,3,2,1,0:T(8,128)S(1)}, f32[256,128]{1,0:T(8,128)S(1)}, f32[256,128]{1,0:T(8,128)S(1)}) custom-call(s32[32]{0:T(128)S(1)} %copy-done.2, s32[32,3]{1,0:T(8,128)S(1)} %copy.7.corner_ref.refs_9_, f32[3072,128]{1,0:T(8,128)S(1)} %get-tuple-element.22.vel_ref.rows_ref, f32[512,256]{1,0:T(8,128)S(1)} %bitcast.6, ...), custom_call_target="tpu_custom_call" | custom-call | flops 30000000 | bytes 5000000 | tf_op jit(solution)/shard_map/boxes/pallas_call | solution.py:301
  26.4 0.0 collective-permute-done.2.left_ref.left
  26.4 0.0 collective-permute-done.3.right_ref.right
  26.4 2.6 %collective-permute-start.4 = (f32[3,88,128]{2,1,0:T(8,128)S(1)}, f32[3,88,128]{2,1,0:T(8,128)S(1)}, u32[]{:S(2)}, u32[]{:S(2)}) collective-permute-start(f32[3,88,128]{2,1,0:T(8,128)S(1)} %get-tuple-element.29), channel_id=1, source_target_pairs={{0,32},{32,64},{64,96},{96,128},{128,160},{160,192},{192,224},{224... | collective-permute-start | bytes 405512 | tf_op jit(solution)/shard_map/ppermute | solution.py:417
  29.0 0.0 collective-permute-start.5
  29.0 11.4 %boxes.5 = (f32[2,3,16,16,128]{4,3,2,1,0:T(8,128)S(1)}, f32[512,128]{1,0:T(8,128)S(1)}, f32[512,128]{1,0:T(8,128)S(1)}) custom-call(s32[32]{0:T(128)S(1)} %copy-done.2, s32[32,3]{1,0:T(8,128)S(1)} %copy.7.corner_ref.refs_9_, f32[3072,128]{1,0:T(8,128)S(1)} %get-tuple-element.22.vel_ref.rows_ref, f32[512,256]{1,0:T(8,128)S(1)} %bitcast.7, ...), custom_call_target="tpu_custom_call" | custom-call | flops 30000000 | bytes 5000000 | tf_op jit(solution)/shard_map/boxes/pallas_call | solution.py:301
  40.5 0.0 collective-permute-done.4.front
  40.5 0.0 collective-permute-done.5.back
  40.5 10.9 %momentum.1 = (f32[3072,128]{1,0:T(8,128)}, f32[512,256]{1,0:T(8,128)}, f32[512,256]{1,0:T(8,128)}) custom-call(f32[3072,128]{1,0:T(8,128)S(1)} %get-tuple-element.22.vel_ref.rows_ref, f32[2,3,8,128]{3,2,1,0:T(8,128)S(1)} %get-tuple-element.23.rest_0_.z_lo, f32[2,3,8,128]{3,2,1,0:T(8,128)S(1)} %get-tuple-element.24.z_hi, ...), custom_call_target="tpu_custom_call" | custom-call | tf_op jit(solution)/shard_map/momentum/pallas_call | solution.py:641
  (1 shorter events, 0.0 us)
Async XLA Ops:
  0.6 10.5 %copy-start = (f32[32,16,256]{2,1,0:T(8,128)S(1)}, f32[32,16,256]{2,1,0:T(8,128)}, u32[]{:S(2)}) copy-start(f32[32,16,256]{2,1,0:T(8,128)} %param.5) | copy-start | bytes 1572868
  0.6 1.5 %copy-start.1 = (f32[3,32,32,128]{3,2,1,0:T(8,128)S(1)}, f32[3,32,32,128]{3,2,1,0:T(8,128)}, u32[]{:S(2)}) copy-start(f32[3,32,32,128]{3,2,1,0:T(8,128)} %param.4) | copy-start | bytes 4718596
  2.1 8.9 %copy-start.3 = (s32[32,3]{0,1:T(4,128)S(1)}, s32[32,3]{0,1:T(4,128)}, u32[]{:S(2)}) copy-start(s32[32,3]{0,1:T(4,128)} %param.6) | copy-start | bytes 1156
  2.1 9.0 %copy-start.2 = (s32[32]{0:T(128)S(1)}, s32[32]{0:T(128)}, u32[]{:S(2)}) copy-start(s32[32]{0:T(128)} %owner_ref.5) | copy-start | bytes 388
  4.5 12.7 %collective-permute-start = (f32[2,3,8,128]{3,2,1,0:T(8,128)S(1)}, f32[2,3,8,128]{3,2,1,0:T(8,128)S(1)}, u32[]{:S(2)}, u32[]{:S(2)}) collective-permute-start(f32[2,3,8,128]{3,2,1,0:T(8,128)S(1)} %get-tuple-element.24.z_hi), channel_id=1, source_target_pairs={{0,1},{1,2},{2,3},{3,4},{4,5},{5,6},{6,7},{7,0},{8,9},{9,10},{10,1... | collective-permute-start | bytes 73736 | tf_op jit(solution)/shard_map/ppermute | solution.py:417
  7.0 10.3 %collective-permute-start.1 = (f32[2,3,8,128]{3,2,1,0:T(8,128)S(1)}, f32[2,3,8,128]{3,2,1,0:T(8,128)S(1)}, u32[]{:S(2)}, u32[]{:S(2)}) collective-permute-start(f32[2,3,8,128]{3,2,1,0:T(8,128)S(1)} %get-tuple-element.23.rest_0_.z_lo), channel_id=1, source_target_pairs={{1,0},{2,1},{3,2},{4,3},{5,4},{6,5},{7,6},{0,7},{9,8},{10,9},{11,1... | collective-permute-start | bytes 73736 | tf_op jit(solution)/shard_map/ppermute | solution.py:417
  17.4 8.9 %collective-permute-start.2 = (f32[3,80,128]{2,1,0:T(8,128)S(1)}, f32[3,80,128]{2,1,0:T(8,128)S(1)}, u32[]{:S(2)}, u32[]{:S(2)}) collective-permute-start(f32[3,80,128]{2,1,0:T(8,128)S(1)} %get-tuple-element.26), channel_id=1, source_target_pairs={{0,8},{8,16},{16,24},{24,0},{1,9},{9,17},{17,25},{25,1},{2,10},{10... | collective-permute-start | bytes 368648 | tf_op jit(solution)/shard_map/ppermute | solution.py:417
  18.7 7.7 %collective-permute-start.3 = (f32[3,80,128]{2,1,0:T(8,128)S(1)}, f32[3,80,128]{2,1,0:T(8,128)S(1)}, u32[]{:S(2)}, u32[]{:S(2)}) collective-permute-start(f32[3,80,128]{2,1,0:T(8,128)S(1)} %get-tuple-element.27.rest_0_), channel_id=1, source_target_pairs={{8,0},{16,8},{24,16},{0,24},{9,1},{17,9},{25,17},{1,25},{10,2},{18... | collective-permute-start | bytes 368648 | tf_op jit(solution)/shard_map/ppermute | solution.py:417
  26.4 14.1 %collective-permute-start.4 = (f32[3,88,128]{2,1,0:T(8,128)S(1)}, f32[3,88,128]{2,1,0:T(8,128)S(1)}, u32[]{:S(2)}, u32[]{:S(2)}) collective-permute-start(f32[3,88,128]{2,1,0:T(8,128)S(1)} %get-tuple-element.29), channel_id=1, source_target_pairs={{0,32},{32,64},{64,96},{96,128},{128,160},{160,192},{192,224},{224... | collective-permute-start | bytes 405512 | tf_op jit(solution)/shard_map/ppermute | solution.py:417
  29.0 11.4 %collective-permute-start.5 = (f32[3,88,128]{2,1,0:T(8,128)S(1)}, f32[3,88,128]{2,1,0:T(8,128)S(1)}, u32[]{:S(2)}, u32[]{:S(2)}) collective-permute-start(f32[3,88,128]{2,1,0:T(8,128)S(1)} %get-tuple-element.30.rest_0_), channel_id=1, source_target_pairs={{32,0},{64,32},{96,64},{128,96},{160,128},{192,160},{224,192},{0,2... | collective-permute-start | bytes 405512 | tf_op jit(solution)/shard_map/ppermute | solution.py:417

commit v5 on v4

--- a/solution.py
+++ b/solution.py
@@ -13,7 +13,7 @@
 LANES = 128
 PER = 8
 
-CUT, LEVEL, MI, MJ, WENO, CENTRAL, KAPPA, PLANES = 6, 8, 5, 4, 16, 8, 16, 4
+CUT, LEVEL, MI, MJ, WENO, CENTRAL, KAPPA, PLANES = 6, 8, 5, 4, 16, 8, 16, 8
 
 box_step = 0.25
 pseudo_step = 0.3
@@ -187,33 +187,28 @@
                 for i in range(BOX):
                     s = s_ref[i, at, :]
                     terms = []
+                    sc = s * cur
                     if i < BOX - 1:
                         nxt = src[i + 1, pl.ds(8 + 8 * jt, 8), :]
-                        down_i = cur - nxt
+                        sides = s * nxt if behind_i is None else jnp.minimum(s * nxt, s * behind_i)
                     else:
-                        nxt = down_i = None
-                    if behind_i is None:
-                        terms.append(jnp.maximum(s * down_i, 0.0))
-                    elif down_i is None:
-                        terms.append(jnp.maximum(-(s * behind_i), 0.0))
+                        nxt = None
+                        sides = s * behind_i
+                    terms.append(sc - jnp.minimum(sides, sc))
+                    lower = src[i, pl.ds(7 + 8 * jt, 8), :]
+                    upper = src[i, pl.ds(9 + 8 * jt, 8), :]
+                    if jt == 0:
+                        lower = jnp.where(top, cur, lower)
                     else:
-                        terms.append(
-                            jnp.maximum(jnp.maximum(s * down_i, -(s * behind_i)), 0.0)
-                        )
-                    below = cur - src[i, pl.ds(7 + 8 * jt, 8), :]
-                    above = cur - src[i, pl.ds(9 + 8 * jt, 8), :]
-                    if jt == 0:
-                        below = jnp.where(top, 0.0, below)
-                    else:
-                        above = jnp.where(bottom, 0.0, above)
-                    terms.append(jnp.maximum(jnp.maximum(s * below, s * above), 0.0))
-                    down_k = jnp.where(k_last, 0.0, cur - pltpu.roll(cur, LANES - 1, 1))
-                    up_k = pltpu.roll(down_k, 1, 1)
-                    terms.append(jnp.maximum(jnp.maximum(s * down_k, -(s * up_k)), 0.0))
+                        upper = jnp.where(bottom, cur, upper)
+                    terms.append(sc - jnp.minimum(jnp.minimum(s * lower, s * upper), sc))
+                    lower = jnp.where(k_first, cur, pltpu.roll(cur, 1, 1))
+                    upper = jnp.where(k_last, cur, pltpu.roll(cur, LANES - 1, 1))
+                    terms.append(sc - jnp.minimum(jnp.minimum(s * lower, s * upper), sc))
                     squared = terms[0] * terms[0] + terms[1] * terms[1] + terms[2] * terms[2]
                     root = squared * lax.rsqrt(jnp.maximum(squared, 1e-37))
                     dst[i, pl.ds(8 + 8 * jt, 8), :] = cur - c_ref[i, at, :] * (root - 1.0)
-                    behind_i, cur = down_i, nxt
+                    behind_i, cur = cur, nxt
 
         @pl.loop(0, ITERS // 2)
         def _(_):
@@ -363,58 +358,74 @@
 X_ROWS = 88
 
 
-def z_faces(rows_ref, kept_ref, lo_ref, hi_ref):
+def z_faces(rows_ref, kept_ref, near_ref, far_ref):
     _, lane = iotas()
-    for c in range(3):
-
-        def one(x, parts):
+    even = is_even("gz")
+
+    def one(x, packed):
+        out = []
+        for c in range(3):
+            parts = packed[4 * c : 4 * c + 4]
             for yt in range(4):
                 n = x * 4 + yt
                 at = pl.multiple_of(c * 1024 + x * 32 + 8 * yt, 8)
                 tile = rows_ref[pl.ds(at, 8), :]
                 kept_ref[pl.ds(at, 8), :] = tile
                 turned = pltpu.roll(tile, n, 1)
-                parts = tuple(
+                parts = [
                     jnp.where(lane == (n + shift + LANES) % LANES, turned, part)
                     for shift, part in zip((0, 1, -1, -2), parts)
-                )
-            return parts
-
-        first, second, last, before = lax.fori_loop(
-            0, 32, one, (jnp.zeros(TILE, F32),) * 4, unroll=2 * PLANES
-        )
-        lo_ref[0, c] = first
-        lo_ref[1, c] = pltpu.roll(second, LANES - 1, 1)
-        hi_ref[0, c] = pltpu.roll(last, 1, 1)
-        hi_ref[1, c] = pltpu.roll(before, 2, 1)
-
-
-def y_faces(rows_ref, below_ref, above_ref, _, lo_ref, hi_ref):
+                ]
+            out += parts
+        return tuple(out)
+
+    packed = lax.fori_loop(0, 32, one, (jnp.zeros(TILE, F32),) * 12, unroll=PLANES)
     for c in range(3):
-        for out, layers in ((lo_ref, (0, 1)), (hi_ref, (31, 30))):
-            for n, y in enumerate(layers):
+        first, second, last, before = packed[4 * c : 4 * c + 4]
+        lower = (first, pltpu.roll(second, LANES - 1, 1))
+        upper = (pltpu.roll(last, 1, 1), pltpu.roll(before, 2, 1))
+        for layer in range(2):
+            near_ref[layer, c] = jnp.where(even, upper[layer], lower[layer])
+            far_ref[layer, c] = jnp.where(even, lower[layer], upper[layer])
+
+
+def y_faces(rows_ref, z_near, z_far, _, near_ref, far_ref):
+    even, z_even = is_even("gy"), is_even("gz")
+    for out, upper in ((near_ref, even), (far_ref, jnp.logical_not(even))):
+        for c in range(3):
+            for n in range(2):
+                y = jnp.where(upper, 31 - n, n)
                 out[c, pl.ds(32 * n, 32), :] = rows_ref[pl.ds(c * 1024 + y, 32, stride=32), :]
-            out[c, pl.ds(64, 8), :] = below_ref[0, c]
-            out[c, pl.ds(72, 8), :] = above_ref[0, c]
-
-
-def x_faces(rows_ref, below_ref, above_ref, left_ref, right_ref, _, lo_ref, hi_ref):
-    for c in range(3):
-        for out, layers in ((lo_ref, (0, 1)), (hi_ref, (31, 30))):
-            for n, x in enumerate(layers):
-                out[c, pl.ds(32 * n, 32), :] = rows_ref[pl.ds(c * 1024 + 32 * x, 32), :]
+            out[c, pl.ds(64, 8), :] = jnp.where(z_even, z_far[0, c], z_near[0, c])
+            out[c, pl.ds(72, 8), :] = jnp.where(z_even, z_near[0, c], z_far[0, c])
+
+
+def x_faces(rows_ref, z_near, z_far, y_near, y_far, _, near_ref, far_ref):
+    even, y_even, z_even = is_even("gx"), is_even("gy"), is_even("gz")
+    for out, upper in ((near_ref, even), (far_ref, jnp.logical_not(even))):
+        for c in range(3):
+            for n in range(2):
+                x = jnp.where(upper, 31 - n, n)
+                at = pl.multiple_of(c * 1024 + 32 * x, 8)
+                out[c, pl.ds(32 * n, 32), :] = rows_ref[pl.ds(at, 32), :]
+            x = jnp.where(upper, 31, 0)
+            near, far = y_near[c, pl.ds(x, 1), :], y_far[c, pl.ds(x, 1), :]
             out[c, pl.ds(64, 8), :] = jnp.zeros(TILE, F32)
-            out[c, pl.ds(64, 1), :] = left_ref[c, pl.ds(layers[0], 1), :]
-            out[c, pl.ds(65, 1), :] = right_ref[c, pl.ds(layers[0], 1), :]
-            out[c, pl.ds(72, 8), :] = below_ref[0, c]
-            out[c, pl.ds(80, 8), :] = above_ref[0, c]
-
-
-def exchange(lo, hi, axis):
+            out[c, pl.ds(64, 1), :] = jnp.where(y_even, far, near)
+            out[c, pl.ds(65, 1), :] = jnp.where(y_even, near, far)
+            out[c, pl.ds(72, 8), :] = jnp.where(z_even, z_far[0, c], z_near[0, c])
+            out[c, pl.ds(80, 8), :] = jnp.where(z_even, z_near[0, c], z_far[0, c])
+
+
+def exchange(first, second, axis):
     size = lax.axis_size(axis)
-    up = [(i, (i + 1) % size) for i in range(size)]
-    down = [(j, i) for i, j in up]
-    return lax.ppermute(hi, axis, up), lax.ppermute(lo, axis, down)
+    near = [(i, i ^ 1) for i in range(size)]
+    far = [(i, (i + 1) % size if i % 2 else (i - 1) % size) for i in range(size)]
+    return lax.ppermute(first, axis, near), lax.ppermute(second, axis, far)
+
+
+def is_even(axis):
+    return lax.axis_index(axis) % 2 == 0
 
 
 def slopes_to_f(centre, v, lower, upper):
@@ -476,11 +487,25 @@
 
 
 def momentum_body(
-    vel_ref, z_lo, z_hi, below, above, left, right, front, back, *refs,
+    vel_ref, face_near, face_far, z_near, z_far, y_near, y_far, x_near, x_far, *refs,
 ):
     forces, settled, bending, corner_ref = refs[:3], refs[3:6], refs[6:9], refs[9]
-    new_out, settled_out, bending_out, ext, later, sides, packed, out_ref, sems, grid_sems = refs[10:]
+    new_out, settled_out, bending_out, ext, later, sides, packed, out_ref, sems, grid_sems = refs[10:20]
+    own_faces, z_halos, y_halos, x_halos = refs[20:]
     row, lane = iotas()
+    for axis, kept, near, far in (
+        ("gz", own_faces, face_near, face_far),
+        ("gz", z_halos, z_near, z_far),
+        ("gy", y_halos, y_near, y_far),
+        ("gx", x_halos, x_near, x_far),
+    ):
+        upper = jnp.where(is_even(axis), 1, 0)
+        kept[upper] = near[...]
+        kept[1 - upper] = far[...]
+    z_lo, z_hi = own_faces.at[0], own_faces.at[1]
+    below, above = z_halos.at[0], z_halos.at[1]
+    left, right = y_halos.at[0], y_halos.at[1]
+    front, back = x_halos.at[0], x_halos.at[1]
 
     leaving = []
     for n, (parts, out) in enumerate(((settled, settled_out), (bending, bending_out))):
@@ -618,24 +643,24 @@
     level_rows = box_level.reshape(slots * BOX, BOX * BOX)
     rows = velocity.reshape(-1, LANES)
     kept = jax.ShapeDtypeStruct(rows.shape, F32)
-    rows, z_lo, z_hi = call(z_faces, (kept, PACKED, PACKED), [rows], "z_faces")
-    below, above = exchange(z_lo, z_hi, "gz")
+    rows, *z_own = call(z_faces, (kept, PACKED, PACKED), [rows], "z_faces")
+    z_halos = exchange(*z_own, "gz")
     work = functools.partial(
         boxes, owner=owner_list, corners=corners, rows=rows, level_rows=level_rows
     )
-    first = work(0, 1, after=z_lo)
+    first = work(0, 1, after=z_own[0])
     sent = jax.ShapeDtypeStruct((3, Y_ROWS, LANES), F32)
-    faces = call(y_faces, (sent,) * 2, [rows, below, above, first[0]], "y_faces", unread=1)
-    left, right = exchange(*faces, "gy")
+    faces = call(y_faces, (sent,) * 2, [rows, *z_halos, first[0]], "y_faces", unread=1)
+    y_halos = exchange(*faces, "gy")
     second = work(1, 1, after=faces[0])
     sent = jax.ShapeDtypeStruct((3, X_ROWS, LANES), F32)
     faces = call(
-        x_faces, (sent,) * 2, [rows, below, above, left, right, second[0]], "x_faces", unread=1
+        x_faces, (sent,) * 2, [rows, *z_halos, *y_halos, second[0]], "x_faces", unread=1
     )
-    front, back = exchange(*faces, "gx")
+    x_halos = exchange(*faces, "gx")
     third = work(2, slots // PER - 2, after=faces[0])
     parts = [part for kind in zip(first, second, third) for part in kind]
-    operands = [rows, z_lo, z_hi, below, above, left, right, front, back, *parts]
+    operands = [rows, *z_own, *z_halos, *y_halos, *x_halos, *parts]
     hbm = pl.BlockSpec(memory_space=pltpu.HBM)
     boxed = jax.ShapeDtypeStruct(level_rows.shape, F32)
     result, settled, bending = pl.pallas_call(
@@ -652,6 +677,10 @@
             pltpu.VMEM(rows.shape, F32),
             pltpu.SemaphoreType.DMA((2, slots // PER, 2)),
             pltpu.SemaphoreType.DMA((3,)),
+            pltpu.VMEM((2, *PACKED.shape), F32),
+            pltpu.VMEM((2, *PACKED.shape), F32),
+            pltpu.VMEM((2, 3, Y_ROWS, LANES), F32),
+            pltpu.VMEM((2, 3, X_ROWS, LANES), F32),
         ],
         compiler_params=pltpu.CompilerParams(vmem_limit_bytes=24 * 2**20),
         name="momentum",

time: 51.7 us -> 47.4 us (0.917)
  Pallas kernels: 37.1 us -> 32.6 us
    pallas_call x3, Pallas kernels: 23.6 us -> 21.1 us  [boxes(): pl.pallas_call(functools.partial(box_body, first_group, count), out_shape...]
    pallas_call x3, Pallas kernels: 2.56 us -> 1.1 us  [call(): pl.pallas_call(body, out_shape=out_shape, in_specs=specs, out_specs=jax.t...]
    pallas_call x1, Pallas kernels: 10.9 us -> 10.4 us  [local(): pl.pallas_call(momentum_body, out_shape=(jax.ShapeDtypeStruct(rows.shape,...]
  transfers between devices with their start and end apart: 6 -> 6, of which waited for: 0 -> 0; matrix products, arithmetic and copies ran while one was open for 0% -> 0% of each run, Pallas kernels for 46% -> 45%
where the time goes in v5:
time: 47.4 us; the launch traced here: 47.3 us
  Pallas kernels  32.6 us (69%)
  starting transfers between devices  12.3 us (26%)
  local copies, waits for them, and re-layouts  1.56 us (3%)
  between operations  0.9 us (2%)
    pallas_call x3, Pallas kernels, boxes(): pl.pallas_call(functools.partial(box_body, first_group, count), out_shape...  21.1 us
    ppermute x6, starting transfers between devices, exchange(): return (lax.ppermute(first, axis, near), lax.ppermute(second, axis, far))  12.3 us
    pallas_call x1, Pallas kernels, local(): pl.pallas_call(momentum_body, out_shape=(jax.ShapeDtypeStruct(rows.shape,...  10.4 us
    unnamed x9, local copies, waits for them, and re-layouts  1.56 us
    pallas_call x3, Pallas kernels, call(): pl.pallas_call(body, out_shape=out_shape, in_specs=specs, out_specs=jax.t...  1.1 us
  transfers between devices with their start and end apart: 6, of which 0 were waited for; matrix products, arithmetic and copies ran while one was open for 0% of the time, Pallas kernels for 45%

profile of v5, /device:TPU:1, one launch (start us, length us, event | category | flops | bytes accessed | tf_op | source)
XLA Modules:
  0.0 47.3 jit_solution(6476273814420086078)
XLA Ops:
  0.6 0.0 copy-start
  0.6 0.0 copy-start.1
  0.7 1.5 %copy-done.1 = f32[3,32,32,128]{3,2,1,0:T(8,128)S(1)} copy-done((f32[3,32,32,128]{3,2,1,0:T(8,128)S(1)}, f32[3,32,32,128]{3,2,1,0:T(8,128)}, u32[]{:S(2)}) %copy-start.1) | copy-done | bytes 1572888
  2.1 0.0 copy-start.3
  2.1 0.0 copy-start.2
  2.1 0.8 %z_faces.1 = (f32[3072,128]{1,0:T(8,128)S(1)}, f32[2,3,8,128]{3,2,1,0:T(8,128)S(1)}, f32[2,3,8,128]{3,2,1,0:T(8,128)S(1)}) custom-call(f32[3072,128]{1,0:T(8,128)S(1)} %bitcast.8), custom_call_target="tpu_custom_call" | custom-call | tf_op jit(solution)/shard_map/z_faces/pallas_call | solution.py:631
  2.9 6.5 %collective-permute-start.1 = (f32[2,3,8,128]{3,2,1,0:T(8,128)S(1)}, f32[2,3,8,128]{3,2,1,0:T(8,128)S(1)}, u32[]{:S(2)}, u32[]{:S(2)}) collective-permute-start(f32[2,3,8,128]{3,2,1,0:T(8,128)S(1)} %get-tuple-element.24.face_far), channel_id=1, source_target_pairs={{0,7},{1,2},{2,1},{3,4},{4,3},{5,6},{6,5},{7,0},{8,15},{9,10},{10,... | collective-permute-start | bytes 73736 | tf_op jit(solution)/shard_map/ppermute | solution.py:424
  9.4 0.0 collective-permute-start
  9.4 0.0 copy-done.3
  9.4 0.1 copy.7.corner_ref.refs_9_
  9.5 0.0 copy-done
  9.5 0.0 copy-done.2
  9.5 5.5 %boxes.3 = (f32[1,3,16,16,128]{4,3,2,1,0:T(8,128)S(1)}, f32[256,128]{1,0:T(8,128)S(1)}, f32[256,128]{1,0:T(8,128)S(1)}) custom-call(s32[32]{0:T(128)S(1)} %copy-done.2, s32[32,3]{1,0:T(8,128)S(1)} %copy.7.corner_ref.refs_9_, f32[3072,128]{1,0:T(8,128)S(1)} %get-tuple-element.22.vel_ref.rows_ref, f32[512,256]{1,0:T(8,128)S(1)} %bitcast.5, ...), custom_call_target="tpu_custom_call" | custom-call | flops 30000000 | bytes 5000000 | tf_op jit(solution)/shard_map/boxes/pallas_call | solution.py:296
  15.0 0.0 collective-permute-done.1.z_far
  15.0 0.0 collective-permute-done.z_near
  15.0 0.2 y_faces.1
  15.3 2.6 %collective-permute-start.3 = (f32[3,80,128]{2,1,0:T(8,128)S(1)}, f32[3,80,128]{2,1,0:T(8,128)S(1)}, u32[]{:S(2)}, u32[]{:S(2)}) collective-permute-start(f32[3,80,128]{2,1,0:T(8,128)S(1)} %get-tuple-element.27), channel_id=1, source_target_pairs={{0,24},{8,16},{16,8},{24,0},{1,25},{9,17},{17,9},{25,1},{2,26},{10... | collective-permute-start | bytes 368648 | tf_op jit(solution)/shard_map/ppermute | solution.py:424
  17.8 0.0 collective-permute-start.2
  17.8 5.5 %boxes.4 = (f32[1,3,16,16,128]{4,3,2,1,0:T(8,128)S(1)}, f32[256,128]{1,0:T(8,128)S(1)}, f32[256,128]{1,0:T(8,128)S(1)}) custom-call(s32[32]{0:T(128)S(1)} %copy-done.2, s32[32,3]{1,0:T(8,128)S(1)} %copy.7.corner_ref.refs_9_, f32[3072,128]{1,0:T(8,128)S(1)} %get-tuple-element.22.vel_ref.rows_ref, f32[512,256]{1,0:T(8,128)S(1)} %bitcast.6, ...), custom_call_target="tpu_custom_call" | custom-call | flops 30000000 | bytes 5000000 | tf_op jit(solution)/shard_map/boxes/pallas_call | solution.py:296
  23.3 0.0 collective-permute-done.3.y_far
  23.3 0.0 collective-permute-done.2.y_near
  23.4 2.7 %collective-permute-start.5 = (f32[3,88,128]{2,1,0:T(8,128)S(1)}, f32[3,88,128]{2,1,0:T(8,128)S(1)}, u32[]{:S(2)}, u32[]{:S(2)}) collective-permute-start(f32[3,88,128]{2,1,0:T(8,128)S(1)} %get-tuple-element.30), channel_id=1, source_target_pairs={{0,224},{32,64},{64,32},{96,128},{128,96},{160,192},{192,160},{224... | collective-permute-start | bytes 405512 | tf_op jit(solution)/shard_map/ppermute | solution.py:424
  26.1 0.5 %collective-permute-start.4 = (f32[3,88,128]{2,1,0:T(8,128)S(1)}, f32[3,88,128]{2,1,0:T(8,128)S(1)}, u32[]{:S(2)}, u32[]{:S(2)}) collective-permute-start(f32[3,88,128]{2,1,0:T(8,128)S(1)} %get-tuple-element.29.rest_0_), channel_id=1, source_target_pairs={{0,32},{32,0},{64,96},{96,64},{128,160},{160,128},{192,224},{224,1... | collective-permute-start | bytes 405512 | tf_op jit(solution)/shard_map/ppermute | solution.py:424
  26.6 10.1 %boxes.5 = (f32[2,3,16,16,128]{4,3,2,1,0:T(8,128)S(1)}, f32[512,128]{1,0:T(8,128)S(1)}, f32[512,128]{1,0:T(8,128)S(1)}) custom-call(s32[32]{0:T(128)S(1)} %copy-done.2, s32[32,3]{1,0:T(8,128)S(1)} %copy.7.corner_ref.refs_9_, f32[3072,128]{1,0:T(8,128)S(1)} %get-tuple-element.22.vel_ref.rows_ref, f32[512,256]{1,0:T(8,128)S(1)} %bitcast.7, ...), custom_call_target="tpu_custom_call" | custom-call | flops 30000000 | bytes 5000000 | tf_op jit(solution)/shard_map/boxes/pallas_call | solution.py:296
  36.8 0.0 collective-permute-done.5.x_far
  36.8 0.0 collective-permute-done.4.x_near
  36.8 10.4 %momentum.1 = (f32[3072,128]{1,0:T(8,128)}, f32[512,256]{1,0:T(8,128)}, f32[512,256]{1,0:T(8,128)}) custom-call(f32[3072,128]{1,0:T(8,128)S(1)} %get-tuple-element.22.vel_ref.rows_ref, f32[2,3,8,128]{3,2,1,0:T(8,128)S(1)} %get-tuple-element.23.rest_0_.face_near, f32[2,3,8,128]{3,2,1,0:T(8,128)S(1)} %get-tuple-element.24.face_far, ...), custom_call_target="tpu_custom_call" | custom-call | tf_op jit(solution)/shard_map/momentum/pallas_call | solution.py:666
  (1 shorter events, 0.0 us)
Async XLA Ops:
  0.6 8.9 %copy-start = (f32[32,16,256]{2,1,0:T(8,128)S(1)}, f32[32,16,256]{2,1,0:T(8,128)}, u32[]{:S(2)}) copy-start(f32[32,16,256]{2,1,0:T(8,128)} %param.5) | copy-start | bytes 1572868
  0.6 1.5 %copy-start.1 = (f32[3,32,32,128]{3,2,1,0:T(8,128)S(1)}, f32[3,32,32,128]{3,2,1,0:T(8,128)}, u32[]{:S(2)}) copy-start(f32[3,32,32,128]{3,2,1,0:T(8,128)} %param.4) | copy-start | bytes 4718596
  2.1 7.3 %copy-start.3 = (s32[32,3]{0,1:T(4,128)S(1)}, s32[32,3]{0,1:T(4,128)}, u32[]{:S(2)}) copy-start(s32[32,3]{0,1:T(4,128)} %param.6) | copy-start | bytes 1156
  2.1 7.4 %copy-start.2 = (s32[32]{0:T(128)S(1)}, s32[32]{0:T(128)}, u32[]{:S(2)}) copy-start(s32[32]{0:T(128)} %owner_ref.5) | copy-start | bytes 388
  2.9 12.1 %collective-permute-start.1 = (f32[2,3,8,128]{3,2,1,0:T(8,128)S(1)}, f32[2,3,8,128]{3,2,1,0:T(8,128)S(1)}, u32[]{:S(2)}, u32[]{:S(2)}) collective-permute-start(f32[2,3,8,128]{3,2,1,0:T(8,128)S(1)} %get-tuple-element.24.face_far), channel_id=1, source_target_pairs={{0,7},{1,2},{2,1},{3,4},{4,3},{5,6},{6,5},{7,0},{8,15},{9,10},{10,... | collective-permute-start | bytes 73736 | tf_op jit(solution)/shard_map/ppermute | solution.py:424
  9.4 5.6 %collective-permute-start = (f32[2,3,8,128]{3,2,1,0:T(8,128)S(1)}, f32[2,3,8,128]{3,2,1,0:T(8,128)S(1)}, u32[]{:S(2)}, u32[]{:S(2)}) collective-permute-start(f32[2,3,8,128]{3,2,1,0:T(8,128)S(1)} %get-tuple-element.23.rest_0_.face_near), channel_id=1, source_target_pairs={{0,1},{1,0},{2,3},{3,2},{4,5},{5,4},{6,7},{7,6},{8,9},{9,8},{10,11... | collective-permute-start | bytes 73736 | tf_op jit(solution)/shard_map/ppermute | solution.py:424
  15.3 8.1 %collective-permute-start.3 = (f32[3,80,128]{2,1,0:T(8,128)S(1)}, f32[3,80,128]{2,1,0:T(8,128)S(1)}, u32[]{:S(2)}, u32[]{:S(2)}) collective-permute-start(f32[3,80,128]{2,1,0:T(8,128)S(1)} %get-tuple-element.27), channel_id=1, source_target_pairs={{0,24},{8,16},{16,8},{24,0},{1,25},{9,17},{17,9},{25,1},{2,26},{10... | collective-permute-start | bytes 368648 | tf_op jit(solution)/shard_map/ppermute | solution.py:424
  17.8 5.5 %collective-permute-start.2 = (f32[3,80,128]{2,1,0:T(8,128)S(1)}, f32[3,80,128]{2,1,0:T(8,128)S(1)}, u32[]{:S(2)}, u32[]{:S(2)}) collective-permute-start(f32[3,80,128]{2,1,0:T(8,128)S(1)} %get-tuple-element.26.rest_0_), channel_id=1, source_target_pairs={{0,8},{8,0},{16,24},{24,16},{1,9},{9,1},{17,25},{25,17},{2,10},{10... | collective-permute-start | bytes 368648 | tf_op jit(solution)/shard_map/ppermute | solution.py:424
  23.4 13.4 %collective-permute-start.5 = (f32[3,88,128]{2,1,0:T(8,128)S(1)}, f32[3,88,128]{2,1,0:T(8,128)S(1)}, u32[]{:S(2)}, u32[]{:S(2)}) collective-permute-start(f32[3,88,128]{2,1,0:T(8,128)S(1)} %get-tuple-element.30), channel_id=1, source_target_pairs={{0,224},{32,64},{64,32},{96,128},{128,96},{160,192},{192,160},{224... | collective-permute-start | bytes 405512 | tf_op jit(solution)/shard_map/ppermute | solution.py:424
  26.1 10.7 %collective-permute-start.4 = (f32[3,88,128]{2,1,0:T(8,128)S(1)}, f32[3,88,128]{2,1,0:T(8,128)S(1)}, u32[]{:S(2)}, u32[]{:S(2)}) collective-permute-start(f32[3,88,128]{2,1,0:T(8,128)S(1)} %get-tuple-element.29.rest_0_), channel_id=1, source_target_pairs={{0,32},{32,0},{64,96},{96,64},{128,160},{160,128},{192,224},{224,1... | collective-permute-start | bytes 405512 | tf_op jit(solution)/shard_map/ppermute | solution.py:424

commit v6 on v5

--- a/solution.py
+++ b/solution.py
@@ -440,7 +440,16 @@
     return lower, upper
 
 
-def tile_step(ext, planes, plane, yt, below, above, n, lane):
+def z_ends(below, above, lane):
+    even = lane % 2 == 0
+    out = []
+    for lower, upper in zip(below, above):
+        upper = pltpu.roll(upper, LANES - 1, 1)
+        out.append((jnp.where(even, lower, upper), jnp.where(even, upper, lower)))
+    return out
+
+
+def tile_step(ext, planes, plane, yt, ends, n, lane):
     at = [
         pl.multiple_of((c * planes + plane) * PLANE + 8 + 8 * yt, 8) for c in range(3)
     ]
@@ -448,12 +457,8 @@
     out = []
     for c in range(3):
         v = centre[c]
-        lower2, upper2 = along_z(
-            v,
-            pltpu.roll(below[c], (LANES - n) % LANES, 1),
-            pltpu.roll(above[c], LANES - 1 - n, 1),
-            lane,
-        )
+        end = pltpu.roll(ends[c][yt % 2], (LANES - n) % LANES, 1)
+        lower2, upper2 = along_z(v, end, end, lane)
         lower = (ext[pl.ds(at[c] - PLANE, 8), :], ext[pl.ds(at[c] - 1, 8), :], lower2)
         upper = (ext[pl.ds(at[c] + PLANE, 8), :], ext[pl.ds(at[c] + 1, 8), :], upper2)
         out.append(v + grid_step * slopes_to_f(centre, v, lower, upper))
@@ -542,21 +547,24 @@
             at = pl.multiple_of((c * 36 + x + 2) * PLANE + 8, 8)
             ext[pl.ds(at, 32), :] = vel_ref[pl.ds(pl.multiple_of(c * 1024 + x * 32, 8), 32), :]
 
+    ends = z_ends([below[0, c] for c in range(3)], [above[0, c] for c in range(3)], lane)
+
     @pl.loop(0, 32, unroll=PLANES)
     def _(x):
-        lo = [below[0, c] for c in range(3)]
-        hi = [above[0, c] for c in range(3)]
         for yt in range(4):
-            new = tile_step(ext, 36, x + 2, yt, lo, hi, x * 4 + yt, lane)
+            new = tile_step(ext, 36, x + 2, yt, ends, x * 4 + yt, lane)
             for c in range(3):
                 at = pl.multiple_of((c * 34 + x + 1) * PLANE + 8 + 8 * yt, 8)
                 later[pl.ds(at, 8), :] = new[c]
 
     for halo, plane, x in ((front, 1, 31), (back, 34, 0)):
-        lo = [halo[c, pl.ds(72, 8), :] for c in range(3)]
-        hi = [halo[c, pl.ds(80, 8), :] for c in range(3)]
+        side_ends = z_ends(
+            [halo[c, pl.ds(72, 8), :] for c in range(3)],
+            [halo[c, pl.ds(80, 8), :] for c in range(3)],
+            lane,
+        )
         for yt in range(4):
-            new = tile_step(ext, 36, plane, yt, lo, hi, x * 4 + yt, lane)
+            new = tile_step(ext, 36, plane, yt, side_ends, x * 4 + yt, lane)
             for c in range(3):
                 later[pl.ds((c * 34 + plane - 1) * PLANE + 8 + 8 * yt, 8), :] = new[c]
 
@@ -604,12 +612,14 @@
         for c in range(3):
             packed[outward, c] = new[c]
 
+    later_ends = z_ends(
+        [packed[0, c] for c in range(3)], [packed[1, c] for c in range(3)], lane
+    )
+
     @pl.loop(0, 32, unroll=PLANES)
     def _(x):
-        lo = [packed[0, c] for c in range(3)]
-        hi = [packed[1, c] for c in range(3)]
         for yt in range(4):
-            new = tile_step(later, 34, x + 1, yt, lo, hi, x * 4 + yt, lane)
+            new = tile_step(later, 34, x + 1, yt, later_ends, x * 4 + yt, lane)
             for c in range(3):
                 at = pl.ds(pl.multiple_of(c * 1024 + x * 32 + 8 * yt, 8), 8)
                 out_ref[at, :] = 0.5 * (vel_ref[at, :] + new[c])

time: 47.4 us -> 46.8 us (0.987)
  Pallas kernels: 32.6 us -> 31.9 us
    pallas_call x1, Pallas kernels: 10.4 us -> 9.7 us  [local(): pl.pallas_call(momentum_body, out_shape=(jax.ShapeDtypeStruct(rows.shape,...]
where the time goes in v6:
time: 46.8 us; the launch traced here: 46.6 us
  Pallas kernels  31.9 us (68%)
  starting transfers between devices  12.3 us (26%)
  local copies, waits for them, and re-layouts  1.56 us (3%)
  between operations  0.9 us (2%)
    pallas_call x3, Pallas kernels, boxes(): pl.pallas_call(functools.partial(box_body, first_group, count), out_shape...  21.1 us
    ppermute x6, starting transfers between devices, exchange(): return (lax.ppermute(first, axis, near), lax.ppermute(second, axis, far))  12.3 us
    pallas_call x1, Pallas kernels, local(): pl.pallas_call(momentum_body, out_shape=(jax.ShapeDtypeStruct(rows.shape,...  9.7 us
    unnamed x9, local copies, waits for them, and re-layouts  1.56 us
    pallas_call x3, Pallas kernels, call(): pl.pallas_call(body, out_shape=out_shape, in_specs=specs, out_specs=jax.t...  1.1 us
  transfers between devices with their start and end apart: 6, of which 0 were waited for; matrix products, arithmetic and copies ran while one was open for 0% of the time, Pallas kernels for 45%

profile of v6, /device:TPU:1, one launch (start us, length us, event | category | flops | bytes accessed | tf_op | source)
XLA Modules:
  0.0 46.6 jit_solution(14932980027288129963)
XLA Ops:
  0.6 0.0 copy-start
  0.6 0.0 copy-start.1
  0.7 1.5 %copy-done.1 = f32[3,32,32,128]{3,2,1,0:T(8,128)S(1)} copy-done((f32[3,32,32,128]{3,2,1,0:T(8,128)S(1)}, f32[3,32,32,128]{3,2,1,0:T(8,128)}, u32[]{:S(2)}) %copy-start.1) | copy-done | bytes 1572888
  2.1 0.0 copy-start.3
  2.1 0.0 copy-start.2
  2.1 0.8 %z_faces.1 = (f32[3072,128]{1,0:T(8,128)S(1)}, f32[2,3,8,128]{3,2,1,0:T(8,128)S(1)}, f32[2,3,8,128]{3,2,1,0:T(8,128)S(1)}) custom-call(f32[3072,128]{1,0:T(8,128)S(1)} %bitcast.8), custom_call_target="tpu_custom_call" | custom-call | tf_op jit(solution)/shard_map/z_faces/pallas_call | solution.py:641
  2.9 6.5 %collective-permute-start.1 = (f32[2,3,8,128]{3,2,1,0:T(8,128)S(1)}, f32[2,3,8,128]{3,2,1,0:T(8,128)S(1)}, u32[]{:S(2)}, u32[]{:S(2)}) collective-permute-start(f32[2,3,8,128]{3,2,1,0:T(8,128)S(1)} %get-tuple-element.24.face_far), channel_id=1, source_target_pairs={{0,7},{1,2},{2,1},{3,4},{4,3},{5,6},{6,5},{7,0},{8,15},{9,10},{10,... | collective-permute-start | bytes 73736 | tf_op jit(solution)/shard_map/ppermute | solution.py:424
  9.4 0.0 collective-permute-start
  9.4 0.0 copy-done.3
  9.4 0.1 copy.7.corner_ref.refs_9_
  9.5 0.0 copy-done
  9.5 0.0 copy-done.2
  9.5 5.5 %boxes.3 = (f32[1,3,16,16,128]{4,3,2,1,0:T(8,128)S(1)}, f32[256,128]{1,0:T(8,128)S(1)}, f32[256,128]{1,0:T(8,128)S(1)}) custom-call(s32[32]{0:T(128)S(1)} %copy-done.2, s32[32,3]{1,0:T(8,128)S(1)} %copy.7.corner_ref.refs_9_, f32[3072,128]{1,0:T(8,128)S(1)} %get-tuple-element.22.vel_ref.rows_ref, f32[512,256]{1,0:T(8,128)S(1)} %bitcast.5, ...), custom_call_target="tpu_custom_call" | custom-call | flops 30000000 | bytes 5000000 | tf_op jit(solution)/shard_map/boxes/pallas_call | solution.py:296
  15.0 0.0 collective-permute-done.1.z_far
  15.0 0.0 collective-permute-done.z_near
  15.0 0.2 y_faces.1
  15.3 2.6 %collective-permute-start.3 = (f32[3,80,128]{2,1,0:T(8,128)S(1)}, f32[3,80,128]{2,1,0:T(8,128)S(1)}, u32[]{:S(2)}, u32[]{:S(2)}) collective-permute-start(f32[3,80,128]{2,1,0:T(8,128)S(1)} %get-tuple-element.27), channel_id=1, source_target_pairs={{0,24},{8,16},{16,8},{24,0},{1,25},{9,17},{17,9},{25,1},{2,26},{10... | collective-permute-start | bytes 368648 | tf_op jit(solution)/shard_map/ppermute | solution.py:424
  17.8 0.0 collective-permute-start.2
  17.8 5.5 %boxes.4 = (f32[1,3,16,16,128]{4,3,2,1,0:T(8,128)S(1)}, f32[256,128]{1,0:T(8,128)S(1)}, f32[256,128]{1,0:T(8,128)S(1)}) custom-call(s32[32]{0:T(128)S(1)} %copy-done.2, s32[32,3]{1,0:T(8,128)S(1)} %copy.7.corner_ref.refs_9_, f32[3072,128]{1,0:T(8,128)S(1)} %get-tuple-element.22.vel_ref.rows_ref, f32[512,256]{1,0:T(8,128)S(1)} %bitcast.6, ...), custom_call_target="tpu_custom_call" | custom-call | flops 30000000 | bytes 5000000 | tf_op jit(solution)/shard_map/boxes/pallas_call | solution.py:296
  23.3 0.0 collective-permute-done.3.y_far
  23.3 0.0 collective-permute-done.2.y_near
  23.4 2.7 %collective-permute-start.5 = (f32[3,88,128]{2,1,0:T(8,128)S(1)}, f32[3,88,128]{2,1,0:T(8,128)S(1)}, u32[]{:S(2)}, u32[]{:S(2)}) collective-permute-start(f32[3,88,128]{2,1,0:T(8,128)S(1)} %get-tuple-element.30), channel_id=1, source_target_pairs={{0,224},{32,64},{64,32},{96,128},{128,96},{160,192},{192,160},{224... | collective-permute-start | bytes 405512 | tf_op jit(solution)/shard_map/ppermute | solution.py:424
  26.1 0.5 %collective-permute-start.4 = (f32[3,88,128]{2,1,0:T(8,128)S(1)}, f32[3,88,128]{2,1,0:T(8,128)S(1)}, u32[]{:S(2)}, u32[]{:S(2)}) collective-permute-start(f32[3,88,128]{2,1,0:T(8,128)S(1)} %get-tuple-element.29.rest_0_), channel_id=1, source_target_pairs={{0,32},{32,0},{64,96},{96,64},{128,160},{160,128},{192,224},{224,1... | collective-permute-start | bytes 405512 | tf_op jit(solution)/shard_map/ppermute | solution.py:424
  26.6 10.1 %boxes.5 = (f32[2,3,16,16,128]{4,3,2,1,0:T(8,128)S(1)}, f32[512,128]{1,0:T(8,128)S(1)}, f32[512,128]{1,0:T(8,128)S(1)}) custom-call(s32[32]{0:T(128)S(1)} %copy-done.2, s32[32,3]{1,0:T(8,128)S(1)} %copy.7.corner_ref.refs_9_, f32[3072,128]{1,0:T(8,128)S(1)} %get-tuple-element.22.vel_ref.rows_ref, f32[512,256]{1,0:T(8,128)S(1)} %bitcast.7, ...), custom_call_target="tpu_custom_call" | custom-call | flops 30000000 | bytes 5000000 | tf_op jit(solution)/shard_map/boxes/pallas_call | solution.py:296
  36.8 0.0 collective-permute-done.5.x_far
  36.8 0.0 collective-permute-done.4.x_near
  36.8 9.7 %momentum.1 = (f32[3072,128]{1,0:T(8,128)}, f32[512,256]{1,0:T(8,128)}, f32[512,256]{1,0:T(8,128)}) custom-call(f32[3072,128]{1,0:T(8,128)S(1)} %get-tuple-element.22.vel_ref.rows_ref, f32[2,3,8,128]{3,2,1,0:T(8,128)S(1)} %get-tuple-element.23.rest_0_.face_near, f32[2,3,8,128]{3,2,1,0:T(8,128)S(1)} %get-tuple-element.24.face_far, ...), custom_call_target="tpu_custom_call" | custom-call | tf_op jit(solution)/shard_map/momentum/pallas_call | solution.py:676
  (1 shorter events, 0.0 us)
Async XLA Ops:
  0.6 8.9 %copy-start = (f32[32,16,256]{2,1,0:T(8,128)S(1)}, f32[32,16,256]{2,1,0:T(8,128)}, u32[]{:S(2)}) copy-start(f32[32,16,256]{2,1,0:T(8,128)} %param.5) | copy-start | bytes 1572868
  0.6 1.5 %copy-start.1 = (f32[3,32,32,128]{3,2,1,0:T(8,128)S(1)}, f32[3,32,32,128]{3,2,1,0:T(8,128)}, u32[]{:S(2)}) copy-start(f32[3,32,32,128]{3,2,1,0:T(8,128)} %param.4) | copy-start | bytes 4718596
  2.1 7.3 %copy-start.3 = (s32[32,3]{0,1:T(4,128)S(1)}, s32[32,3]{0,1:T(4,128)}, u32[]{:S(2)}) copy-start(s32[32,3]{0,1:T(4,128)} %param.6) | copy-start | bytes 1156
  2.1 7.4 %copy-start.2 = (s32[32]{0:T(128)S(1)}, s32[32]{0:T(128)}, u32[]{:S(2)}) copy-start(s32[32]{0:T(128)} %owner_ref.5) | copy-start | bytes 388
  2.9 12.1 %collective-permute-start.1 = (f32[2,3,8,128]{3,2,1,0:T(8,128)S(1)}, f32[2,3,8,128]{3,2,1,0:T(8,128)S(1)}, u32[]{:S(2)}, u32[]{:S(2)}) collective-permute-start(f32[2,3,8,128]{3,2,1,0:T(8,128)S(1)} %get-tuple-element.24.face_far), channel_id=1, source_target_pairs={{0,7},{1,2},{2,1},{3,4},{4,3},{5,6},{6,5},{7,0},{8,15},{9,10},{10,... | collective-permute-start | bytes 73736 | tf_op jit(solution)/shard_map/ppermute | solution.py:424
  9.4 5.6 %collective-permute-start = (f32[2,3,8,128]{3,2,1,0:T(8,128)S(1)}, f32[2,3,8,128]{3,2,1,0:T(8,128)S(1)}, u32[]{:S(2)}, u32[]{:S(2)}) collective-permute-start(f32[2,3,8,128]{3,2,1,0:T(8,128)S(1)} %get-tuple-element.23.rest_0_.face_near), channel_id=1, source_target_pairs={{0,1},{1,0},{2,3},{3,2},{4,5},{5,4},{6,7},{7,6},{8,9},{9,8},{10,11... | collective-permute-start | bytes 73736 | tf_op jit(solution)/shard_map/ppermute | solution.py:424
  15.3 8.1 %collective-permute-start.3 = (f32[3,80,128]{2,1,0:T(8,128)S(1)}, f32[3,80,128]{2,1,0:T(8,128)S(1)}, u32[]{:S(2)}, u32[]{:S(2)}) collective-permute-start(f32[3,80,128]{2,1,0:T(8,128)S(1)} %get-tuple-element.27), channel_id=1, source_target_pairs={{0,24},{8,16},{16,8},{24,0},{1,25},{9,17},{17,9},{25,1},{2,26},{10... | collective-permute-start | bytes 368648 | tf_op jit(solution)/shard_map/ppermute | solution.py:424
  17.8 5.5 %collective-permute-start.2 = (f32[3,80,128]{2,1,0:T(8,128)S(1)}, f32[3,80,128]{2,1,0:T(8,128)S(1)}, u32[]{:S(2)}, u32[]{:S(2)}) collective-permute-start(f32[3,80,128]{2,1,0:T(8,128)S(1)} %get-tuple-element.26.rest_0_), channel_id=1, source_target_pairs={{0,8},{8,0},{16,24},{24,16},{1,9},{9,1},{17,25},{25,17},{2,10},{10... | collective-permute-start | bytes 368648 | tf_op jit(solution)/shard_map/ppermute | solution.py:424
  23.4 13.4 %collective-permute-start.5 = (f32[3,88,128]{2,1,0:T(8,128)S(1)}, f32[3,88,128]{2,1,0:T(8,128)S(1)}, u32[]{:S(2)}, u32[]{:S(2)}) collective-permute-start(f32[3,88,128]{2,1,0:T(8,128)S(1)} %get-tuple-element.30), channel_id=1, source_target_pairs={{0,224},{32,64},{64,32},{96,128},{128,96},{160,192},{192,160},{224... | collective-permute-start | bytes 405512 | tf_op jit(solution)/shard_map/ppermute | solution.py:424
  26.1 10.7 %collective-permute-start.4 = (f32[3,88,128]{2,1,0:T(8,128)S(1)}, f32[3,88,128]{2,1,0:T(8,128)S(1)}, u32[]{:S(2)}, u32[]{:S(2)}) collective-permute-start(f32[3,88,128]{2,1,0:T(8,128)S(1)} %get-tuple-element.29.rest_0_), channel_id=1, source_target_pairs={{0,32},{32,0},{64,96},{96,64},{128,160},{160,128},{192,224},{224,1... | collective-permute-start | bytes 405512 | tf_op jit(solution)/shard_map/ppermute | solution.py:424

commit v7 on v6

--- a/solution.py
+++ b/solution.py
@@ -41,8 +41,7 @@
     return jnp.take_along_axis(x, (lane + BOX * row) % LANES, axis=1)
 
 
-def weno(a, b, c, e, f):
-    ab, bc, ce, ef = a - b, b - c, c - e, e - f
+def weno(ab, bc, ce, ef):
     d1, d2, d3 = ab - bc, bc - ce, ce - ef
     bc2, ce2 = bc + bc, ce + ce
     t1, t2, t3 = d1 - bc2, bc + ce, d3 + ce2
@@ -56,18 +55,18 @@
     w2 = 6.0 * (q1 * q3)
     w3 = 3.0 * (q1 * q2)
     top = w1 * ((ab + ab) - 5.0 * bc) - w2 * (bc + ce2) + w3 * (ef - (ce2 + ce2))
-    return c + top / (6.0 * (w1 + w2 + w3))
-
-
-def upwind(speed, back_two, back_one, here, ahead_one, ahead_two, ahead_three):
+    return top / (6.0 * (w1 + w2 + w3))
+
+
+def upwind(speed, here, ahead, far_back, back, middle, front, far_front):
     pos = speed > 0.0
-    return speed * weno(
-        jnp.where(pos, back_two, ahead_three),
-        jnp.where(pos, back_one, ahead_two),
-        jnp.where(pos, here, ahead_one),
-        jnp.where(pos, ahead_one, here),
-        jnp.where(pos, ahead_two, back_one),
+    turn = weno(
+        jnp.where(pos, far_back, far_front),
+        jnp.where(pos, back, front),
+        middle,
+        jnp.where(pos, front, back),
     )
+    return speed * jnp.where(pos, here, ahead) - jnp.abs(speed) * turn
 
 
 ROWS = 32
@@ -156,23 +155,28 @@
                 at = pl.ds(8 * jt, 8)
                 padded_at = pl.ds(8 + 8 * jt, 8)
                 here = l_ref[i, padded_at, :]
-                change = upwind(u_ref[0, i, at, :], *[mi_ref[i + t, at, :] for t in range(6)])
+                m = [mi_ref[i + t, at, :] for t in range(6)]
+                change = upwind(
+                    u_ref[0, i, at, :], m[2], m[3], *[m[t + 1] - m[t] for t in range(5)]
+                )
+                m = [mj_ref[i, pl.ds(6 + t + 8 * jt, 8), :] for t in range(6)]
                 change += upwind(
-                    u_ref[1, i, at, :],
-                    *[mj_ref[i, pl.ds(6 + t + 8 * jt, 8), :] for t in range(6)],
+                    u_ref[1, i, at, :], m[2], m[3], *[m[t + 1] - m[t] for t in range(5)]
                 )
                 m = here - prev_k(here)
-                back_one = prev_k(m)
-                ahead_one = next_k(m)
-                ahead_two = next_k(ahead_one)
+                ahead = next_k(m)
+                middle = ahead - m
+                back = pltpu.roll(middle, 1, 1)
+                front = next_k(middle)
                 change += upwind(
                     u_ref[2, i, at, :],
-                    prev_k(back_one),
-                    back_one,
                     m,
-                    ahead_one,
-                    ahead_two,
-                    next_k(ahead_two),
+                    ahead,
+                    jnp.where(k_first, 0.0, pltpu.roll(back, 1, 1)),
+                    back,
+                    middle,
+                    front,
+                    next_k(front),
                 )
                 advected = here - box_step * change
                 pa[i, padded_at, :] = advected

time: 46.8 us -> 46.8 us (level)
  no operation moved by 1% of the time
where the time goes in v7:
time: 46.8 us; the launch traced here: 46.7 us
  Pallas kernels  31.9 us (68%)
  starting transfers between devices  12.3 us (26%)
  local copies, waits for them, and re-layouts  1.56 us (3%)
  between operations  0.9 us (2%)
    pallas_call x3, Pallas kernels, boxes(): pl.pallas_call(functools.partial(box_body, first_group, count), out_shape...  21.1 us
    ppermute x6, starting transfers between devices, exchange(): return (lax.ppermute(first, axis, near), lax.ppermute(second, axis, far))  12.3 us
    pallas_call x1, Pallas kernels, local(): pl.pallas_call(momentum_body, out_shape=(jax.ShapeDtypeStruct(rows.shape,...  9.71 us
    unnamed x9, local copies, waits for them, and re-layouts  1.56 us
    pallas_call x3, Pallas kernels, call(): pl.pallas_call(body, out_shape=out_shape, in_specs=specs, out_specs=jax.t...  1.1 us
  transfers between devices with their start and end apart: 6, of which 0 were waited for; matrix products, arithmetic and copies ran while one was open for 0% of the time, Pallas kernels for 45%

profile of v7, /device:TPU:1, one launch (start us, length us, event | category | flops | bytes accessed | tf_op | source)
XLA Modules:
  0.0 46.7 jit_solution(705999275043473177)
XLA Ops:
  0.6 0.0 copy-start
  0.6 0.0 copy-start.1
  0.7 1.5 %copy-done.1 = f32[3,32,32,128]{3,2,1,0:T(8,128)S(1)} copy-done((f32[3,32,32,128]{3,2,1,0:T(8,128)S(1)}, f32[3,32,32,128]{3,2,1,0:T(8,128)}, u32[]{:S(2)}) %copy-start.1) | copy-done | bytes 1572888
  2.1 0.0 copy-start.3
  2.1 0.0 copy-start.2
  2.1 0.8 %z_faces.1 = (f32[3072,128]{1,0:T(8,128)S(1)}, f32[2,3,8,128]{3,2,1,0:T(8,128)S(1)}, f32[2,3,8,128]{3,2,1,0:T(8,128)S(1)}) custom-call(f32[3072,128]{1,0:T(8,128)S(1)} %bitcast.8), custom_call_target="tpu_custom_call" | custom-call | tf_op jit(solution)/shard_map/z_faces/pallas_call | solution.py:645
  2.9 6.5 %collective-permute-start.1 = (f32[2,3,8,128]{3,2,1,0:T(8,128)S(1)}, f32[2,3,8,128]{3,2,1,0:T(8,128)S(1)}, u32[]{:S(2)}, u32[]{:S(2)}) collective-permute-start(f32[2,3,8,128]{3,2,1,0:T(8,128)S(1)} %get-tuple-element.24.face_far), channel_id=1, source_target_pairs={{0,7},{1,2},{2,1},{3,4},{4,3},{5,6},{6,5},{7,0},{8,15},{9,10},{10,... | collective-permute-start | bytes 73736 | tf_op jit(solution)/shard_map/ppermute | solution.py:428
  9.4 0.0 collective-permute-start
  9.4 0.0 copy-done.3
  9.4 0.1 copy.7.corner_ref.refs_9_
  9.5 0.0 copy-done
  9.5 0.0 copy-done.2
  9.5 5.5 %boxes.3 = (f32[1,3,16,16,128]{4,3,2,1,0:T(8,128)S(1)}, f32[256,128]{1,0:T(8,128)S(1)}, f32[256,128]{1,0:T(8,128)S(1)}) custom-call(s32[32]{0:T(128)S(1)} %copy-done.2, s32[32,3]{1,0:T(8,128)S(1)} %copy.7.corner_ref.refs_9_, f32[3072,128]{1,0:T(8,128)S(1)} %get-tuple-element.22.vel_ref.rows_ref, f32[512,256]{1,0:T(8,128)S(1)} %bitcast.5, ...), custom_call_target="tpu_custom_call" | custom-call | flops 30000000 | bytes 5000000 | tf_op jit(solution)/shard_map/boxes/pallas_call | solution.py:300
  15.0 0.0 collective-permute-done.1.z_far
  15.0 0.0 collective-permute-done.z_near
  15.0 0.2 y_faces.1
  15.3 2.6 %collective-permute-start.3 = (f32[3,80,128]{2,1,0:T(8,128)S(1)}, f32[3,80,128]{2,1,0:T(8,128)S(1)}, u32[]{:S(2)}, u32[]{:S(2)}) collective-permute-start(f32[3,80,128]{2,1,0:T(8,128)S(1)} %get-tuple-element.27), channel_id=1, source_target_pairs={{0,24},{8,16},{16,8},{24,0},{1,25},{9,17},{17,9},{25,1},{2,26},{10... | collective-permute-start | bytes 368648 | tf_op jit(solution)/shard_map/ppermute | solution.py:428
  17.8 0.0 collective-permute-start.2
  17.8 5.5 %boxes.4 = (f32[1,3,16,16,128]{4,3,2,1,0:T(8,128)S(1)}, f32[256,128]{1,0:T(8,128)S(1)}, f32[256,128]{1,0:T(8,128)S(1)}) custom-call(s32[32]{0:T(128)S(1)} %copy-done.2, s32[32,3]{1,0:T(8,128)S(1)} %copy.7.corner_ref.refs_9_, f32[3072,128]{1,0:T(8,128)S(1)} %get-tuple-element.22.vel_ref.rows_ref, f32[512,256]{1,0:T(8,128)S(1)} %bitcast.6, ...), custom_call_target="tpu_custom_call" | custom-call | flops 30000000 | bytes 5000000 | tf_op jit(solution)/shard_map/boxes/pallas_call | solution.py:300
  23.3 0.0 collective-permute-done.3.y_far
  23.4 0.0 collective-permute-done.2.y_near
  23.4 2.7 %collective-permute-start.5 = (f32[3,88,128]{2,1,0:T(8,128)S(1)}, f32[3,88,128]{2,1,0:T(8,128)S(1)}, u32[]{:S(2)}, u32[]{:S(2)}) collective-permute-start(f32[3,88,128]{2,1,0:T(8,128)S(1)} %get-tuple-element.30), channel_id=1, source_target_pairs={{0,224},{32,64},{64,32},{96,128},{128,96},{160,192},{192,160},{224... | collective-permute-start | bytes 405512 | tf_op jit(solution)/shard_map/ppermute | solution.py:428
  26.1 0.5 %collective-permute-start.4 = (f32[3,88,128]{2,1,0:T(8,128)S(1)}, f32[3,88,128]{2,1,0:T(8,128)S(1)}, u32[]{:S(2)}, u32[]{:S(2)}) collective-permute-start(f32[3,88,128]{2,1,0:T(8,128)S(1)} %get-tuple-element.29.rest_0_), channel_id=1, source_target_pairs={{0,32},{32,0},{64,96},{96,64},{128,160},{160,128},{192,224},{224,1... | collective-permute-start | bytes 405512 | tf_op jit(solution)/shard_map/ppermute | solution.py:428
  26.6 10.2 %boxes.5 = (f32[2,3,16,16,128]{4,3,2,1,0:T(8,128)S(1)}, f32[512,128]{1,0:T(8,128)S(1)}, f32[512,128]{1,0:T(8,128)S(1)}) custom-call(s32[32]{0:T(128)S(1)} %copy-done.2, s32[32,3]{1,0:T(8,128)S(1)} %copy.7.corner_ref.refs_9_, f32[3072,128]{1,0:T(8,128)S(1)} %get-tuple-element.22.vel_ref.rows_ref, f32[512,256]{1,0:T(8,128)S(1)} %bitcast.7, ...), custom_call_target="tpu_custom_call" | custom-call | flops 30000000 | bytes 5000000 | tf_op jit(solution)/shard_map/boxes/pallas_call | solution.py:300
  36.8 0.0 collective-permute-done.5.x_far
  36.8 0.0 collective-permute-done.4.x_near
  36.8 9.7 %momentum.1 = (f32[3072,128]{1,0:T(8,128)}, f32[512,256]{1,0:T(8,128)}, f32[512,256]{1,0:T(8,128)}) custom-call(f32[3072,128]{1,0:T(8,128)S(1)} %get-tuple-element.22.vel_ref.rows_ref, f32[2,3,8,128]{3,2,1,0:T(8,128)S(1)} %get-tuple-element.23.rest_0_.face_near, f32[2,3,8,128]{3,2,1,0:T(8,128)S(1)} %get-tuple-element.24.face_far, ...), custom_call_target="tpu_custom_call" | custom-call | tf_op jit(solution)/shard_map/momentum/pallas_call | solution.py:680
  (1 shorter events, 0.0 us)
Async XLA Ops:
  0.6 8.9 %copy-start = (f32[32,16,256]{2,1,0:T(8,128)S(1)}, f32[32,16,256]{2,1,0:T(8,128)}, u32[]{:S(2)}) copy-start(f32[32,16,256]{2,1,0:T(8,128)} %param.5) | copy-start | bytes 1572868
  0.6 1.5 %copy-start.1 = (f32[3,32,32,128]{3,2,1,0:T(8,128)S(1)}, f32[3,32,32,128]{3,2,1,0:T(8,128)}, u32[]{:S(2)}) copy-start(f32[3,32,32,128]{3,2,1,0:T(8,128)} %param.4) | copy-start | bytes 4718596
  2.1 7.3 %copy-start.3 = (s32[32,3]{0,1:T(4,128)S(1)}, s32[32,3]{0,1:T(4,128)}, u32[]{:S(2)}) copy-start(s32[32,3]{0,1:T(4,128)} %param.6) | copy-start | bytes 1156
  2.1 7.4 %copy-start.2 = (s32[32]{0:T(128)S(1)}, s32[32]{0:T(128)}, u32[]{:S(2)}) copy-start(s32[32]{0:T(128)} %owner_ref.5) | copy-start | bytes 388
  2.9 12.1 %collective-permute-start.1 = (f32[2,3,8,128]{3,2,1,0:T(8,128)S(1)}, f32[2,3,8,128]{3,2,1,0:T(8,128)S(1)}, u32[]{:S(2)}, u32[]{:S(2)}) collective-permute-start(f32[2,3,8,128]{3,2,1,0:T(8,128)S(1)} %get-tuple-element.24.face_far), channel_id=1, source_target_pairs={{0,7},{1,2},{2,1},{3,4},{4,3},{5,6},{6,5},{7,0},{8,15},{9,10},{10,... | collective-permute-start | bytes 73736 | tf_op jit(solution)/shard_map/ppermute | solution.py:428
  9.4 5.6 %collective-permute-start = (f32[2,3,8,128]{3,2,1,0:T(8,128)S(1)}, f32[2,3,8,128]{3,2,1,0:T(8,128)S(1)}, u32[]{:S(2)}, u32[]{:S(2)}) collective-permute-start(f32[2,3,8,128]{3,2,1,0:T(8,128)S(1)} %get-tuple-element.23.rest_0_.face_near), channel_id=1, source_target_pairs={{0,1},{1,0},{2,3},{3,2},{4,5},{5,4},{6,7},{7,6},{8,9},{9,8},{10,11... | collective-permute-start | bytes 73736 | tf_op jit(solution)/shard_map/ppermute | solution.py:428
  15.3 8.1 %collective-permute-start.3 = (f32[3,80,128]{2,1,0:T(8,128)S(1)}, f32[3,80,128]{2,1,0:T(8,128)S(1)}, u32[]{:S(2)}, u32[]{:S(2)}) collective-permute-start(f32[3,80,128]{2,1,0:T(8,128)S(1)} %get-tuple-element.27), channel_id=1, source_target_pairs={{0,24},{8,16},{16,8},{24,0},{1,25},{9,17},{17,9},{25,1},{2,26},{10... | collective-permute-start | bytes 368648 | tf_op jit(solution)/shard_map/ppermute | solution.py:428
  17.8 5.5 %collective-permute-start.2 = (f32[3,80,128]{2,1,0:T(8,128)S(1)}, f32[3,80,128]{2,1,0:T(8,128)S(1)}, u32[]{:S(2)}, u32[]{:S(2)}) collective-permute-start(f32[3,80,128]{2,1,0:T(8,128)S(1)} %get-tuple-element.26.rest_0_), channel_id=1, source_target_pairs={{0,8},{8,0},{16,24},{24,16},{1,9},{9,1},{17,25},{25,17},{2,10},{10... | collective-permute-start | bytes 368648 | tf_op jit(solution)/shard_map/ppermute | solution.py:428
  23.4 13.4 %collective-permute-start.5 = (f32[3,88,128]{2,1,0:T(8,128)S(1)}, f32[3,88,128]{2,1,0:T(8,128)S(1)}, u32[]{:S(2)}, u32[]{:S(2)}) collective-permute-start(f32[3,88,128]{2,1,0:T(8,128)S(1)} %get-tuple-element.30), channel_id=1, source_target_pairs={{0,224},{32,64},{64,32},{96,128},{128,96},{160,192},{192,160},{224... | collective-permute-start | bytes 405512 | tf_op jit(solution)/shard_map/ppermute | solution.py:428
  26.1 10.7 %collective-permute-start.4 = (f32[3,88,128]{2,1,0:T(8,128)S(1)}, f32[3,88,128]{2,1,0:T(8,128)S(1)}, u32[]{:S(2)}, u32[]{:S(2)}) collective-permute-start(f32[3,88,128]{2,1,0:T(8,128)S(1)} %get-tuple-element.29.rest_0_), channel_id=1, source_target_pairs={{0,32},{32,0},{64,96},{96,64},{128,160},{160,128},{192,224},{224,1... | collective-permute-start | bytes 405512 | tf_op jit(solution)/shard_map/ppermute | solution.py:428
